TPU v7x, 32 devices: a whole 2x2x4 slice. The times are simulated.
32 devices in a mesh: dp: 8 (over y, x, core), mp: 4 (over z).
Axes of the slice: x: 2, y: 2, z: 4, core: 2. Of those that a mesh axis runs over, the one named last changes fastest.
Arguments:
- tokens: bfloat16 [8192, 2048], P(('dp', 'mp')), may hold values from -6 to 6
- norm_gain: float32 [2048], replicated, may hold values from 0.1 to 1.9
- mlp_gain: float32 [2048], replicated, may hold values from 0.1 to 1.9
- lengths: int32 [8], P('dp'), may hold values from 1 to 1024, as said below
- log_decay: float32 [8192, 8], P('dp'), as said below
- query_master: float32 [2048, 2048], P(('dp', 'mp')), may hold values from -0.125 to 0.125
- key_master: float32 [2048, 2048], P(('dp', 'mp')), may hold values from -0.125 to 0.125
- value_master: float32 [2048, 4096], P(('dp', 'mp')), may hold values from -0.125 to 0.125
- swish_master: float32 [2048, 4096], P(('dp', 'mp')), may hold values from -0.125 to 0.125
- output_master: float32 [4096, 2048], P(None, ('dp', 'mp')), may hold values from -0.09375 to 0.09375
- ffn_gate_master: float32 [2048, 4096], P(('dp', 'mp')), may hold values from -0.125 to 0.125
- ffn_up_master: float32 [2048, 4096], P(('dp', 'mp')), may hold values from -0.125 to 0.125
Outputs:
- residual: bfloat16 [8192, 2048], P(('dp', 'mp'))
- hidden: bfloat16 [8192, 4096], P('dp', 'mp')
Inputs may be any that keep to these rules, and one draw needn't show every extreme that they name: `lengths`: given length of each prompt; in every draw some prompt has exactly 1024 tokens and some has 1. `log_decay`: Negative.
All inputs are finite; a program needn't handle non-finite values.
Results may differ from a plain program's by a relative error of at most 0.023.
Values may be sent and summed in bfloat16 or wider, within the bound.
No kernel may reach another device: no remote copies, remote signals or barrier semaphores. Data moves between devices by JAX's collectives and lax.ppermute only.
A program may use at most 128 MiB of HBM per device.

v0:
```python
import functools
import math

import jax
import jax.numpy as jnp
from jax import lax
from jax.experimental import pallas as pl
from jax.experimental.pallas import tpu as pltpu
from jax.sharding import PartitionSpec as P

H = 8
DK = 256
DV = 512
SPAN = 1024
HALF = DK // 2
BF = jnp.bfloat16
F32 = jnp.float32
STREAMS = 2
CHUNK = 256


def rms_rows(row_block, gain_vec):
    values = row_block.astype(F32)
    scale = lax.rsqrt(jnp.mean(values * values, axis=-1, keepdims=True) + 1e-06)
    return (values * scale * gain_vec).astype(BF)


def even_odd(matrix):
    rows = matrix.shape[0]
    new = jnp.arange(DK, dtype=jnp.int32)
    old = jnp.where(new < HALF, 2 * new, 2 * (new - HALF) + 1)
    one_hot = (jnp.arange(DK, dtype=jnp.int32)[:, None] == old[None, :]).astype(BF)
    heads = matrix.reshape(rows * H, DK)
    return jnp.dot(heads, one_hot, preferred_element_type=F32).astype(BF).reshape(rows, H * DK)


def by_owner(matrix, width, share, mp_count):
    rows = matrix.shape[0]
    if share > 1:
        heads = jnp.repeat(matrix.reshape(rows, H, width), share, axis=1)
        return heads.transpose(1, 0, 2)
    return matrix.reshape(rows, mp_count, -1).transpose(1, 0, 2)


def assemble_kernel(scalars, *refs):
    pieces, out_ref = refs[:-1], refs[-1]
    rows = pieces[0].shape[0]
    for step, piece in enumerate(pieces):
        place = lax.rem(scalars[0] - step + len(pieces), len(pieces))
        out_ref[pl.ds(pl.multiple_of(place * rows, rows), rows), :] = piece[...]


def in_order(pieces, index):
    rows, width = pieces[0].shape
    grid_spec = pltpu.PrefetchScalarGridSpec(
        num_scalar_prefetch=1,
        grid=(1,),
        in_specs=[pl.BlockSpec((rows, width), lambda i, s: (0, 0))] * len(pieces),
        out_specs=pl.BlockSpec((rows * len(pieces), width), lambda i, s: (0, 0)),
    )
    return pl.pallas_call(
        assemble_kernel,
        grid_spec=grid_spec,
        out_shape=jax.ShapeDtypeStruct((rows * len(pieces), width), BF),
        compiler_params=pltpu.CompilerParams(vmem_limit_bytes=16 * 2**20),
        name="assemble",
    )(index.reshape(1).astype(jnp.int32), *pieces)


def exchanged(block, index, count):
    pieces = []
    for shift in range(count):
        piece = lax.dynamic_index_in_dim(block, (index + shift) % count, 0, keepdims=False)
        if shift:
            piece = lax.ppermute(piece, "mp", [(i, (i + shift) % count) for i in range(count)])
        pieces.append(piece)
    return pieces


def stacked(refs):
    return jnp.concatenate([ref[...] for ref in refs], axis=0)


def chunk(i):
    return pl.ds(pl.multiple_of(i * CHUNK, CHUNK), CHUNK)


def project_kernel(heads, scalars, *refs):
    halves, (gain_ref, cos_ref, sin_ref, w_ref, normed_ref, out_ref) = refs[:-6], refs[-6:]
    wq = heads * DK
    normed_ref[...] = rms_rows(stacked(halves), gain_ref[...])

    def turn(h, _):
        both = jnp.dot(normed_ref[...], w_ref[:, chunk(h)], preferred_element_type=F32)
        a, b = both[:, :HALF], both[:, HALF:]
        cos, sin = cos_ref[...], sin_ref[...]
        scale = jnp.where(h < heads, DK**-0.5, 1.0)
        out_ref[:, pl.ds(pl.multiple_of(h * DK, DK), HALF)] = ((a * cos - b * sin) * scale).astype(BF)
        out_ref[:, pl.ds(pl.multiple_of(h * DK + HALF, HALF), HALF)] = ((b * cos + a * sin) * scale).astype(BF)
        return _

    def plain(i, _):
        out_ref[:, chunk(i)] = jnp.dot(normed_ref[...], w_ref[:, chunk(i)], preferred_element_type=F32).astype(BF)
        return _

    lax.fori_loop(0, 2 * heads, turn, 0)
    lax.fori_loop(2 * wq // CHUNK, out_ref.shape[1] // CHUNK, plain, 0)


def project(halves, place, gain, cos, sin, w, heads):
    half, width = halves[0].shape
    rows = half * len(halves)
    out_width = w.shape[1]
    grid_spec = pltpu.PrefetchScalarGridSpec(
        num_scalar_prefetch=1,
        grid=(1,),
        in_specs=[pl.BlockSpec((half, width), lambda i, s: (0, 0))] * len(halves)
        + [
            pl.BlockSpec((1, width), lambda i, s: (0, 0)),
            pl.BlockSpec((rows, HALF), lambda i, s: (s[0], 0)),
            pl.BlockSpec((rows, HALF), lambda i, s: (s[0], 0)),
            pl.BlockSpec(w.shape, lambda i, s: (0, 0), pipeline_mode=pl.Buffered(1)),
        ],
        out_specs=[
            pl.BlockSpec((rows, width), lambda i, s: (0, 0)),
            pl.BlockSpec((rows, out_width), lambda i, s: (0, 0)),
        ],
    )
    return pl.pallas_call(
        lambda *refs: project_kernel(heads, *refs),
        grid_spec=grid_spec,
        out_shape=[jax.ShapeDtypeStruct((rows, width), BF), jax.ShapeDtypeStruct((rows, out_width), BF)],
        compiler_params=pltpu.CompilerParams(vmem_limit_bytes=20 * 2**20),
        cost_estimate=pl.CostEstimate(flops=rows * width * out_width // 2, bytes_accessed=2**20, transcendentals=0),
        name="project",
    )(place.reshape(1).astype(jnp.int32), *halves, gain.reshape(1, -1), cos, sin, w)


def retention_kernel(dims, scalars, run_col, run_row, x_hbm, *refs):
    heads, share, wq, wv, wg, count, own = dims
    blocks, w_hbm, out_refs = refs[:count], refs[count], refs[count + 1 : -7]
    held_ref, x_ref, kept_ref, gated_ref, wg_ref, wo_ref, arrived = refs[-7:]
    rows, width = x_ref.shape
    order = [own] + [k for k in range(count) if k != own]
    copies = [pltpu.make_async_copy(blocks[k], held_ref.at[k], arrived.at[k]) for k in order]
    copies += [
        pltpu.make_async_copy(x_hbm, x_ref, arrived.at[count]),
        pltpu.make_async_copy(w_hbm.at[:, :wg], wg_ref, arrived.at[count + 1]),
        pltpu.make_async_copy(w_hbm.at[:, wg:], wo_ref, arrived.at[count + 2]),
    ]
    for copy in copies:
        copy.start()
    device = scalars[2]
    block = lax.rem(device - own + count, count)
    live = block * rows + lax.broadcasted_iota(jnp.int32, (rows, 1), 0) < scalars[0]

    def add(past, held, first):
        for h in range(heads):
            scores = lax.dot_general(
                held_ref[own, :, h * DK : (h + 1) * DK],
                held_ref[past, :, wq + h * DK : wq + (h + 1) * DK],
                (((1,), (1,)), ((), ())),
                preferred_element_type=F32,
            )
            gap = run_col[:, h : h + 1] - run_row[held, h : h + 1, :]
            if first:
                t = lax.broadcasted_iota(jnp.int32, (rows, rows), 0)
                s = lax.broadcasted_iota(jnp.int32, (rows, rows), 1)
                gap = jnp.where(t >= s, gap, -jnp.inf)
            weights = (scores * jnp.exp(gap)).astype(BF)
            values = held_ref[past, :, 2 * wq + h * DV : 2 * wq + (h + 1) * DV]
            more = jnp.dot(weights, values, preferred_element_type=F32)
            place = slice(h * DV, (h + 1) * DV)
            kept_ref[:, place] = more if first else kept_ref[:, place] + more

    copies[0].wait()
    add(own, block, True)
    for copy in copies[1:count]:
        copy.wait()

    def earlier(held, _):
        add(lax.rem(device - held + count, count), held, False)
        return _

    lax.fori_loop(0, block, earlier, 0)

    for h in range(heads):
        kept = kept_ref[:, h * DV : (h + 1) * DV]
        mean = jnp.mean(kept, axis=-1, keepdims=True)
        spread = jnp.mean(kept * kept, axis=-1, keepdims=True) - mean * mean
        normed = (kept - mean) * lax.rsqrt(spread + 1e-05)
        if share > 1:
            mine = normed[:, :wg]
            for bit in range(1, share):
                mine = jnp.where(scalars[1] == bit, normed[:, bit * wg : (bit + 1) * wg], mine)
            kept_ref[:, :wg] = mine
        else:
            kept_ref[:, h * DV : (h + 1) * DV] = normed

    copies[count].wait()
    copies[count + 1].wait()

    def gating(i, _):
        gate = jnp.dot(x_ref[...], wg_ref[:, chunk(i)], preferred_element_type=F32).astype(BF).astype(F32)
        gate = gate / (1.0 + jnp.exp(-gate))
        gated_ref[:, chunk(i)] = jnp.where(live, gate * kept_ref[:, chunk(i)], 0.0).astype(BF)
        return _

    lax.fori_loop(0, wg // CHUNK, gating, 0)
    copies[count + 2].wait()
    half = rows // len(out_refs)

    def leaving(i, _):
        branch = lax.dot_general(
            gated_ref[...], wo_ref[chunk(i), :], (((1,), (1,)), ((), ())), preferred_element_type=F32
        ).astype(BF)
        for k, out_ref in enumerate(out_refs):
            out_ref[:, chunk(i)] = branch[k * half : (k + 1) * half]
        return _

    lax.fori_loop(0, width // CHUNK, leaving, 0)


def retention(own, index, x, running, length, partner, blocks, w, heads, share):
    count, (rows, width) = len(blocks), x.shape
    wq, wv, wg = heads * DK, heads * DV, w.shape[1] // 2
    dims = (heads, share, wq, wv, wg, count, own)
    scalars = jnp.stack([length, partner, index]).astype(jnp.int32)
    x, w, *blocks = [pltpu.with_memory_space_constraint(a, pltpu.HBM) for a in (x, w, *blocks)]
    by_row = running.T.reshape(heads, count, rows).transpose(1, 0, 2)
    grid_spec = pltpu.PrefetchScalarGridSpec(
        num_scalar_prefetch=1,
        grid=(1,),
        in_specs=[
            pl.BlockSpec((rows, heads), lambda i, s: (lax.rem(s[2] - own + count, count), 0)),
            pl.BlockSpec(by_row.shape, lambda i, s: (0, 0, 0)),
        ]
        + [pl.BlockSpec(memory_space=pl.ANY)] * (count + 2),
        out_specs=[pl.BlockSpec((rows // STREAMS, width), lambda i, s: (0, 0))] * STREAMS,
        scratch_shapes=[
            pltpu.VMEM((count, *blocks[0].shape), BF),
            pltpu.VMEM((rows, width), BF),
            pltpu.VMEM((rows, wv), F32),
            pltpu.VMEM((rows, wg), BF),
            pltpu.VMEM((width, wg), BF),
            pltpu.VMEM((width, wg), BF),
            pltpu.SemaphoreType.DMA((count + 3,)),
        ],
    )
    return pl.pallas_call(
        lambda *refs: retention_kernel(dims, *refs),
        grid_spec=grid_spec,
        out_shape=[jax.ShapeDtypeStruct((rows // STREAMS, width), BF)] * STREAMS,
        compiler_params=pltpu.CompilerParams(vmem_limit_bytes=24 * 2**20),
        cost_estimate=pl.CostEstimate(flops=3 * 10**9, bytes_accessed=2**20, transcendentals=10**5),
        name="retention",
    )(scalars, running, by_row, x, *blocks, w)


def middle_kernel(came_ref, part_ref, token_ref, gain_ref, residual_ref, normed_ref):
    branch = came_ref[...].astype(F32) + part_ref[...].astype(F32)
    residual_ref[...] = (token_ref[...].astype(F32) + branch).astype(BF)
    normed_ref[...] = rms_rows(residual_ref[...], gain_ref[...])


def middle(came, part, tokens, gain):
    rows, width = tokens.shape
    step = min(rows, 64)
    block = pl.BlockSpec((step, width), lambda i: (i, 0))
    return pl.pallas_call(
        middle_kernel,
        grid=(rows // step,),
        in_specs=[block, block, block, pl.BlockSpec((1, width), lambda i: (0, 0))],
        out_specs=[block, block],
        out_shape=[jax.ShapeDtypeStruct((rows, width), BF)] * 2,
        compiler_params=pltpu.CompilerParams(vmem_limit_bytes=16 * 2**20),
        name="middle",
    )(came, part, tokens, gain.reshape(1, -1))


def ffn_kernel(count, scalars, *refs):
    w_ref, out_ref, x_ref = refs[count], refs[-2], refs[-1]
    x_ref[...] = stacked(refs[:count])
    chunks = out_ref.shape[1] // CHUNK

    def one(i, _):
        gate = jnp.dot(x_ref[...], w_ref[:, chunk(i)], preferred_element_type=F32)
        up = jnp.dot(x_ref[...], w_ref[:, chunk(i + chunks)], preferred_element_type=F32)
        out_ref[:, chunk(i)] = (gate / (1.0 + jnp.exp(-gate)) * up).astype(BF)
        return _

    lax.fori_loop(0, chunks, one, 0)


def ffn(halves, place, w, held):
    half, width = halves[0].shape
    rows = half * len(halves)
    out_width = w.shape[1] // 2
    extra = [] if held is None else [held]
    grid_spec = pltpu.PrefetchScalarGridSpec(
        num_scalar_prefetch=1,
        grid=(1,),
        in_specs=[pl.BlockSpec((half, width), lambda i, s: (0, 0))] * len(halves)
        + [pl.BlockSpec(w.shape, lambda i, s: (0, 0))]
        + [pl.BlockSpec(memory_space=pl.ANY)] * len(extra),
        out_specs=pl.BlockSpec((rows, out_width), lambda i, s: (s[0], 0)),
        scratch_shapes=[pltpu.VMEM((rows, width), BF)],
    )
    return pl.pallas_call(
        lambda *refs: ffn_kernel(len(halves), *refs),
        grid_spec=grid_spec,
        out_shape=jax.ShapeDtypeStruct((SPAN, out_width), BF),
        input_output_aliases={len(halves) + 2: 0} if extra else {},
        compiler_params=pltpu.CompilerParams(vmem_limit_bytes=18 * 2**20),
        cost_estimate=pl.CostEstimate(
            flops=2 * rows * width * w.shape[1], bytes_accessed=2 * w.size, transcendentals=rows * out_width
        ),
        name="ffn",
    )(place.reshape(1).astype(jnp.int32), *halves, w, *extra)


def per_device(
    tokens, norm_gain, mlp_gain, lengths, log_decay,
    query_master, key_master, value_master, swish_master, output_master, ffn_gate_master, ffn_up_master,
):
    mp_count = lax.axis_size("mp")
    mp_index = lax.axis_index("mp")
    share = max(1, mp_count // H)
    heads = max(1, H // mp_count)

    angles = jnp.arange(SPAN, dtype=jnp.int32).astype(F32)[:, None] * jnp.exp(
        (2 * jnp.arange(HALF, dtype=jnp.int32)).astype(F32) * (-math.log(10000.0) / DK)
    )
    cos, sin = jnp.cos(angles), jnp.sin(angles)
    first_head = mp_index // share * heads
    running = jnp.cumsum(lax.dynamic_slice_in_dim(log_decay, first_head, heads, 1), axis=0)

    qkv_pieces = exchanged(
        jnp.concatenate(
            [
                by_owner(even_odd(query_master.astype(BF)), DK, share, mp_count),
                by_owner(even_odd(key_master.astype(BF)), DK, share, mp_count),
                by_owner(value_master.astype(BF), DV, share, mp_count),
            ],
            axis=2,
        ),
        mp_index,
        mp_count,
    )
    gate_out_block = jnp.concatenate(
        [by_owner(swish_master.astype(BF), DV, 1, mp_count), by_owner(output_master.astype(BF).T, DV, 1, mp_count)],
        axis=2,
    )
    gate_out_block, qkv_pieces = lax.optimization_barrier((gate_out_block, qkv_pieces))
    gate_out_pieces = exchanged(gate_out_block, mp_index, mp_count)
    qkv_rows = in_order(qkv_pieces, mp_index)
    w_qkv = lax.all_gather(qkv_rows, "dp", axis=0, tiled=True)

    order = [(i, (i + 1) % mp_count) for i in range(mp_count)]

    def onward(halves):
        return [lax.ppermute(half, "mp", order) for half in halves]

    def projected(step):
        return project(blocks[step], (mp_index - step) % mp_count, norm_gain, cos, sin, w_qkv, heads)

    def held_back(later, *first):
        return lax.optimization_barrier((later, first))[0]

    half = tokens.shape[0] // STREAMS
    token_halves = [tokens[k * half : (k + 1) * half] for k in range(STREAMS)]
    masters = held_back((ffn_gate_master, ffn_up_master), qkv_rows)
    ffn_block = jnp.concatenate([by_owner(m.astype(BF), DV, 1, mp_count) for m in masters], axis=2)
    blocks, done = [held_back(token_halves, qkv_rows)], []
    for step in range(1, mp_count):
        blocks.append(onward(blocks[-1]))
        if step == 1:
            blocks[1] = [held_back(h, ffn_block) for h in blocks[1]]
        else:
            done.append(projected(step - 2))
            if step < mp_count - 1:
                blocks[step] = [held_back(h, done[-1]) for h in blocks[step]]
            if step == 2:
                w_gate_out = lax.all_gather(in_order(gate_out_pieces, mp_index), "dp", axis=0, tiled=True)
    done.append(projected(mp_count - 2))
    ffn_block, blocks[-1] = held_back((ffn_block, blocks[-1]), done, blocks[-1])
    ffn_pieces = exchanged(ffn_block, mp_index, mp_count)
    done.append(projected(mp_count - 1))
    normed, qkv = [d[0] for d in done], [d[1] for d in done]

    for step in range(mp_count):
        own = (1 + step) % mp_count
        parts = retention(
            own, mp_index, normed[own], running, lengths[0], mp_index % share, qkv, w_gate_out, heads, share
        )
        if step < mp_count - 1:
            later = (2 + step) % mp_count
            normed[later] = held_back(normed[later], parts)
        if step == 0:
            ffn_pieces = held_back(ffn_pieces, parts)
            w_ffn = lax.all_gather(in_order(ffn_pieces, mp_index), "dp", axis=0, tiled=True)
            totals = parts
        elif step < mp_count - 1:
            totals = [(c.astype(F32) + p.astype(F32)).astype(BF) for c, p in zip(came, parts)]
        if step < mp_count - 1:
            came = onward(totals)
    finished = [middle(c, p, t, mlp_gain) for c, p, t in zip(came, parts, token_halves)]
    residual = jnp.concatenate([f[0] for f in finished], axis=0)
    moving = [f[1] for f in finished]
    hidden = None
    for step in range(mp_count):
        here = moving
        if step < mp_count - 1:
            arriving = onward(moving)
        hidden = ffn(here, (mp_index - step) % mp_count, w_ffn, hidden)
        if step < mp_count - 1:
            moving = [held_back(h, hidden) for h in arriving] if step else arriving
    return residual, hidden


def solution(mesh):
    rows, columns = P(("dp", "mp"), None), P(None, ("dp", "mp"))
    placed = (rows, P(), P(), P("dp"), P("dp", None), rows, rows, rows, rows, columns, rows, rows)
    return jax.shard_map(
        per_device, mesh=mesh, in_specs=placed, out_specs=(rows, P("dp", "mp")), check_vma=False
    )
```

profile of v0, /device:TPU:0, one launch (start us, length us, event | category | flops | bytes accessed | tf_op | source)
XLA Modules:
  0.0 311.7 jit_solution(2854095975781832382)
XLA Ops:
  7.3 1.3 convert_element_type.121
  10.7 3.1 collective-permute-start
  13.8 2.6 collective-permute-start.1
  16.4 1.3 collective-permute-start.2
  18.1 5.0 %collective-permute-done.refs_1_ = bf16[64,2048]{1,0:T(8,128)(2,1)S(1)} collective-permute-done((bf16[64,2048]{1,0:T(8,128)(2,1)S(1)}, bf16[64,2048]{1,0:T(8,128)(2,1)S(1)}, u32[]{:S(2)}, u32[]{:S(2)}) %collective-permute-start) | collective-permute-done | bytes 262176 | tf_op jit(solution)/shard_map/ppermute | solution.py:75
  23.1 10.4 %collective-permute-done.1.refs_2_ = bf16[64,2048]{1,0:T(8,128)(2,1)S(1)} collective-permute-done((bf16[64,2048]{1,0:T(8,128)(2,1)S(1)}, bf16[64,2048]{1,0:T(8,128)(2,1)S(1)}, u32[]{:S(2)}, u32[]{:S(2)}) %collective-permute-start.1) | collective-permute-done | bytes 262176 | tf_op jit(solution)/shard_map/ppermute | solution.py:75
  33.5 1.0 assemble.3
  34.7 6.1 %collective-permute-start.9 = (bf16[64,2048]{1,0:T(8,128)(2,1)S(1)}, bf16[64,2048]{1,0:T(8,128)(2,1)S(1)}, u32[]{:S(2)}, u32[]{:S(2)}) collective-permute-start(bf16[64,2048]{1,0:T(8,128)(2,1)S(1)} %get-tuple-element.102), channel_id=1, source_target_pairs={{0,1},{1,2},{2,3},{3,0},{4,5},{5,6},{6,7},{7,4},{8,9},{9,10},{10,1... | collective-permute-start | bytes 786440 | tf_op jit(solution)/shard_map/ppermute | solution.py:75
  40.9 1.6 collective-permute-start.10
  43.3 5.9 %collective-permute-done.9.refs_1_ = bf16[64,2048]{1,0:T(8,128)(2,1)S(1)} collective-permute-done((bf16[64,2048]{1,0:T(8,128)(2,1)S(1)}, bf16[64,2048]{1,0:T(8,128)(2,1)S(1)}, u32[]{:S(2)}, u32[]{:S(2)}) %collective-permute-start.9) | collective-permute-done | bytes 262176 | tf_op jit(solution)/shard_map/ppermute | solution.py:75
  49.3 9.4 %collective-permute-done.10.refs_2_ = bf16[64,2048]{1,0:T(8,128)(2,1)S(1)} collective-permute-done((bf16[64,2048]{1,0:T(8,128)(2,1)S(1)}, bf16[64,2048]{1,0:T(8,128)(2,1)S(1)}, u32[]{:S(2)}, u32[]{:S(2)}) %collective-permute-start.10) | collective-permute-done | bytes 262176 | tf_op jit(solution)/shard_map/ppermute | solution.py:75
  58.7 1.1 assemble.4
  60.0 6.1 %collective-permute-start.3 = (bf16[128,2048]{1,0:T(8,128)(2,1)S(1)}, bf16[128,2048]{1,0:T(8,128)(2,1)S(1)}, u32[]{:S(2)}, u32[]{:S(2)}) collective-permute-start(bf16[128,2048]{1,0:T(8,128)(2,1)S(1)} %get-tuple-element.53.refs_1_.token_ref), channel_id=1, source_target_pairs={{0,1},{1,2},{2,3},{3,0},{4,5},{5,6},{6,7},{7,4},{8,9},{9,10},{10,1... | collective-permute-start | bytes 1572872 | tf_op jit(solution)/shard_map/ppermute | solution.py:362
  66.8 1.6 convert_element_type.123
  68.4 1.3 convert_element_type.122
  69.8 1.1 pad_maximum_fusion.2
  70.8 9.9 %collective-permute-done.3.refs_1_ = bf16[128,2048]{1,0:T(8,128)(2,1)S(1)} collective-permute-done((bf16[128,2048]{1,0:T(8,128)(2,1)S(1)}, bf16[128,2048]{1,0:T(8,128)(2,1)S(1)}, u32[]{:S(2)}, u32[]{:S(2)}) %collective-permute-start.3) | collective-permute-done | bytes 524320 | tf_op jit(solution)/shard_map/ppermute | solution.py:362
  80.9 11.0 %collective-permute-done.4.refs_2_ = bf16[128,2048]{1,0:T(8,128)(2,1)S(1)} collective-permute-done((bf16[128,2048]{1,0:T(8,128)(2,1)S(1)}, bf16[128,2048]{1,0:T(8,128)(2,1)S(1)}, u32[]{:S(2)}, u32[]{:S(2)}) %collective-permute-start.4) | collective-permute-done | bytes 524320 | tf_op jit(solution)/shard_map/ppermute | solution.py:362
  92.1 1.9 multiply_sine_fusion
  94.1 3.4 %copy-done.2 = bf16[2048,2048]{1,0:T(8,128)(2,1)S(1)} copy-done((bf16[2048,2048]{1,0:T(8,128)(2,1)S(1)}, bf16[2048,2048]{1,0:T(8,128)(2,1)}, u32[]{:S(2)}) %copy-start.2) | copy-done | bytes 8388632
  97.4 4.2 %project.5 = (bf16[256,2048]{1,0:T(8,128)(2,1)S(1)}, bf16[256,2048]{1,0:T(8,128)(2,1)S(1)}) custom-call(s32[1]{0:T(128)} %bitcast.21.refs_0_, bf16[128,2048]{1,0:T(8,128)(2,1)S(1)} %get-tuple-element.53.refs_1_.token_ref, bf16[128,2048]{1,0:T(8,128)(2,1)S(1)} %get-tuple-element.57.refs_2_.token_ref, f32[1,2048]{1,0:T(1,128)S(1)} %bitcast.94, ...), custom_call_target="tpu_custom_call" | custom-call | flops 536870912 | bytes 1048576 | tf_op jit(solution)/shard_map/project/pallas_call | solution.py:129
  102.6 1.0 copy-done.10
  103.7 1.3 collective-permute-start.7
  105.0 9.5 %collective-permute-done.6.refs_2_ = bf16[128,2048]{1,0:T(8,128)(2,1)} collective-permute-done((bf16[128,2048]{1,0:T(8,128)(2,1)S(1)}, bf16[128,2048]{1,0:T(8,128)(2,1)}, u32[]{:S(2)}, u32[]{:S(2)}) %collective-permute-start.6) | collective-permute-done | bytes 524320 | tf_op jit(solution)/shard_map/ppermute | solution.py:362
  116.2 3.4 %copy-done.3 = bf16[2048,2048]{1,0:T(8,128)(2,1)S(1)} copy-done((bf16[2048,2048]{1,0:T(8,128)(2,1)S(1)}, bf16[2048,2048]{1,0:T(8,128)(2,1)}, u32[]{:S(2)}) %copy-start.3) | copy-done | bytes 8388632
  119.6 1.0 copy-done.15
  120.6 4.2 %project.4 = (bf16[256,2048]{1,0:T(8,128)(2,1)S(1)}, bf16[256,2048]{1,0:T(8,128)(2,1)S(1)}) custom-call(s32[1]{0:T(128)} %bitcast.5.refs_0_, bf16[128,2048]{1,0:T(8,128)(2,1)S(1)} %collective-permute-done.3.refs_1_, bf16[128,2048]{1,0:T(8,128)(2,1)S(1)} %copy-done.15, f32[1,2048]{1,0:T(1,128)S(1)} %bitcast.95, f32[1024,128]{1,0:T(8,128)S(1)} %get-tuple-element.111.refs_4_, ...), custom_call_target="tpu_custom_call" | custom-call | flops 536870912 | bytes 1048576 | tf_op jit(solution)/shard_map/project/pallas_call | solution.py:129
  125.8 1.0 copy-done.13
  126.8 5.6 %project.6 = (bf16[256,2048]{1,0:T(8,128)(2,1)S(1)}, bf16[256,2048]{1,0:T(8,128)(2,1)S(1)}) custom-call(s32[1]{0:T(128)} %bitcast.22.refs_0_, bf16[128,2048]{1,0:T(8,128)(2,1)} %collective-permute-done.5.refs_1_, bf16[128,2048]{1,0:T(8,128)(2,1)} %collective-permute-done.6.refs_2_, f32[1,2048]{1,0:T(1,128)S(1)} %bitcast.96, ...), custom_call_target="tpu_custom_call" | custom-call | flops 536870912 | bytes 1048576 | tf_op jit(solution)/shard_map/project/pallas_call | solution.py:129
  133.3 2.4 collective-permute-done.8.refs_2_
  137.1 1.8 collective-permute-start.22
  139.0 1.5 collective-permute-start.23
  140.5 5.4 %project.7 = (bf16[256,2048]{1,0:T(8,128)(2,1)S(1)}, bf16[256,2048]{1,0:T(8,128)(2,1)S(1)}) custom-call(s32[1]{0:T(128)} %bitcast.23.refs_0_, bf16[128,2048]{1,0:T(8,128)(2,1)} %collective-permute-done.7.refs_1_, bf16[128,2048]{1,0:T(8,128)(2,1)} %collective-permute-done.8.refs_2_, f32[1,2048]{1,0:T(1,128)S(1)} %bitcast.97, ...), custom_call_target="tpu_custom_call" | custom-call | flops 536870912 | bytes 1048576 | tf_op jit(solution)/shard_map/project/pallas_call | solution.py:129
  147.9 2.4 all-gather.6.cloned.1.call-done.refs_8_
  150.2 9.4 %retention.4 = (bf16[128,2048]{1,0:T(8,128)(2,1)S(1)}, bf16[128,2048]{1,0:T(8,128)(2,1)S(1)}) custom-call(s32[3]{0:T(128)S(1)} %pad_add_fusion.refs_0_, f32[1024,2]{1,0:T(8,128)S(1)} %bitcast.86, f32[4,2,256]{2,1,0:T(2,128)S(1)} %bitcast.90, bf16[256,2048]{1,0:T(8,128)(2,1)} %copy-done.13, bf16[256,2048]{1,0:T(8,128)(2,1)} %copy-done.6, ...), custom_call_target="tpu_custom_call" | custom-call | flops 3000000000 | bytes 1048576 | tf_op jit(solution)/shard_map/retention/pallas_call | solution.py:250
  159.7 2.0 assemble.5
  161.7 3.3 %collective-permute-start.12 = (bf16[128,2048]{1,0:T(8,128)(2,1)S(1)}, bf16[128,2048]{1,0:T(8,128)(2,1)S(1)}, u32[]{:S(2)}, u32[]{:S(2)}) collective-permute-start(bf16[128,2048]{1,0:T(8,128)(2,1)S(1)} %get-tuple-element.71), channel_id=1, source_target_pairs={{0,1},{1,2},{2,3},{3,0},{4,5},{5,6},{6,7},{7,4},{8,9},{9,10},{10,1... | collective-permute-start | bytes 1572872 | tf_op jit(solution)/shard_map/ppermute | solution.py:362
  165.1 9.2 %retention.5 = (bf16[128,2048]{1,0:T(8,128)(2,1)S(1)}, bf16[128,2048]{1,0:T(8,128)(2,1)S(1)}) custom-call(s32[3]{0:T(128)S(1)} %pad_add_fusion.refs_0_, f32[1024,2]{1,0:T(8,128)S(1)} %bitcast.87, f32[4,2,256]{2,1,0:T(2,128)S(1)} %bitcast.91, bf16[256,2048]{1,0:T(8,128)(2,1)} %copy-done.11, bf16[256,2048]{1,0:T(8,128)(2,1)} %copy-done.6, ...), custom_call_target="tpu_custom_call" | custom-call | flops 3000000000 | bytes 1048576 | tf_op jit(solution)/shard_map/retention/pallas_call | solution.py:250
  174.3 4.0 %collective-permute-done.12 = bf16[128,2048]{1,0:T(8,128)(2,1)S(1)} collective-permute-done((bf16[128,2048]{1,0:T(8,128)(2,1)S(1)}, bf16[128,2048]{1,0:T(8,128)(2,1)S(1)}, u32[]{:S(2)}, u32[]{:S(2)}) %collective-permute-start.12) | collective-permute-done | bytes 524320 | tf_op jit(solution)/shard_map/ppermute | solution.py:362
  178.5 1.6 collective-permute-start.13
  180.1 9.5 %collective-permute-done.15 = bf16[128,2048]{1,0:T(8,128)(2,1)S(1)} collective-permute-done((bf16[128,2048]{1,0:T(8,128)(2,1)S(1)}, bf16[128,2048]{1,0:T(8,128)(2,1)S(1)}, u32[]{:S(2)}, u32[]{:S(2)}) %collective-permute-start.15) | collective-permute-done | bytes 524320 | tf_op jit(solution)/shard_map/ppermute | solution.py:362
  189.7 1.6 collective-permute-start.16
  191.3 9.2 %retention.6 = (bf16[128,2048]{1,0:T(8,128)(2,1)S(1)}, bf16[128,2048]{1,0:T(8,128)(2,1)S(1)}) custom-call(s32[3]{0:T(128)S(1)} %pad_add_fusion.refs_0_, f32[1024,2]{1,0:T(8,128)S(1)} %bitcast.88, f32[4,2,256]{2,1,0:T(2,128)S(1)} %bitcast.92, bf16[256,2048]{1,0:T(8,128)(2,1)} %copy-done.12, bf16[256,2048]{1,0:T(8,128)(2,1)} %copy-done.6, ...), custom_call_target="tpu_custom_call" | custom-call | flops 3000000000 | bytes 1048576 | tf_op jit(solution)/shard_map/retention/pallas_call | solution.py:250
  201.0 1.6 collective-permute-start.14
  202.5 9.5 %collective-permute-done.16 = bf16[128,2048]{1,0:T(8,128)(2,1)S(1)} collective-permute-done((bf16[128,2048]{1,0:T(8,128)(2,1)S(1)}, bf16[128,2048]{1,0:T(8,128)(2,1)S(1)}, u32[]{:S(2)}, u32[]{:S(2)}) %collective-permute-start.16) | collective-permute-done | bytes 524320 | tf_op jit(solution)/shard_map/ppermute | solution.py:362
  212.2 1.6 collective-permute-start.17
  213.8 9.3 %retention.7 = (bf16[128,2048]{1,0:T(8,128)(2,1)S(1)}, bf16[128,2048]{1,0:T(8,128)(2,1)S(1)}) custom-call(s32[3]{0:T(128)S(1)} %pad_add_fusion.refs_0_, f32[1024,2]{1,0:T(8,128)S(1)} %bitcast.89, f32[4,2,256]{2,1,0:T(2,128)S(1)} %bitcast.93, bf16[256,2048]{1,0:T(8,128)(2,1)} %copy-done.10, bf16[256,2048]{1,0:T(8,128)(2,1)} %copy-done.6, ...), custom_call_target="tpu_custom_call" | custom-call | flops 3000000000 | bytes 1048576 | tf_op jit(solution)/shard_map/retention/pallas_call | solution.py:250
  223.8 1.6 collective-permute-start.18
  225.4 9.2 %collective-permute-done.17.came_ref = bf16[128,2048]{1,0:T(8,128)(2,1)S(1)} collective-permute-done((bf16[128,2048]{1,0:T(8,128)(2,1)S(1)}, bf16[128,2048]{1,0:T(8,128)(2,1)S(1)}, u32[]{:S(2)}, u32[]{:S(2)}) %collective-permute-start.17) | collective-permute-done | bytes 524320 | tf_op jit(solution)/shard_map/ppermute | solution.py:362
  235.0 1.6 collective-permute-start.20
  236.6 9.3 %collective-permute-done.18.refs_1_ = bf16[128,2048]{1,0:T(8,128)(2,1)} collective-permute-done((bf16[128,2048]{1,0:T(8,128)(2,1)S(1)}, bf16[128,2048]{1,0:T(8,128)(2,1)}, u32[]{:S(2)}, u32[]{:S(2)}) %collective-permute-start.18) | collective-permute-done | bytes 524320 | tf_op jit(solution)/shard_map/ppermute | solution.py:362
  245.9 1.5 collective-permute-start.19
  247.4 9.7 %collective-permute-done.20.refs_2_ = bf16[128,2048]{1,0:T(8,128)(2,1)} collective-permute-done((bf16[128,2048]{1,0:T(8,128)(2,1)S(1)}, bf16[128,2048]{1,0:T(8,128)(2,1)}, u32[]{:S(2)}, u32[]{:S(2)}) %collective-permute-start.20) | collective-permute-done | bytes 524320 | tf_op jit(solution)/shard_map/ppermute | solution.py:362
  257.1 1.5 collective-permute-start.25
  258.6 3.4 %copy-done.4 = bf16[2048,2048]{1,0:T(8,128)(2,1)S(1)} copy-done((bf16[2048,2048]{1,0:T(8,128)(2,1)S(1)}, bf16[2048,2048]{1,0:T(8,128)(2,1)}, u32[]{:S(2)}) %copy-start.4) | copy-done | bytes 8388632
  262.0 3.9 %ffn.4.refs_4_ = bf16[1024,1024]{1,0:T(8,128)(2,1)} custom-call(s32[1]{0:T(128)} %bitcast.21.refs_0_, bf16[128,2048]{1,0:T(8,128)(2,1)S(1)} %get-tuple-element.85.refs_1_, bf16[128,2048]{1,0:T(8,128)(2,1)S(1)} %get-tuple-element.86.refs_2_, bf16[2048,2048]{1,0:T(8,128)(2,1)S(1)} %copy-done.4), custom_call_target="tpu_custom_call" | custom-call | flops 2147483648 | bytes 8388608 | tf_op jit(solution)/shard_map/ffn/pallas_call | solution.py:309
  265.9 5.1 %ffn.5.refs_4_ = bf16[1024,1024]{1,0:T(8,128)(2,1)} custom-call(s32[1]{0:T(128)} %bitcast.5.refs_0_, bf16[128,2048]{1,0:T(8,128)(2,1)} %collective-permute-done.18.refs_1_, bf16[128,2048]{1,0:T(8,128)(2,1)} %collective-permute-done.20.refs_2_, bf16[2048,2048]{1,0:T(8,128)(2,1)S(1)} %copy-done.5, ...), custom_call_target="tpu_custom_call", output_to_operand_aliasing={{}: (4, {})} | custom-call | flops 2147483648 | bytes 8388608 | tf_op jit(solution)/shard_map/ffn/pallas_call | solution.py:309
  271.0 8.4 %collective-permute-done.25.refs_2_ = bf16[128,2048]{1,0:T(8,128)(2,1)S(1)} collective-permute-done((bf16[128,2048]{1,0:T(8,128)(2,1)}, bf16[128,2048]{1,0:T(8,128)(2,1)S(1)}, u32[]{:S(2)}, u32[]{:S(2)}) %collective-permute-start.25) | collective-permute-done | bytes 524320 | tf_op jit(solution)/shard_map/ppermute | solution.py:362
  279.5 1.5 collective-permute-start.26
  281.0 1.0 pad_maximum_fusion.3
  282.0 3.9 %ffn.6.refs_4_ = bf16[1024,1024]{1,0:T(8,128)(2,1)} custom-call(s32[1]{0:T(128)} %bitcast.22.refs_0_, bf16[128,2048]{1,0:T(8,128)(2,1)S(1)} %collective-permute-done.19.refs_1_, bf16[128,2048]{1,0:T(8,128)(2,1)S(1)} %collective-permute-done.25.refs_2_, bf16[2048,2048]{1,0:T(8,128)(2,1)S(1)} %copy-done.5, ...), custom_call_target="tpu_custom_call", output_to_operand_aliasing={{}: (4, {})} | custom-call | flops 2147483648 | bytes 8388608 | tf_op jit(solution)/shard_map/ffn/pallas_call | solution.py:309
  285.9 4.8 %collective-permute-done.24.refs_1_ = bf16[128,2048]{1,0:T(8,128)(2,1)S(1)} collective-permute-done((bf16[128,2048]{1,0:T(8,128)(2,1)S(1)}, bf16[128,2048]{1,0:T(8,128)(2,1)S(1)}, u32[]{:S(2)}, u32[]{:S(2)}) %collective-permute-start.24) | collective-permute-done | bytes 524320 | tf_op jit(solution)/shard_map/ppermute | solution.py:362
  290.7 10.6 %collective-permute-done.26.refs_2_ = bf16[128,2048]{1,0:T(8,128)(2,1)S(1)} collective-permute-done((bf16[128,2048]{1,0:T(8,128)(2,1)S(1)}, bf16[128,2048]{1,0:T(8,128)(2,1)S(1)}, u32[]{:S(2)}, u32[]{:S(2)}) %collective-permute-start.26) | collective-permute-done | bytes 524320 | tf_op jit(solution)/shard_map/ppermute | solution.py:362
  301.3 3.9 %ffn.7 = bf16[1024,1024]{1,0:T(8,128)(2,1)} custom-call(s32[1]{0:T(128)} %bitcast.23.refs_0_, bf16[128,2048]{1,0:T(8,128)(2,1)S(1)} %collective-permute-done.24.refs_1_, bf16[128,2048]{1,0:T(8,128)(2,1)S(1)} %collective-permute-done.26.refs_2_, bf16[2048,2048]{1,0:T(8,128)(2,1)S(1)} %copy-done.5, ...), custom_call_target="tpu_custom_call", output_to_operand_aliasing={{}: (4, {})} | custom-call | flops 2147483648 | bytes 8388608 | tf_op jit(solution)/shard_map/ffn/pallas_call | solution.py:309
  (116 shorter events, 14.0 us)
Async XLA Ops:
  7.2 59.0 %copy-start = (f32[1024,8]{0,1:T(8,128)S(1)}, f32[1024,8]{0,1:T(8,128)}, u32[]{:S(2)}) copy-start(f32[1024,8]{0,1:T(8,128)} %param.16) | copy-start | bytes 98308
  7.2 1.5 copy-start.22
  7.2 86.9 %all-gather.4.cloned.1.call-start = ((), (), s32[]{:S(2)}) async-start(), calls=%async_computation | async-start | bytes 9437184 | tf_op jit(solution)/shard_map/all_gather | solution.py:357
  8.6 1.0 copy-start.23
  10.5 7.2 %copy-start.19 = (f32[4096,64]{0,1:T(8,128)S(1)}, f32[4096,64]{0,1:T(8,128)}, u32[]{:S(2)}) copy-start(f32[4096,64]{0,1:T(8,128)} %param.21) | copy-start | bytes 3145732
  10.6 7.2 %copy-start.20 = (f32[64,4096]{1,0:T(8,128)S(1)}, f32[64,4096]{1,0:T(8,128)}, u32[]{:S(2)}) copy-start(f32[64,4096]{1,0:T(8,128)} %param.20) | copy-start | bytes 3145732
  10.7 12.4 %collective-permute-start = (bf16[64,2048]{1,0:T(8,128)(2,1)S(1)}, bf16[64,2048]{1,0:T(8,128)(2,1)S(1)}, u32[]{:S(2)}, u32[]{:S(2)}) collective-permute-start(bf16[64,2048]{1,0:T(8,128)(2,1)S(1)} %get-tuple-element.108), channel_id=1, source_target_pairs={{0,1},{1,2},{2,3},{3,0},{4,5},{5,6},{6,7},{7,4},{8,9},{9,10},{10,1... | collective-permute-start | bytes 786440 | tf_op jit(solution)/shard_map/ppermute | solution.py:75
  13.8 19.7 %collective-permute-start.1 = (bf16[64,2048]{1,0:T(8,128)(2,1)S(1)}, bf16[64,2048]{1,0:T(8,128)(2,1)S(1)}, u32[]{:S(2)}, u32[]{:S(2)}) collective-permute-start(bf16[64,2048]{1,0:T(8,128)(2,1)S(1)} %get-tuple-element.107), channel_id=1, source_target_pairs={{0,2},{1,3},{2,0},{3,1},{4,6},{5,7},{6,4},{7,5},{8,10},{9,11},{10,... | collective-permute-start | bytes 786440 | tf_op jit(solution)/shard_map/ppermute | solution.py:75
  16.4 17.1 %collective-permute-start.2 = (bf16[64,2048]{1,0:T(8,128)(2,1)S(1)}, bf16[64,2048]{1,0:T(8,128)(2,1)S(1)}, u32[]{:S(2)}, u32[]{:S(2)}) collective-permute-start(bf16[64,2048]{1,0:T(8,128)(2,1)S(1)} %get-tuple-element.106), channel_id=1, source_target_pairs={{0,3},{1,0},{2,1},{3,2},{4,7},{5,4},{6,5},{7,6},{8,11},{9,8},{10,9... | collective-permute-start | bytes 786440 | tf_op jit(solution)/shard_map/ppermute | solution.py:75
  34.6 115.7 %all-gather.6.cloned.1.call-start = ((), (), s32[]{:S(2)}) async-start(), calls=%async_computation.1 | async-start | bytes 9437184 | tf_op jit(solution)/shard_map/all_gather | solution.py:384
  34.7 25.1 %copy-start.21 = (bf16[256,2048]{1,0:T(8,128)(2,1)S(1)}, bf16[256,2048]{1,0:T(8,128)(2,1)}, u32[]{:S(2)}) copy-start(bf16[256,2048]{1,0:T(8,128)(2,1)} %param.12) | copy-start | bytes 3145732
  34.7 14.5 %collective-permute-start.9 = (bf16[64,2048]{1,0:T(8,128)(2,1)S(1)}, bf16[64,2048]{1,0:T(8,128)(2,1)S(1)}, u32[]{:S(2)}, u32[]{:S(2)}) collective-permute-start(bf16[64,2048]{1,0:T(8,128)(2,1)S(1)} %get-tuple-element.102), channel_id=1, source_target_pairs={{0,1},{1,2},{2,3},{3,0},{4,5},{5,6},{6,7},{7,4},{8,9},{9,10},{10,1... | collective-permute-start | bytes 786440 | tf_op jit(solution)/shard_map/ppermute | solution.py:75
  40.9 17.8 %collective-permute-start.10 = (bf16[64,2048]{1,0:T(8,128)(2,1)S(1)}, bf16[64,2048]{1,0:T(8,128)(2,1)S(1)}, u32[]{:S(2)}, u32[]{:S(2)}) collective-permute-start(bf16[64,2048]{1,0:T(8,128)(2,1)S(1)} %get-tuple-element.101), channel_id=1, source_target_pairs={{0,2},{1,3},{2,0},{3,1},{4,6},{5,7},{6,4},{7,5},{8,10},{9,11},{10,... | collective-permute-start | bytes 786440 | tf_op jit(solution)/shard_map/ppermute | solution.py:75
  42.5 16.2 %collective-permute-start.11 = (bf16[64,2048]{1,0:T(8,128)(2,1)S(1)}, bf16[64,2048]{1,0:T(8,128)(2,1)S(1)}, u32[]{:S(2)}, u32[]{:S(2)}) collective-permute-start(bf16[64,2048]{1,0:T(8,128)(2,1)S(1)} %get-tuple-element.100), channel_id=1, source_target_pairs={{0,3},{1,0},{2,1},{3,2},{4,7},{5,4},{6,5},{7,6},{8,11},{9,8},{10,9... | collective-permute-start | bytes 786440 | tf_op jit(solution)/shard_map/ppermute | solution.py:75
  59.8 198.8 %all-gather.8.cloned.1.call-start = ((), (), s32[]{:S(2)}) async-start(), calls=%async_computation.2 | async-start | bytes 9437184 | tf_op jit(solution)/shard_map/all_gather | solution.py:401
  60.0 20.7 %collective-permute-start.3 = (bf16[128,2048]{1,0:T(8,128)(2,1)S(1)}, bf16[128,2048]{1,0:T(8,128)(2,1)S(1)}, u32[]{:S(2)}, u32[]{:S(2)}) collective-permute-start(bf16[128,2048]{1,0:T(8,128)(2,1)S(1)} %get-tuple-element.53.refs_1_.token_ref), channel_id=1, source_target_pairs={{0,1},{1,2},{2,3},{3,0},{4,5},{5,6},{6,7},{7,4},{8,9},{9,10},{10,1... | collective-permute-start | bytes 1572872 | tf_op jit(solution)/shard_map/ppermute | solution.py:362
  66.1 25.8 %collective-permute-start.4 = (bf16[128,2048]{1,0:T(8,128)(2,1)S(1)}, bf16[128,2048]{1,0:T(8,128)(2,1)S(1)}, u32[]{:S(2)}, u32[]{:S(2)}) collective-permute-start(bf16[128,2048]{1,0:T(8,128)(2,1)S(1)} %get-tuple-element.57.refs_2_.token_ref), channel_id=1, source_target_pairs={{0,1},{1,2},{2,3},{3,0},{4,5},{5,6},{6,7},{7,4},{8,9},{9,10},{10,1... | collective-permute-start | bytes 1572872 | tf_op jit(solution)/shard_map/ppermute | solution.py:362
  69.7 24.4 %copy-start.16 = (f32[2048]{0:T(1024)S(1)}, f32[2048]{0:T(1024)}, u32[]{:S(2)}) copy-start(f32[2048]{0:T(1024)} %param.13) | copy-start | bytes 24580
  80.7 23.0 %collective-permute-start.5 = (bf16[128,2048]{1,0:T(8,128)(2,1)S(1)}, bf16[128,2048]{1,0:T(8,128)(2,1)}, u32[]{:S(2)}, u32[]{:S(2)}) collective-permute-start(bf16[128,2048]{1,0:T(8,128)(2,1)S(1)} %collective-permute-done.3.refs_1_), channel_id=1, source_target_pairs={{0,1},{1,2},{2,3},{3,0},{4,5},{5,6},{6,7},{7,4},{8,9},{9,10},{10,1... | collective-permute-start | bytes 1572872 | tf_op jit(solution)/shard_map/ppermute | solution.py:362
  91.9 9.7 %copy-start.14 = (bf16[128,2048]{1,0:T(8,128)(2,1)}, bf16[128,2048]{1,0:T(8,128)(2,1)S(1)}, u32[]{:S(2)}) copy-start(bf16[128,2048]{1,0:T(8,128)(2,1)S(1)} %collective-permute-done.4.refs_2_) | copy-start | bytes 1572868
  91.9 22.6 %collective-permute-start.6 = (bf16[128,2048]{1,0:T(8,128)(2,1)S(1)}, bf16[128,2048]{1,0:T(8,128)(2,1)}, u32[]{:S(2)}, u32[]{:S(2)}) collective-permute-start(bf16[128,2048]{1,0:T(8,128)(2,1)S(1)} %collective-permute-done.4.refs_2_), channel_id=1, source_target_pairs={{0,1},{1,2},{2,3},{3,0},{4,5},{5,6},{6,7},{7,4},{8,9},{9,10},{10,1... | collective-permute-start | bytes 1572872 | tf_op jit(solution)/shard_map/ppermute | solution.py:362
  94.1 3.4 %copy-start.2 = (bf16[2048,2048]{1,0:T(8,128)(2,1)S(1)}, bf16[2048,2048]{1,0:T(8,128)(2,1)}, u32[]{:S(2)}) copy-start(bf16[2048,2048]{1,0:T(8,128)(2,1)} %all-gather.4.cloned.1.call-done.refs_6_) | copy-start | bytes 25165828
  101.7 1.0 copy-start.6
  102.6 1.0 copy-start.10
  103.7 29.7 %collective-permute-start.7 = (bf16[128,2048]{1,0:T(8,128)(2,1)}, bf16[128,2048]{1,0:T(8,128)(2,1)}, u32[]{:S(2)}, u32[]{:S(2)}) collective-permute-start(bf16[128,2048]{1,0:T(8,128)(2,1)} %collective-permute-done.5.refs_1_), channel_id=1, source_target_pairs={{0,1},{1,2},{2,3},{3,0},{4,5},{5,6},{6,7},{7,4},{8,9},{9,10},{10,1... | collective-permute-start | bytes 1572872 | tf_op jit(solution)/shard_map/ppermute | solution.py:362
  114.5 21.2 %collective-permute-start.8 = (bf16[128,2048]{1,0:T(8,128)(2,1)}, bf16[128,2048]{1,0:T(8,128)(2,1)}, u32[]{:S(2)}, u32[]{:S(2)}) collective-permute-start(bf16[128,2048]{1,0:T(8,128)(2,1)} %collective-permute-done.6.refs_2_), channel_id=1, source_target_pairs={{0,1},{1,2},{2,3},{3,0},{4,5},{5,6},{6,7},{7,4},{8,9},{9,10},{10,1... | collective-permute-start | bytes 1572872 | tf_op jit(solution)/shard_map/ppermute | solution.py:362
  116.2 3.4 %copy-start.3 = (bf16[2048,2048]{1,0:T(8,128)(2,1)S(1)}, bf16[2048,2048]{1,0:T(8,128)(2,1)}, u32[]{:S(2)}) copy-start(bf16[2048,2048]{1,0:T(8,128)(2,1)} %all-gather.4.cloned.1.call-done.refs_6_) | copy-start | bytes 25165828
  119.5 1.0 copy-start.15
  120.6 19.9 %slice-start = ((s8[8388608]{0:T(1024)(128)(4,1)}), s8[4194304]{0:T(1024)(128)(4,1)S(1)}, s32[]{:S(2)}) async-start(s8[8388608]{0:T(1024)(128)(4,1)} %bitcast.84), calls=%async_computation.3 | async-start | bytes 8388608
  124.8 1.0 copy-start.7
  125.8 1.0 copy-start.13
  126.8 9.0 %copy-start.18 = (bf16[4,64,2048]{2,1,0:T(8,128)(2,1)S(1)}, bf16[4,64,2048]{2,1,0:T(8,128)(2,1)}, u32[]{:S(2)}) copy-start(bf16[4,64,2048]{2,1,0:T(8,128)(2,1)} %pad_maximum_fusion.2) | copy-start | bytes 3145732
  126.8 13.7 %slice-start.1 = ((s8[8388608]{0:T(1024)(128)(4,1)}), s8[4194304]{0:T(1024)(128)(4,1)S(1)}, s32[]{:S(2)}) async-start(s8[8388608]{0:T(1024)(128)(4,1)} %bitcast.84), calls=%async_computation.4 | async-start | bytes 8388608
  132.4 1.0 copy-start.8
  133.3 7.2 %copy-start.11 = (bf16[256,2048]{1,0:T(8,128)(2,1)}, bf16[256,2048]{1,0:T(8,128)(2,1)S(1)}, u32[]{:S(2)}) copy-start(bf16[256,2048]{1,0:T(8,128)(2,1)S(1)} %get-tuple-element.73.refs_3_) | copy-start | bytes 3145732
  136.6 23.0 %collective-permute-start.21 = (bf16[64,2048]{1,0:T(8,128)(2,1)}, bf16[64,2048]{1,0:T(8,128)(2,1)S(1)}, u32[]{:S(2)}, u32[]{:S(2)}) collective-permute-start(bf16[64,2048]{1,0:T(8,128)(2,1)} %get-tuple-element.98), channel_id=1, source_target_pairs={{0,1},{1,2},{2,3},{3,0},{4,5},{5,6},{6,7},{7,4},{8,9},{9,10},{10,1... | collective-permute-start | bytes 786440 | tf_op jit(solution)/shard_map/ppermute | solution.py:75
  137.1 22.6 %collective-permute-start.22 = (bf16[64,2048]{1,0:T(8,128)(2,1)}, bf16[64,2048]{1,0:T(8,128)(2,1)S(1)}, u32[]{:S(2)}, u32[]{:S(2)}) collective-permute-start(bf16[64,2048]{1,0:T(8,128)(2,1)} %get-tuple-element.97), channel_id=1, source_target_pairs={{0,2},{1,3},{2,0},{3,1},{4,6},{5,7},{6,4},{7,5},{8,10},{9,11},{10,... | collective-permute-start | bytes 786440 | tf_op jit(solution)/shard_map/ppermute | solution.py:75
  139.0 20.7 %collective-permute-start.23 = (bf16[64,2048]{1,0:T(8,128)(2,1)}, bf16[64,2048]{1,0:T(8,128)(2,1)}, u32[]{:S(2)}, u32[]{:S(2)}) collective-permute-start(bf16[64,2048]{1,0:T(8,128)(2,1)} %get-tuple-element.96), channel_id=1, source_target_pairs={{0,3},{1,0},{2,1},{3,2},{4,7},{5,4},{6,5},{7,6},{8,11},{9,8},{10,9... | collective-permute-start | bytes 786440 | tf_op jit(solution)/shard_map/ppermute | solution.py:75
  145.9 1.0 copy-start.9
  146.9 1.0 copy-start.12
  161.7 16.6 %collective-permute-start.12 = (bf16[128,2048]{1,0:T(8,128)(2,1)S(1)}, bf16[128,2048]{1,0:T(8,128)(2,1)S(1)}, u32[]{:S(2)}, u32[]{:S(2)}) collective-permute-start(bf16[128,2048]{1,0:T(8,128)(2,1)S(1)} %get-tuple-element.71), channel_id=1, source_target_pairs={{0,1},{1,2},{2,3},{3,0},{4,5},{5,6},{6,7},{7,4},{8,9},{9,10},{10,1... | collective-permute-start | bytes 1572872 | tf_op jit(solution)/shard_map/ppermute | solution.py:362
  165.0 24.6 %collective-permute-start.15 = (bf16[128,2048]{1,0:T(8,128)(2,1)S(1)}, bf16[128,2048]{1,0:T(8,128)(2,1)S(1)}, u32[]{:S(2)}, u32[]{:S(2)}) collective-permute-start(bf16[128,2048]{1,0:T(8,128)(2,1)S(1)} %get-tuple-element.72), channel_id=1, source_target_pairs={{0,1},{1,2},{2,3},{3,0},{4,5},{5,6},{6,7},{7,4},{8,9},{9,10},{10,1... | collective-permute-start | bytes 1572872 | tf_op jit(solution)/shard_map/ppermute | solution.py:362
  178.5 22.3 %collective-permute-start.13 = (bf16[128,2048]{1,0:T(8,128)(2,1)S(1)}, bf16[128,2048]{1,0:T(8,128)(2,1)S(1)}, u32[]{:S(2)}, u32[]{:S(2)}) collective-permute-start(bf16[128,2048]{1,0:T(8,128)(2,1)S(1)} %add_convert_fusion.3), channel_id=1, source_target_pairs={{0,1},{1,2},{2,3},{3,0},{4,5},{5,6},{6,7},{7,4},{8,9},{9,10},{10,1... | collective-permute-start | bytes 1572872 | tf_op jit(solution)/shard_map/ppermute | solution.py:362
  189.7 22.3 %collective-permute-start.16 = (bf16[128,2048]{1,0:T(8,128)(2,1)S(1)}, bf16[128,2048]{1,0:T(8,128)(2,1)S(1)}, u32[]{:S(2)}, u32[]{:S(2)}) collective-permute-start(bf16[128,2048]{1,0:T(8,128)(2,1)S(1)} %add_convert_fusion.1), channel_id=1, source_target_pairs={{0,1},{1,2},{2,3},{3,0},{4,5},{5,6},{6,7},{7,4},{8,9},{9,10},{10,1... | collective-permute-start | bytes 1572872 | tf_op jit(solution)/shard_map/ppermute | solution.py:362
  201.0 22.3 %collective-permute-start.14 = (bf16[128,2048]{1,0:T(8,128)(2,1)S(1)}, bf16[128,2048]{1,0:T(8,128)(2,1)S(1)}, u32[]{:S(2)}, u32[]{:S(2)}) collective-permute-start(bf16[128,2048]{1,0:T(8,128)(2,1)S(1)} %add_convert_fusion.2), channel_id=1, source_target_pairs={{0,1},{1,2},{2,3},{3,0},{4,5},{5,6},{6,7},{7,4},{8,9},{9,10},{10,1... | collective-permute-start | bytes 1572872 | tf_op jit(solution)/shard_map/ppermute | solution.py:362
  212.2 11.1 %copy-start.17 = (f32[2048]{0:T(1024)S(1)}, f32[2048]{0:T(1024)}, u32[]{:S(2)}) copy-start(f32[2048]{0:T(1024)} %param.14) | copy-start | bytes 24580
  212.2 22.3 %collective-permute-start.17 = (bf16[128,2048]{1,0:T(8,128)(2,1)S(1)}, bf16[128,2048]{1,0:T(8,128)(2,1)S(1)}, u32[]{:S(2)}, u32[]{:S(2)}) collective-permute-start(bf16[128,2048]{1,0:T(8,128)(2,1)S(1)} %add_convert_fusion), channel_id=1, source_target_pairs={{0,1},{1,2},{2,3},{3,0},{4,5},{5,6},{6,7},{7,4},{8,9},{9,10},{10,1... | collective-permute-start | bytes 1572872 | tf_op jit(solution)/shard_map/ppermute | solution.py:362
  223.8 22.1 %collective-permute-start.18 = (bf16[128,2048]{1,0:T(8,128)(2,1)S(1)}, bf16[128,2048]{1,0:T(8,128)(2,1)}, u32[]{:S(2)}, u32[]{:S(2)}) collective-permute-start(bf16[128,2048]{1,0:T(8,128)(2,1)S(1)} %get-tuple-element.85.refs_1_), channel_id=1, source_target_pairs={{0,1},{1,2},{2,3},{3,0},{4,5},{5,6},{6,7},{7,4},{8,9},{9,10},{10,1... | collective-permute-start | bytes 1572872 | tf_op jit(solution)/shard_map/ppermute | solution.py:362
  235.0 22.1 %collective-permute-start.20 = (bf16[128,2048]{1,0:T(8,128)(2,1)S(1)}, bf16[128,2048]{1,0:T(8,128)(2,1)}, u32[]{:S(2)}, u32[]{:S(2)}) collective-permute-start(bf16[128,2048]{1,0:T(8,128)(2,1)S(1)} %get-tuple-element.86.refs_2_), channel_id=1, source_target_pairs={{0,1},{1,2},{2,3},{3,0},{4,5},{5,6},{6,7},{7,4},{8,9},{9,10},{10,1... | collective-permute-start | bytes 1572872 | tf_op jit(solution)/shard_map/ppermute | solution.py:362
  245.9 25.2 %collective-permute-start.19 = (bf16[128,2048]{1,0:T(8,128)(2,1)}, bf16[128,2048]{1,0:T(8,128)(2,1)S(1)}, u32[]{:S(2)}, u32[]{:S(2)}) collective-permute-start(bf16[128,2048]{1,0:T(8,128)(2,1)} %collective-permute-done.18.refs_1_), channel_id=1, source_target_pairs={{0,1},{1,2},{2,3},{3,0},{4,5},{5,6},{6,7},{7,4},{8,9},{9,10},{10,1... | collective-permute-start | bytes 1572872 | tf_op jit(solution)/shard_map/ppermute | solution.py:362
  257.1 22.4 %collective-permute-start.25 = (bf16[128,2048]{1,0:T(8,128)(2,1)}, bf16[128,2048]{1,0:T(8,128)(2,1)S(1)}, u32[]{:S(2)}, u32[]{:S(2)}) collective-permute-start(bf16[128,2048]{1,0:T(8,128)(2,1)} %collective-permute-done.20.refs_2_), channel_id=1, source_target_pairs={{0,1},{1,2},{2,3},{3,0},{4,5},{5,6},{6,7},{7,4},{8,9},{9,10},{10,1... | collective-permute-start | bytes 1572872 | tf_op jit(solution)/shard_map/ppermute | solution.py:362
  258.6 3.4 %copy-start.4 = (bf16[2048,2048]{1,0:T(8,128)(2,1)S(1)}, bf16[2048,2048]{1,0:T(8,128)(2,1)}, u32[]{:S(2)}) copy-start(bf16[2048,2048]{1,0:T(8,128)(2,1)} %all-gather.8.cloned.1.call-done.refs_3_) | copy-start | bytes 25165828
  262.0 3.9 %copy-start.5 = (bf16[2048,2048]{1,0:T(8,128)(2,1)S(1)}, bf16[2048,2048]{1,0:T(8,128)(2,1)}, u32[]{:S(2)}) copy-start(bf16[2048,2048]{1,0:T(8,128)(2,1)} %all-gather.8.cloned.1.call-done.refs_3_) | copy-start | bytes 25165828
  271.0 19.7 %collective-permute-start.24 = (bf16[128,2048]{1,0:T(8,128)(2,1)S(1)}, bf16[128,2048]{1,0:T(8,128)(2,1)S(1)}, u32[]{:S(2)}, u32[]{:S(2)}) collective-permute-start(bf16[128,2048]{1,0:T(8,128)(2,1)S(1)} %collective-permute-done.19.refs_1_), channel_id=1, source_target_pairs={{0,1},{1,2},{2,3},{3,0},{4,5},{5,6},{6,7},{7,4},{8,9},{9,10},{10,1... | collective-permute-start | bytes 1572872 | tf_op jit(solution)/shard_map/ppermute | solution.py:362
  279.5 21.8 %collective-permute-start.26 = (bf16[128,2048]{1,0:T(8,128)(2,1)S(1)}, bf16[128,2048]{1,0:T(8,128)(2,1)S(1)}, u32[]{:S(2)}, u32[]{:S(2)}) collective-permute-start(bf16[128,2048]{1,0:T(8,128)(2,1)S(1)} %collective-permute-done.25.refs_2_), channel_id=1, source_target_pairs={{0,1},{1,2},{2,3},{3,0},{4,5},{5,6},{6,7},{7,4},{8,9},{9,10},{10,1... | collective-permute-start | bytes 1572872 | tf_op jit(solution)/shard_map/ppermute | solution.py:362
  301.3 3.9 %copy-start.1 = (f32[1024,8]{0,1:T(8,128)S(1)}, f32[1024,8]{0,1:T(8,128)}, u32[]{:S(2)}) copy-start(f32[1024,8]{0,1:T(8,128)} %param.16) | copy-start | bytes 98308
Sparse Core Ops, SparseCore 0:
  34.7 59.1 all-gather.3
  95.8 54.4 all-gather.5
  161.9 55.2 all-gather.7
where the time goes:
time: 312 us
  waiting for transfers between devices  142 us (46%)
  Pallas kernels  78.5 us (25%)
  starting transfers between devices  44.8 us (14%)
  local copies, waits for them, and re-layouts  21 us (7%)
  between operations  15.1 us (5%)
  other arithmetic  10 us (3%)
    ppermute x18, waiting for transfers between devices, onward(): return [lax.ppermute(half, 'mp', order) for half in halves]  108 us
    pallas_call x4, Pallas kernels, retention(): pl.pallas_call(lambda *refs: retention_kernel(dims, *refs), grid_spec=gri...  37.1 us
    ppermute x9, waiting for transfers between devices, exchanged(): lax.ppermute(piece, 'mp', [(i, (i + shift) % count) for i in range(count)])  30.8 us
    ppermute x18, starting transfers between devices, onward(): return [lax.ppermute(half, 'mp', order) for half in halves]  25.3 us
    ppermute x9, starting transfers between devices, exchanged(): lax.ppermute(piece, 'mp', [(i, (i + shift) % count) for i in range(count)])  19.4 us
    pallas_call x4, Pallas kernels, project(): pl.pallas_call(lambda *refs: project_kernel(heads, *refs), grid_spec=grid...  19.4 us
    unnamed x54, local copies, waits for them, and re-layouts  18.3 us
    pallas_call x4, Pallas kernels, ffn(): pl.pallas_call(lambda *refs: ffn_kernel(len(halves), *refs), grid_spec=gr...  16.9 us
  transfers between devices with their start and end apart: 30, of which 20 were waited for; matrix products, arithmetic and copies ran while one was open for 3% of the time, Pallas kernels for 23%

commit v1 on v0

--- a/solution.py
+++ b/solution.py
@@ -81,8 +81,8 @@
     return jnp.concatenate([ref[...] for ref in refs], axis=0)
 
 
-def chunk(i):
-    return pl.ds(pl.multiple_of(i * CHUNK, CHUNK), CHUNK)
+def chunk(i, size=CHUNK):
+    return pl.ds(pl.multiple_of(i * size, size), size)
 
 
 def project_kernel(heads, scalars, *refs):
@@ -100,11 +100,12 @@
         return _
 
     def plain(i, _):
-        out_ref[:, chunk(i)] = jnp.dot(normed_ref[...], w_ref[:, chunk(i)], preferred_element_type=F32).astype(BF)
+        band = chunk(i, DV)
+        out_ref[:, band] = jnp.dot(normed_ref[...], w_ref[:, band], preferred_element_type=F32).astype(BF)
         return _
 
     lax.fori_loop(0, 2 * heads, turn, 0)
-    lax.fori_loop(2 * wq // CHUNK, out_ref.shape[1] // CHUNK, plain, 0)
+    lax.fori_loop(2 * wq // DV, out_ref.shape[1] // DV, plain, 0)
 
 
 def project(halves, place, gain, cos, sin, w, heads):
@@ -129,7 +130,7 @@
     return pl.pallas_call(
         lambda *refs: project_kernel(heads, *refs),
         grid_spec=grid_spec,
-        out_shape=[jax.ShapeDtypeStruct((rows, width), BF), jax.ShapeDtypeStruct((rows, out_width), BF)],
+        out_shape=[pltpu.HBM((rows, width), BF), pltpu.HBM((rows, out_width), BF)],
         compiler_params=pltpu.CompilerParams(vmem_limit_bytes=20 * 2**20),
         cost_estimate=pl.CostEstimate(flops=rows * width * out_width // 2, bytes_accessed=2**20, transcendentals=0),
         name="project",
@@ -200,25 +201,29 @@
     copies[count].wait()
     copies[count + 1].wait()
 
+    wide = min(wg, 2 * CHUNK)
+
     def gating(i, _):
-        gate = jnp.dot(x_ref[...], wg_ref[:, chunk(i)], preferred_element_type=F32).astype(BF).astype(F32)
+        band = chunk(i, wide)
+        gate = jnp.dot(x_ref[...], wg_ref[:, band], preferred_element_type=F32).astype(BF).astype(F32)
         gate = gate / (1.0 + jnp.exp(-gate))
-        gated_ref[:, chunk(i)] = jnp.where(live, gate * kept_ref[:, chunk(i)], 0.0).astype(BF)
-        return _
-
-    lax.fori_loop(0, wg // CHUNK, gating, 0)
+        gated_ref[:, band] = jnp.where(live, gate * kept_ref[:, band], 0.0).astype(BF)
+        return _
+
+    lax.fori_loop(0, wg // wide, gating, 0)
     copies[count + 2].wait()
     half = rows // len(out_refs)
 
     def leaving(i, _):
+        band = chunk(i, 2 * CHUNK)
         branch = lax.dot_general(
-            gated_ref[...], wo_ref[chunk(i), :], (((1,), (1,)), ((), ())), preferred_element_type=F32
+            gated_ref[...], wo_ref[band, :], (((1,), (1,)), ((), ())), preferred_element_type=F32
         ).astype(BF)
         for k, out_ref in enumerate(out_refs):
-            out_ref[:, chunk(i)] = branch[k * half : (k + 1) * half]
-        return _
-
-    lax.fori_loop(0, width // CHUNK, leaving, 0)
+            out_ref[:, band] = branch[k * half : (k + 1) * half]
+        return _
+
+    lax.fori_loop(0, width // (2 * CHUNK), leaving, 0)
 
 
 def retention(own, index, x, running, length, partner, blocks, w, heads, share):
@@ -281,12 +286,13 @@
 def ffn_kernel(count, scalars, *refs):
     w_ref, out_ref, x_ref = refs[count], refs[-2], refs[-1]
     x_ref[...] = stacked(refs[:count])
-    chunks = out_ref.shape[1] // CHUNK
+    wide = min(out_ref.shape[1], 2 * CHUNK)
+    chunks = out_ref.shape[1] // wide
 
     def one(i, _):
-        gate = jnp.dot(x_ref[...], w_ref[:, chunk(i)], preferred_element_type=F32)
-        up = jnp.dot(x_ref[...], w_ref[:, chunk(i + chunks)], preferred_element_type=F32)
-        out_ref[:, chunk(i)] = (gate / (1.0 + jnp.exp(-gate)) * up).astype(BF)
+        gate = jnp.dot(x_ref[...], w_ref[:, chunk(i, wide)], preferred_element_type=F32)
+        up = jnp.dot(x_ref[...], w_ref[:, chunk(i + chunks, wide)], preferred_element_type=F32)
+        out_ref[:, chunk(i, wide)] = (gate / (1.0 + jnp.exp(-gate)) * up).astype(BF)
         return _
 
     lax.fori_loop(0, chunks, one, 0)

time: 312 us -> 311 us (level)
  starting transfers between devices: 44.8 us -> 53.7 us
  local copies, waits for them, and re-layouts: 21 us -> 14.2 us
  Pallas kernels: 78.5 us -> 73.8 us
    ppermute x18, starting transfers between devices: 25.3 us -> 34.2 us  [onward(): return [lax.ppermute(half, 'mp', order) for half in halves]]
    unnamed x54 -> x38, local copies, waits for them, and re-layouts: 18.3 us -> 11.4 us
    pallas_call x4, Pallas kernels: 37.1 us -> 32.3 us  [retention(): pl.pallas_call(lambda *refs: retention_kernel(dims, *refs), grid_spec=gri...]
  transfers between devices with their start and end apart: 30 -> 30, of which waited for: 20 -> 21; matrix products, arithmetic and copies ran while one was open for 3% -> 3% of each run, Pallas kernels for 23% -> 22%
where the time goes in v1:
time: 311 us; the launch traced here: 310 us
  waiting for transfers between devices  143 us (46%)
  Pallas kernels  73.8 us (24%)
  starting transfers between devices  53.7 us (17%)
  between operations  15 us (5%)
  local copies, waits for them, and re-layouts  14.2 us (5%)
  other arithmetic  10 us (3%)
    ppermute x18, waiting for transfers between devices, onward(): return [lax.ppermute(half, 'mp', order) for half in halves]  108 us
    ppermute x18, starting transfers between devices, onward(): return [lax.ppermute(half, 'mp', order) for half in halves]  34.2 us
    pallas_call x4, Pallas kernels, retention(): pl.pallas_call(lambda *refs: retention_kernel(dims, *refs), grid_spec=gri...  32.3 us
    ppermute x9, waiting for transfers between devices, exchanged(): lax.ppermute(piece, 'mp', [(i, (i + shift) % count) for i in range(count)])  30.8 us
    pallas_call x4, Pallas kernels, project(): pl.pallas_call(lambda *refs: project_kernel(heads, *refs), grid_spec=grid...  21.6 us
    ppermute x9, starting transfers between devices, exchanged(): lax.ppermute(piece, 'mp', [(i, (i + shift) % count) for i in range(count)])  19.4 us
    pallas_call x4, Pallas kernels, ffn(): pl.pallas_call(lambda *refs: ffn_kernel(len(halves), *refs), grid_spec=gr...  14.8 us
    unnamed x38, local copies, waits for them, and re-layouts  11.4 us
  transfers between devices with their start and end apart: 30, of which 21 were waited for; matrix products, arithmetic and copies ran while one was open for 3% of the time, Pallas kernels for 22%

profile of v1, /device:TPU:0, one launch (start us, length us, event | category | flops | bytes accessed | tf_op | source)
XLA Modules:
  0.0 310.0 jit_solution(6865826519650790923)
XLA Ops:
  7.3 1.3 convert_element_type.121
  10.7 3.1 collective-permute-start
  13.8 2.6 collective-permute-start.1
  16.4 1.3 collective-permute-start.2
  18.1 5.0 %collective-permute-done.refs_1_ = bf16[64,2048]{1,0:T(8,128)(2,1)S(1)} collective-permute-done((bf16[64,2048]{1,0:T(8,128)(2,1)S(1)}, bf16[64,2048]{1,0:T(8,128)(2,1)S(1)}, u32[]{:S(2)}, u32[]{:S(2)}) %collective-permute-start) | collective-permute-done | bytes 262176 | tf_op jit(solution)/shard_map/ppermute | solution.py:75
  23.1 10.4 %collective-permute-done.1.refs_2_ = bf16[64,2048]{1,0:T(8,128)(2,1)S(1)} collective-permute-done((bf16[64,2048]{1,0:T(8,128)(2,1)S(1)}, bf16[64,2048]{1,0:T(8,128)(2,1)S(1)}, u32[]{:S(2)}, u32[]{:S(2)}) %collective-permute-start.1) | collective-permute-done | bytes 262176 | tf_op jit(solution)/shard_map/ppermute | solution.py:75
  33.5 1.0 assemble.3
  34.7 6.1 %collective-permute-start.9 = (bf16[64,2048]{1,0:T(8,128)(2,1)S(1)}, bf16[64,2048]{1,0:T(8,128)(2,1)S(1)}, u32[]{:S(2)}, u32[]{:S(2)}) collective-permute-start(bf16[64,2048]{1,0:T(8,128)(2,1)S(1)} %get-tuple-element.102), channel_id=1, source_target_pairs={{0,1},{1,2},{2,3},{3,0},{4,5},{5,6},{6,7},{7,4},{8,9},{9,10},{10,1... | collective-permute-start | bytes 786440 | tf_op jit(solution)/shard_map/ppermute | solution.py:75
  40.9 1.6 collective-permute-start.10
  42.5 0.9 collective-permute-start.11
  43.3 5.9 %collective-permute-done.9.refs_1_ = bf16[64,2048]{1,0:T(8,128)(2,1)S(1)} collective-permute-done((bf16[64,2048]{1,0:T(8,128)(2,1)S(1)}, bf16[64,2048]{1,0:T(8,128)(2,1)S(1)}, u32[]{:S(2)}, u32[]{:S(2)}) %collective-permute-start.9) | collective-permute-done | bytes 262176 | tf_op jit(solution)/shard_map/ppermute | solution.py:75
  49.3 9.4 %collective-permute-done.10.refs_2_ = bf16[64,2048]{1,0:T(8,128)(2,1)S(1)} collective-permute-done((bf16[64,2048]{1,0:T(8,128)(2,1)S(1)}, bf16[64,2048]{1,0:T(8,128)(2,1)S(1)}, u32[]{:S(2)}, u32[]{:S(2)}) %collective-permute-start.10) | collective-permute-done | bytes 262176 | tf_op jit(solution)/shard_map/ppermute | solution.py:75
  58.7 1.1 assemble.4
  59.9 6.1 %collective-permute-start.3 = (bf16[128,2048]{1,0:T(8,128)(2,1)S(1)}, bf16[128,2048]{1,0:T(8,128)(2,1)S(1)}, u32[]{:S(2)}, u32[]{:S(2)}) collective-permute-start(bf16[128,2048]{1,0:T(8,128)(2,1)S(1)} %get-tuple-element.53.refs_1_.token_ref), channel_id=1, source_target_pairs={{0,1},{1,2},{2,3},{3,0},{4,5},{5,6},{6,7},{7,4},{8,9},{9,10},{10,1... | collective-permute-start | bytes 1572872 | tf_op jit(solution)/shard_map/ppermute | solution.py:368
  66.8 1.6 convert_element_type.123
  68.4 1.3 convert_element_type.122
  69.7 1.1 pad_maximum_fusion.2
  70.8 9.9 %collective-permute-done.3.refs_1_ = bf16[128,2048]{1,0:T(8,128)(2,1)S(1)} collective-permute-done((bf16[128,2048]{1,0:T(8,128)(2,1)S(1)}, bf16[128,2048]{1,0:T(8,128)(2,1)S(1)}, u32[]{:S(2)}, u32[]{:S(2)}) %collective-permute-start.3) | collective-permute-done | bytes 524320 | tf_op jit(solution)/shard_map/ppermute | solution.py:368
  80.9 11.0 %collective-permute-done.4.refs_2_ = bf16[128,2048]{1,0:T(8,128)(2,1)S(1)} collective-permute-done((bf16[128,2048]{1,0:T(8,128)(2,1)S(1)}, bf16[128,2048]{1,0:T(8,128)(2,1)S(1)}, u32[]{:S(2)}, u32[]{:S(2)}) %collective-permute-start.4) | collective-permute-done | bytes 524320 | tf_op jit(solution)/shard_map/ppermute | solution.py:368
  92.1 1.9 multiply_sine_fusion
  94.1 3.4 %copy-done.2 = bf16[2048,2048]{1,0:T(8,128)(2,1)S(1)} copy-done((bf16[2048,2048]{1,0:T(8,128)(2,1)S(1)}, bf16[2048,2048]{1,0:T(8,128)(2,1)}, u32[]{:S(2)}) %copy-start.2) | copy-done | bytes 8388632
  97.4 4.7 %project.5 = (bf16[256,2048]{1,0:T(8,128)(2,1)}, bf16[256,2048]{1,0:T(8,128)(2,1)}) custom-call(s32[1]{0:T(128)} %bitcast.21.refs_0_, bf16[128,2048]{1,0:T(8,128)(2,1)S(1)} %get-tuple-element.53.refs_1_.token_ref, bf16[128,2048]{1,0:T(8,128)(2,1)S(1)} %get-tuple-element.57.refs_2_.token_ref, f32[1,2048]{1,0:T(1,128)S(1)} %bitcast.94, ...), custom_call_target="tpu_custom_call" | custom-call | flops 536870912 | bytes 1048576 | tf_op jit(solution)/shard_map/project/pallas_call | solution.py:130
  102.2 1.1 collective-permute-done.5.refs_1_
  103.5 10.9 %collective-permute-done.6.refs_2_ = bf16[128,2048]{1,0:T(8,128)(2,1)} collective-permute-done((bf16[128,2048]{1,0:T(8,128)(2,1)S(1)}, bf16[128,2048]{1,0:T(8,128)(2,1)}, u32[]{:S(2)}, u32[]{:S(2)}) %collective-permute-start.6) | collective-permute-done | bytes 524320 | tf_op jit(solution)/shard_map/ppermute | solution.py:368
  116.2 3.4 %copy-done.3 = bf16[2048,2048]{1,0:T(8,128)(2,1)S(1)} copy-done((bf16[2048,2048]{1,0:T(8,128)(2,1)S(1)}, bf16[2048,2048]{1,0:T(8,128)(2,1)}, u32[]{:S(2)}) %copy-start.3) | copy-done | bytes 8388632
  119.5 1.0 copy-done.7
  120.6 4.7 %project.4 = (bf16[256,2048]{1,0:T(8,128)(2,1)}, bf16[256,2048]{1,0:T(8,128)(2,1)}) custom-call(s32[1]{0:T(128)} %bitcast.5.refs_0_, bf16[128,2048]{1,0:T(8,128)(2,1)S(1)} %collective-permute-done.3.refs_1_, bf16[128,2048]{1,0:T(8,128)(2,1)S(1)} %copy-done.7, f32[1,2048]{1,0:T(1,128)S(1)} %bitcast.95, f32[1024,128]{1,0:T(8,128)S(1)} %get-tuple-element.111.refs_4_, ...), custom_call_target="tpu_custom_call" | custom-call | flops 536870912 | bytes 1048576 | tf_op jit(solution)/shard_map/project/pallas_call | solution.py:130
  125.3 6.1 %project.6 = (bf16[256,2048]{1,0:T(8,128)(2,1)}, bf16[256,2048]{1,0:T(8,128)(2,1)}) custom-call(s32[1]{0:T(128)} %bitcast.22.refs_0_, bf16[128,2048]{1,0:T(8,128)(2,1)} %collective-permute-done.5.refs_1_, bf16[128,2048]{1,0:T(8,128)(2,1)} %collective-permute-done.6.refs_2_, f32[1,2048]{1,0:T(1,128)S(1)} %bitcast.96, ...), custom_call_target="tpu_custom_call" | custom-call | flops 536870912 | bytes 1048576 | tf_op jit(solution)/shard_map/project/pallas_call | solution.py:130
  131.4 4.3 %collective-permute-done.8.refs_2_ = bf16[128,2048]{1,0:T(8,128)(2,1)} collective-permute-done((bf16[128,2048]{1,0:T(8,128)(2,1)}, bf16[128,2048]{1,0:T(8,128)(2,1)}, u32[]{:S(2)}, u32[]{:S(2)}) %collective-permute-start.8) | collective-permute-done | bytes 524320 | tf_op jit(solution)/shard_map/ppermute | solution.py:368
  135.7 0.9 dynamic-slice_bitcast_fusion
  137.1 1.8 collective-permute-start.22
  139.0 1.5 collective-permute-start.23
  140.5 6.0 %project.7 = (bf16[256,2048]{1,0:T(8,128)(2,1)}, bf16[256,2048]{1,0:T(8,128)(2,1)}) custom-call(s32[1]{0:T(128)} %bitcast.23.refs_0_, bf16[128,2048]{1,0:T(8,128)(2,1)} %collective-permute-done.7.refs_1_, bf16[128,2048]{1,0:T(8,128)(2,1)} %collective-permute-done.8.refs_2_, f32[1,2048]{1,0:T(1,128)S(1)} %bitcast.97, ...), custom_call_target="tpu_custom_call" | custom-call | flops 536870912 | bytes 1048576 | tf_op jit(solution)/shard_map/project/pallas_call | solution.py:130
  146.5 3.8 %all-gather.6.cloned.1.call-done.refs_8_ = bf16[2048,2048]{1,0:T(8,128)(2,1)} async-done(((bf16[256,2048]{1,0:T(8,128)(2,1)}), bf16[2048,2048]{1,0:T(8,128)(2,1)}) %all-gather.6.cloned.1.call-update) | async-done | bytes 8388624 | tf_op jit(solution)/shard_map/all_gather | solution.py:390
  150.2 8.2 %retention.4 = (bf16[128,2048]{1,0:T(8,128)(2,1)S(1)}, bf16[128,2048]{1,0:T(8,128)(2,1)S(1)}) custom-call(s32[3]{0:T(128)S(1)} %pad_add_fusion.refs_0_, f32[1024,2]{1,0:T(8,128)S(1)} %bitcast.86, f32[4,2,256]{2,1,0:T(2,128)S(1)} %bitcast.90, bf16[256,2048]{1,0:T(8,128)(2,1)} %get-tuple-element.59.refs_3_, bf16[256,2048]{1,0:T(8,128)(2,1)} %get-tuple-element.60.refs_4_, ...), custom_call_target="tpu_custom_call" | custom-call | flops 3000000000 | bytes 1048576 | tf_op jit(solution)/shard_map/retention/pallas_call | solution.py:255
  158.5 2.0 assemble.5
  160.5 4.5 %collective-permute-start.12 = (bf16[128,2048]{1,0:T(8,128)(2,1)S(1)}, bf16[128,2048]{1,0:T(8,128)(2,1)S(1)}, u32[]{:S(2)}, u32[]{:S(2)}) collective-permute-start(bf16[128,2048]{1,0:T(8,128)(2,1)S(1)} %get-tuple-element.71), channel_id=1, source_target_pairs={{0,1},{1,2},{2,3},{3,0},{4,5},{5,6},{6,7},{7,4},{8,9},{9,10},{10,1... | collective-permute-start | bytes 1572872 | tf_op jit(solution)/shard_map/ppermute | solution.py:368
  165.1 8.1 %retention.5 = (bf16[128,2048]{1,0:T(8,128)(2,1)S(1)}, bf16[128,2048]{1,0:T(8,128)(2,1)S(1)}) custom-call(s32[3]{0:T(128)S(1)} %pad_add_fusion.refs_0_, f32[1024,2]{1,0:T(8,128)S(1)} %bitcast.87, f32[4,2,256]{2,1,0:T(2,128)S(1)} %bitcast.91, bf16[256,2048]{1,0:T(8,128)(2,1)} %get-tuple-element.73.refs_3_, bf16[256,2048]{1,0:T(8,128)(2,1)} %get-tuple-element.60.refs_4_, ...), custom_call_target="tpu_custom_call" | custom-call | flops 3000000000 | bytes 1048576 | tf_op jit(solution)/shard_map/retention/pallas_call | solution.py:255
  173.1 4.3 %collective-permute-done.12 = bf16[128,2048]{1,0:T(8,128)(2,1)S(1)} collective-permute-done((bf16[128,2048]{1,0:T(8,128)(2,1)S(1)}, bf16[128,2048]{1,0:T(8,128)(2,1)S(1)}, u32[]{:S(2)}, u32[]{:S(2)}) %collective-permute-start.12) | collective-permute-done | bytes 524320 | tf_op jit(solution)/shard_map/ppermute | solution.py:368
  177.5 2.5 collective-permute-start.13
  180.1 8.5 %collective-permute-done.15 = bf16[128,2048]{1,0:T(8,128)(2,1)S(1)} collective-permute-done((bf16[128,2048]{1,0:T(8,128)(2,1)S(1)}, bf16[128,2048]{1,0:T(8,128)(2,1)S(1)}, u32[]{:S(2)}, u32[]{:S(2)}) %collective-permute-start.15) | collective-permute-done | bytes 524320 | tf_op jit(solution)/shard_map/ppermute | solution.py:368
  188.7 2.5 collective-permute-start.16
  191.3 8.0 %retention.6 = (bf16[128,2048]{1,0:T(8,128)(2,1)S(1)}, bf16[128,2048]{1,0:T(8,128)(2,1)S(1)}) custom-call(s32[3]{0:T(128)S(1)} %pad_add_fusion.refs_0_, f32[1024,2]{1,0:T(8,128)S(1)} %bitcast.88, f32[4,2,256]{2,1,0:T(2,128)S(1)} %bitcast.92, bf16[256,2048]{1,0:T(8,128)(2,1)} %get-tuple-element.77.refs_3_, bf16[256,2048]{1,0:T(8,128)(2,1)} %get-tuple-element.60.refs_4_, ...), custom_call_target="tpu_custom_call" | custom-call | flops 3000000000 | bytes 1048576 | tf_op jit(solution)/shard_map/retention/pallas_call | solution.py:255
  200.0 2.5 collective-permute-start.14
  202.5 8.5 %collective-permute-done.16 = bf16[128,2048]{1,0:T(8,128)(2,1)S(1)} collective-permute-done((bf16[128,2048]{1,0:T(8,128)(2,1)S(1)}, bf16[128,2048]{1,0:T(8,128)(2,1)S(1)}, u32[]{:S(2)}, u32[]{:S(2)}) %collective-permute-start.16) | collective-permute-done | bytes 524320 | tf_op jit(solution)/shard_map/ppermute | solution.py:368
  211.2 2.5 collective-permute-start.17
  213.8 8.1 %retention.7 = (bf16[128,2048]{1,0:T(8,128)(2,1)S(1)}, bf16[128,2048]{1,0:T(8,128)(2,1)S(1)}) custom-call(s32[3]{0:T(128)S(1)} %pad_add_fusion.refs_0_, f32[1024,2]{1,0:T(8,128)S(1)} %bitcast.89, f32[4,2,256]{2,1,0:T(2,128)S(1)} %bitcast.93, bf16[256,2048]{1,0:T(8,128)(2,1)} %get-tuple-element.80.refs_3_, bf16[256,2048]{1,0:T(8,128)(2,1)} %get-tuple-element.60.refs_4_, ...), custom_call_target="tpu_custom_call" | custom-call | flops 3000000000 | bytes 1048576 | tf_op jit(solution)/shard_map/retention/pallas_call | solution.py:255
  222.8 2.5 collective-permute-start.18
  225.4 8.2 %collective-permute-done.17.came_ref = bf16[128,2048]{1,0:T(8,128)(2,1)S(1)} collective-permute-done((bf16[128,2048]{1,0:T(8,128)(2,1)S(1)}, bf16[128,2048]{1,0:T(8,128)(2,1)S(1)}, u32[]{:S(2)}, u32[]{:S(2)}) %collective-permute-start.17) | collective-permute-done | bytes 524320 | tf_op jit(solution)/shard_map/ppermute | solution.py:368
  234.1 2.5 collective-permute-start.20
  236.6 8.3 %collective-permute-done.18.refs_1_ = bf16[128,2048]{1,0:T(8,128)(2,1)} collective-permute-done((bf16[128,2048]{1,0:T(8,128)(2,1)S(1)}, bf16[128,2048]{1,0:T(8,128)(2,1)}, u32[]{:S(2)}, u32[]{:S(2)}) %collective-permute-start.18) | collective-permute-done | bytes 524320 | tf_op jit(solution)/shard_map/ppermute | solution.py:368
  244.9 2.5 collective-permute-start.19
  247.4 8.8 %collective-permute-done.20.refs_2_ = bf16[128,2048]{1,0:T(8,128)(2,1)} collective-permute-done((bf16[128,2048]{1,0:T(8,128)(2,1)S(1)}, bf16[128,2048]{1,0:T(8,128)(2,1)}, u32[]{:S(2)}, u32[]{:S(2)}) %collective-permute-start.20) | collective-permute-done | bytes 524320 | tf_op jit(solution)/shard_map/ppermute | solution.py:368
  256.1 2.5 collective-permute-start.25
  258.6 3.4 %copy-done.4 = bf16[2048,2048]{1,0:T(8,128)(2,1)S(1)} copy-done((bf16[2048,2048]{1,0:T(8,128)(2,1)S(1)}, bf16[2048,2048]{1,0:T(8,128)(2,1)}, u32[]{:S(2)}) %copy-start.4) | copy-done | bytes 8388632
  262.0 3.4 %ffn.4.refs_4_ = bf16[1024,1024]{1,0:T(8,128)(2,1)} custom-call(s32[1]{0:T(128)} %bitcast.21.refs_0_, bf16[128,2048]{1,0:T(8,128)(2,1)S(1)} %get-tuple-element.85.refs_1_, bf16[128,2048]{1,0:T(8,128)(2,1)S(1)} %get-tuple-element.86.refs_2_, bf16[2048,2048]{1,0:T(8,128)(2,1)S(1)} %copy-done.4), custom_call_target="tpu_custom_call" | custom-call | flops 2147483648 | bytes 8388608 | tf_op jit(solution)/shard_map/ffn/pallas_call | solution.py:315
  265.4 4.6 %ffn.5.refs_4_ = bf16[1024,1024]{1,0:T(8,128)(2,1)} custom-call(s32[1]{0:T(128)} %bitcast.5.refs_0_, bf16[128,2048]{1,0:T(8,128)(2,1)} %collective-permute-done.18.refs_1_, bf16[128,2048]{1,0:T(8,128)(2,1)} %collective-permute-done.20.refs_2_, bf16[2048,2048]{1,0:T(8,128)(2,1)S(1)} %copy-done.5, ...), custom_call_target="tpu_custom_call", output_to_operand_aliasing={{}: (4, {})} | custom-call | flops 2147483648 | bytes 8388608 | tf_op jit(solution)/shard_map/ffn/pallas_call | solution.py:315
  270.0 8.6 %collective-permute-done.25.refs_2_ = bf16[128,2048]{1,0:T(8,128)(2,1)S(1)} collective-permute-done((bf16[128,2048]{1,0:T(8,128)(2,1)}, bf16[128,2048]{1,0:T(8,128)(2,1)S(1)}, u32[]{:S(2)}, u32[]{:S(2)}) %collective-permute-start.25) | collective-permute-done | bytes 524320 | tf_op jit(solution)/shard_map/ppermute | solution.py:368
  278.6 2.4 collective-permute-start.26
  281.0 1.0 pad_maximum_fusion.3
  282.0 3.4 %ffn.6.refs_4_ = bf16[1024,1024]{1,0:T(8,128)(2,1)} custom-call(s32[1]{0:T(128)} %bitcast.22.refs_0_, bf16[128,2048]{1,0:T(8,128)(2,1)S(1)} %collective-permute-done.19.refs_1_, bf16[128,2048]{1,0:T(8,128)(2,1)S(1)} %collective-permute-done.25.refs_2_, bf16[2048,2048]{1,0:T(8,128)(2,1)S(1)} %copy-done.5, ...), custom_call_target="tpu_custom_call", output_to_operand_aliasing={{}: (4, {})} | custom-call | flops 2147483648 | bytes 8388608 | tf_op jit(solution)/shard_map/ffn/pallas_call | solution.py:315
  285.4 4.3 %collective-permute-done.24.refs_1_ = bf16[128,2048]{1,0:T(8,128)(2,1)S(1)} collective-permute-done((bf16[128,2048]{1,0:T(8,128)(2,1)S(1)}, bf16[128,2048]{1,0:T(8,128)(2,1)S(1)}, u32[]{:S(2)}, u32[]{:S(2)}) %collective-permute-start.24) | collective-permute-done | bytes 524320 | tf_op jit(solution)/shard_map/ppermute | solution.py:368
  289.7 10.3 %collective-permute-done.26.refs_2_ = bf16[128,2048]{1,0:T(8,128)(2,1)S(1)} collective-permute-done((bf16[128,2048]{1,0:T(8,128)(2,1)S(1)}, bf16[128,2048]{1,0:T(8,128)(2,1)S(1)}, u32[]{:S(2)}, u32[]{:S(2)}) %collective-permute-start.26) | collective-permute-done | bytes 524320 | tf_op jit(solution)/shard_map/ppermute | solution.py:368
  300.0 3.4 %ffn.7 = bf16[1024,1024]{1,0:T(8,128)(2,1)} custom-call(s32[1]{0:T(128)} %bitcast.23.refs_0_, bf16[128,2048]{1,0:T(8,128)(2,1)S(1)} %collective-permute-done.24.refs_1_, bf16[128,2048]{1,0:T(8,128)(2,1)S(1)} %collective-permute-done.26.refs_2_, bf16[2048,2048]{1,0:T(8,128)(2,1)S(1)} %copy-done.5, ...), custom_call_target="tpu_custom_call", output_to_operand_aliasing={{}: (4, {})} | custom-call | flops 2147483648 | bytes 8388608 | tf_op jit(solution)/shard_map/ffn/pallas_call | solution.py:315
  (100 shorter events, 8.2 us)
Async XLA Ops:
  7.2 59.0 %copy-start = (f32[1024,8]{0,1:T(8,128)S(1)}, f32[1024,8]{0,1:T(8,128)}, u32[]{:S(2)}) copy-start(f32[1024,8]{0,1:T(8,128)} %param.16) | copy-start | bytes 98308
  7.2 1.5 copy-start.14
  7.2 86.8 %all-gather.4.cloned.1.call-start = ((), (), s32[]{:S(2)}) async-start(), calls=%async_computation | async-start | bytes 9437184 | tf_op jit(solution)/shard_map/all_gather | solution.py:363
  8.6 1.0 copy-start.15
  10.5 7.2 %copy-start.11 = (f32[4096,64]{0,1:T(8,128)S(1)}, f32[4096,64]{0,1:T(8,128)}, u32[]{:S(2)}) copy-start(f32[4096,64]{0,1:T(8,128)} %param.21) | copy-start | bytes 3145732
  10.6 7.2 %copy-start.12 = (f32[64,4096]{1,0:T(8,128)S(1)}, f32[64,4096]{1,0:T(8,128)}, u32[]{:S(2)}) copy-start(f32[64,4096]{1,0:T(8,128)} %param.20) | copy-start | bytes 3145732
  10.7 12.4 %collective-permute-start = (bf16[64,2048]{1,0:T(8,128)(2,1)S(1)}, bf16[64,2048]{1,0:T(8,128)(2,1)S(1)}, u32[]{:S(2)}, u32[]{:S(2)}) collective-permute-start(bf16[64,2048]{1,0:T(8,128)(2,1)S(1)} %get-tuple-element.108), channel_id=1, source_target_pairs={{0,1},{1,2},{2,3},{3,0},{4,5},{5,6},{6,7},{7,4},{8,9},{9,10},{10,1... | collective-permute-start | bytes 786440 | tf_op jit(solution)/shard_map/ppermute | solution.py:75
  13.8 19.7 %collective-permute-start.1 = (bf16[64,2048]{1,0:T(8,128)(2,1)S(1)}, bf16[64,2048]{1,0:T(8,128)(2,1)S(1)}, u32[]{:S(2)}, u32[]{:S(2)}) collective-permute-start(bf16[64,2048]{1,0:T(8,128)(2,1)S(1)} %get-tuple-element.107), channel_id=1, source_target_pairs={{0,2},{1,3},{2,0},{3,1},{4,6},{5,7},{6,4},{7,5},{8,10},{9,11},{10,... | collective-permute-start | bytes 786440 | tf_op jit(solution)/shard_map/ppermute | solution.py:75
  16.4 17.1 %collective-permute-start.2 = (bf16[64,2048]{1,0:T(8,128)(2,1)S(1)}, bf16[64,2048]{1,0:T(8,128)(2,1)S(1)}, u32[]{:S(2)}, u32[]{:S(2)}) collective-permute-start(bf16[64,2048]{1,0:T(8,128)(2,1)S(1)} %get-tuple-element.106), channel_id=1, source_target_pairs={{0,3},{1,0},{2,1},{3,2},{4,7},{5,4},{6,5},{7,6},{8,11},{9,8},{10,9... | collective-permute-start | bytes 786440 | tf_op jit(solution)/shard_map/ppermute | solution.py:75
  34.6 115.6 %all-gather.6.cloned.1.call-start = ((), (), s32[]{:S(2)}) async-start(), calls=%async_computation.1 | async-start | bytes 9437184 | tf_op jit(solution)/shard_map/all_gather | solution.py:390
  34.7 25.1 %copy-start.13 = (bf16[256,2048]{1,0:T(8,128)(2,1)S(1)}, bf16[256,2048]{1,0:T(8,128)(2,1)}, u32[]{:S(2)}) copy-start(bf16[256,2048]{1,0:T(8,128)(2,1)} %param.12) | copy-start | bytes 3145732
  34.7 14.5 %collective-permute-start.9 = (bf16[64,2048]{1,0:T(8,128)(2,1)S(1)}, bf16[64,2048]{1,0:T(8,128)(2,1)S(1)}, u32[]{:S(2)}, u32[]{:S(2)}) collective-permute-start(bf16[64,2048]{1,0:T(8,128)(2,1)S(1)} %get-tuple-element.102), channel_id=1, source_target_pairs={{0,1},{1,2},{2,3},{3,0},{4,5},{5,6},{6,7},{7,4},{8,9},{9,10},{10,1... | collective-permute-start | bytes 786440 | tf_op jit(solution)/shard_map/ppermute | solution.py:75
  40.9 17.8 %collective-permute-start.10 = (bf16[64,2048]{1,0:T(8,128)(2,1)S(1)}, bf16[64,2048]{1,0:T(8,128)(2,1)S(1)}, u32[]{:S(2)}, u32[]{:S(2)}) collective-permute-start(bf16[64,2048]{1,0:T(8,128)(2,1)S(1)} %get-tuple-element.101), channel_id=1, source_target_pairs={{0,2},{1,3},{2,0},{3,1},{4,6},{5,7},{6,4},{7,5},{8,10},{9,11},{10,... | collective-permute-start | bytes 786440 | tf_op jit(solution)/shard_map/ppermute | solution.py:75
  42.5 16.2 %collective-permute-start.11 = (bf16[64,2048]{1,0:T(8,128)(2,1)S(1)}, bf16[64,2048]{1,0:T(8,128)(2,1)S(1)}, u32[]{:S(2)}, u32[]{:S(2)}) collective-permute-start(bf16[64,2048]{1,0:T(8,128)(2,1)S(1)} %get-tuple-element.100), channel_id=1, source_target_pairs={{0,3},{1,0},{2,1},{3,2},{4,7},{5,4},{6,5},{7,6},{8,11},{9,8},{10,9... | collective-permute-start | bytes 786440 | tf_op jit(solution)/shard_map/ppermute | solution.py:75
  59.8 198.8 %all-gather.8.cloned.1.call-start = ((), (), s32[]{:S(2)}) async-start(), calls=%async_computation.2 | async-start | bytes 9437184 | tf_op jit(solution)/shard_map/all_gather | solution.py:407
  59.9 20.7 %collective-permute-start.3 = (bf16[128,2048]{1,0:T(8,128)(2,1)S(1)}, bf16[128,2048]{1,0:T(8,128)(2,1)S(1)}, u32[]{:S(2)}, u32[]{:S(2)}) collective-permute-start(bf16[128,2048]{1,0:T(8,128)(2,1)S(1)} %get-tuple-element.53.refs_1_.token_ref), channel_id=1, source_target_pairs={{0,1},{1,2},{2,3},{3,0},{4,5},{5,6},{6,7},{7,4},{8,9},{9,10},{10,1... | collective-permute-start | bytes 1572872 | tf_op jit(solution)/shard_map/ppermute | solution.py:368
  66.1 25.8 %collective-permute-start.4 = (bf16[128,2048]{1,0:T(8,128)(2,1)S(1)}, bf16[128,2048]{1,0:T(8,128)(2,1)S(1)}, u32[]{:S(2)}, u32[]{:S(2)}) collective-permute-start(bf16[128,2048]{1,0:T(8,128)(2,1)S(1)} %get-tuple-element.57.refs_2_.token_ref), channel_id=1, source_target_pairs={{0,1},{1,2},{2,3},{3,0},{4,5},{5,6},{6,7},{7,4},{8,9},{9,10},{10,1... | collective-permute-start | bytes 1572872 | tf_op jit(solution)/shard_map/ppermute | solution.py:368
  69.7 24.4 %copy-start.8 = (f32[2048]{0:T(1024)S(1)}, f32[2048]{0:T(1024)}, u32[]{:S(2)}) copy-start(f32[2048]{0:T(1024)} %param.13) | copy-start | bytes 24580
  80.7 22.6 %collective-permute-start.5 = (bf16[128,2048]{1,0:T(8,128)(2,1)S(1)}, bf16[128,2048]{1,0:T(8,128)(2,1)}, u32[]{:S(2)}, u32[]{:S(2)}) collective-permute-start(bf16[128,2048]{1,0:T(8,128)(2,1)S(1)} %collective-permute-done.3.refs_1_), channel_id=1, source_target_pairs={{0,1},{1,2},{2,3},{3,0},{4,5},{5,6},{6,7},{7,4},{8,9},{9,10},{10,1... | collective-permute-start | bytes 1572872 | tf_op jit(solution)/shard_map/ppermute | solution.py:368
  91.9 10.3 %copy-start.6 = (bf16[128,2048]{1,0:T(8,128)(2,1)}, bf16[128,2048]{1,0:T(8,128)(2,1)S(1)}, u32[]{:S(2)}) copy-start(bf16[128,2048]{1,0:T(8,128)(2,1)S(1)} %collective-permute-done.4.refs_2_) | copy-start | bytes 1572868
  91.9 22.6 %collective-permute-start.6 = (bf16[128,2048]{1,0:T(8,128)(2,1)S(1)}, bf16[128,2048]{1,0:T(8,128)(2,1)}, u32[]{:S(2)}, u32[]{:S(2)}) collective-permute-start(bf16[128,2048]{1,0:T(8,128)(2,1)S(1)} %collective-permute-done.4.refs_2_), channel_id=1, source_target_pairs={{0,1},{1,2},{2,3},{3,0},{4,5},{5,6},{6,7},{7,4},{8,9},{9,10},{10,1... | collective-permute-start | bytes 1572872 | tf_op jit(solution)/shard_map/ppermute | solution.py:368
  94.1 3.4 %copy-start.2 = (bf16[2048,2048]{1,0:T(8,128)(2,1)S(1)}, bf16[2048,2048]{1,0:T(8,128)(2,1)}, u32[]{:S(2)}) copy-start(bf16[2048,2048]{1,0:T(8,128)(2,1)} %all-gather.4.cloned.1.call-done.refs_6_) | copy-start | bytes 25165828
  103.3 28.2 %collective-permute-start.7 = (bf16[128,2048]{1,0:T(8,128)(2,1)}, bf16[128,2048]{1,0:T(8,128)(2,1)}, u32[]{:S(2)}, u32[]{:S(2)}) collective-permute-start(bf16[128,2048]{1,0:T(8,128)(2,1)} %collective-permute-done.5.refs_1_), channel_id=1, source_target_pairs={{0,1},{1,2},{2,3},{3,0},{4,5},{5,6},{6,7},{7,4},{8,9},{9,10},{10,1... | collective-permute-start | bytes 1572872 | tf_op jit(solution)/shard_map/ppermute | solution.py:368
  114.5 21.2 %collective-permute-start.8 = (bf16[128,2048]{1,0:T(8,128)(2,1)}, bf16[128,2048]{1,0:T(8,128)(2,1)}, u32[]{:S(2)}, u32[]{:S(2)}) collective-permute-start(bf16[128,2048]{1,0:T(8,128)(2,1)} %collective-permute-done.6.refs_2_), channel_id=1, source_target_pairs={{0,1},{1,2},{2,3},{3,0},{4,5},{5,6},{6,7},{7,4},{8,9},{9,10},{10,1... | collective-permute-start | bytes 1572872 | tf_op jit(solution)/shard_map/ppermute | solution.py:368
  116.2 3.4 %copy-start.3 = (bf16[2048,2048]{1,0:T(8,128)(2,1)S(1)}, bf16[2048,2048]{1,0:T(8,128)(2,1)}, u32[]{:S(2)}) copy-start(bf16[2048,2048]{1,0:T(8,128)(2,1)} %all-gather.4.cloned.1.call-done.refs_6_) | copy-start | bytes 25165828
  119.5 1.0 copy-start.7
  120.6 19.9 %slice-start = ((s8[8388608]{0:T(1024)(128)(4,1)}), s8[4194304]{0:T(1024)(128)(4,1)S(1)}, s32[]{:S(2)}) async-start(s8[8388608]{0:T(1024)(128)(4,1)} %bitcast.84), calls=%async_computation.3 | async-start | bytes 8388608
  125.3 10.4 %copy-start.10 = (bf16[4,64,2048]{2,1,0:T(8,128)(2,1)S(1)}, bf16[4,64,2048]{2,1,0:T(8,128)(2,1)}, u32[]{:S(2)}) copy-start(bf16[4,64,2048]{2,1,0:T(8,128)(2,1)} %pad_maximum_fusion.2) | copy-start | bytes 3145732
  125.3 15.2 %slice-start.1 = ((s8[8388608]{0:T(1024)(128)(4,1)}), s8[4194304]{0:T(1024)(128)(4,1)S(1)}, s32[]{:S(2)}) async-start(s8[8388608]{0:T(1024)(128)(4,1)} %bitcast.84), calls=%async_computation.4 | async-start | bytes 8388608
  136.7 21.8 %collective-permute-start.21 = (bf16[64,2048]{1,0:T(8,128)(2,1)}, bf16[64,2048]{1,0:T(8,128)(2,1)S(1)}, u32[]{:S(2)}, u32[]{:S(2)}) collective-permute-start(bf16[64,2048]{1,0:T(8,128)(2,1)} %get-tuple-element.98), channel_id=1, source_target_pairs={{0,1},{1,2},{2,3},{3,0},{4,5},{5,6},{6,7},{7,4},{8,9},{9,10},{10,1... | collective-permute-start | bytes 786440 | tf_op jit(solution)/shard_map/ppermute | solution.py:75
  137.1 21.3 %collective-permute-start.22 = (bf16[64,2048]{1,0:T(8,128)(2,1)}, bf16[64,2048]{1,0:T(8,128)(2,1)S(1)}, u32[]{:S(2)}, u32[]{:S(2)}) collective-permute-start(bf16[64,2048]{1,0:T(8,128)(2,1)} %get-tuple-element.97), channel_id=1, source_target_pairs={{0,2},{1,3},{2,0},{3,1},{4,6},{5,7},{6,4},{7,5},{8,10},{9,11},{10,... | collective-permute-start | bytes 786440 | tf_op jit(solution)/shard_map/ppermute | solution.py:75
  139.0 19.5 %collective-permute-start.23 = (bf16[64,2048]{1,0:T(8,128)(2,1)}, bf16[64,2048]{1,0:T(8,128)(2,1)}, u32[]{:S(2)}, u32[]{:S(2)}) collective-permute-start(bf16[64,2048]{1,0:T(8,128)(2,1)} %get-tuple-element.96), channel_id=1, source_target_pairs={{0,3},{1,0},{2,1},{3,2},{4,7},{5,4},{6,5},{7,6},{8,11},{9,8},{10,9... | collective-permute-start | bytes 786440 | tf_op jit(solution)/shard_map/ppermute | solution.py:75
  160.5 16.9 %collective-permute-start.12 = (bf16[128,2048]{1,0:T(8,128)(2,1)S(1)}, bf16[128,2048]{1,0:T(8,128)(2,1)S(1)}, u32[]{:S(2)}, u32[]{:S(2)}) collective-permute-start(bf16[128,2048]{1,0:T(8,128)(2,1)S(1)} %get-tuple-element.71), channel_id=1, source_target_pairs={{0,1},{1,2},{2,3},{3,0},{4,5},{5,6},{6,7},{7,4},{8,9},{9,10},{10,1... | collective-permute-start | bytes 1572872 | tf_op jit(solution)/shard_map/ppermute | solution.py:368
  165.0 23.6 %collective-permute-start.15 = (bf16[128,2048]{1,0:T(8,128)(2,1)S(1)}, bf16[128,2048]{1,0:T(8,128)(2,1)S(1)}, u32[]{:S(2)}, u32[]{:S(2)}) collective-permute-start(bf16[128,2048]{1,0:T(8,128)(2,1)S(1)} %get-tuple-element.72), channel_id=1, source_target_pairs={{0,1},{1,2},{2,3},{3,0},{4,5},{5,6},{6,7},{7,4},{8,9},{9,10},{10,1... | collective-permute-start | bytes 1572872 | tf_op jit(solution)/shard_map/ppermute | solution.py:368
  177.5 22.3 %collective-permute-start.13 = (bf16[128,2048]{1,0:T(8,128)(2,1)S(1)}, bf16[128,2048]{1,0:T(8,128)(2,1)S(1)}, u32[]{:S(2)}, u32[]{:S(2)}) collective-permute-start(bf16[128,2048]{1,0:T(8,128)(2,1)S(1)} %add_convert_fusion.3), channel_id=1, source_target_pairs={{0,1},{1,2},{2,3},{3,0},{4,5},{5,6},{6,7},{7,4},{8,9},{9,10},{10,1... | collective-permute-start | bytes 1572872 | tf_op jit(solution)/shard_map/ppermute | solution.py:368
  188.7 22.3 %collective-permute-start.16 = (bf16[128,2048]{1,0:T(8,128)(2,1)S(1)}, bf16[128,2048]{1,0:T(8,128)(2,1)S(1)}, u32[]{:S(2)}, u32[]{:S(2)}) collective-permute-start(bf16[128,2048]{1,0:T(8,128)(2,1)S(1)} %add_convert_fusion.1), channel_id=1, source_target_pairs={{0,1},{1,2},{2,3},{3,0},{4,5},{5,6},{6,7},{7,4},{8,9},{9,10},{10,1... | collective-permute-start | bytes 1572872 | tf_op jit(solution)/shard_map/ppermute | solution.py:368
  200.0 22.3 %collective-permute-start.14 = (bf16[128,2048]{1,0:T(8,128)(2,1)S(1)}, bf16[128,2048]{1,0:T(8,128)(2,1)S(1)}, u32[]{:S(2)}, u32[]{:S(2)}) collective-permute-start(bf16[128,2048]{1,0:T(8,128)(2,1)S(1)} %add_convert_fusion.2), channel_id=1, source_target_pairs={{0,1},{1,2},{2,3},{3,0},{4,5},{5,6},{6,7},{7,4},{8,9},{9,10},{10,1... | collective-permute-start | bytes 1572872 | tf_op jit(solution)/shard_map/ppermute | solution.py:368
  211.2 11.1 %copy-start.9 = (f32[2048]{0:T(1024)S(1)}, f32[2048]{0:T(1024)}, u32[]{:S(2)}) copy-start(f32[2048]{0:T(1024)} %param.14) | copy-start | bytes 24580
  211.2 22.3 %collective-permute-start.17 = (bf16[128,2048]{1,0:T(8,128)(2,1)S(1)}, bf16[128,2048]{1,0:T(8,128)(2,1)S(1)}, u32[]{:S(2)}, u32[]{:S(2)}) collective-permute-start(bf16[128,2048]{1,0:T(8,128)(2,1)S(1)} %add_convert_fusion), channel_id=1, source_target_pairs={{0,1},{1,2},{2,3},{3,0},{4,5},{5,6},{6,7},{7,4},{8,9},{9,10},{10,1... | collective-permute-start | bytes 1572872 | tf_op jit(solution)/shard_map/ppermute | solution.py:368
  222.8 22.1 %collective-permute-start.18 = (bf16[128,2048]{1,0:T(8,128)(2,1)S(1)}, bf16[128,2048]{1,0:T(8,128)(2,1)}, u32[]{:S(2)}, u32[]{:S(2)}) collective-permute-start(bf16[128,2048]{1,0:T(8,128)(2,1)S(1)} %get-tuple-element.85.refs_1_), channel_id=1, source_target_pairs={{0,1},{1,2},{2,3},{3,0},{4,5},{5,6},{6,7},{7,4},{8,9},{9,10},{10,1... | collective-permute-start | bytes 1572872 | tf_op jit(solution)/shard_map/ppermute | solution.py:368
  234.1 22.1 %collective-permute-start.20 = (bf16[128,2048]{1,0:T(8,128)(2,1)S(1)}, bf16[128,2048]{1,0:T(8,128)(2,1)}, u32[]{:S(2)}, u32[]{:S(2)}) collective-permute-start(bf16[128,2048]{1,0:T(8,128)(2,1)S(1)} %get-tuple-element.86.refs_2_), channel_id=1, source_target_pairs={{0,1},{1,2},{2,3},{3,0},{4,5},{5,6},{6,7},{7,4},{8,9},{9,10},{10,1... | collective-permute-start | bytes 1572872 | tf_op jit(solution)/shard_map/ppermute | solution.py:368
  244.9 25.1 %collective-permute-start.19 = (bf16[128,2048]{1,0:T(8,128)(2,1)}, bf16[128,2048]{1,0:T(8,128)(2,1)S(1)}, u32[]{:S(2)}, u32[]{:S(2)}) collective-permute-start(bf16[128,2048]{1,0:T(8,128)(2,1)} %collective-permute-done.18.refs_1_), channel_id=1, source_target_pairs={{0,1},{1,2},{2,3},{3,0},{4,5},{5,6},{6,7},{7,4},{8,9},{9,10},{10,1... | collective-permute-start | bytes 1572872 | tf_op jit(solution)/shard_map/ppermute | solution.py:368
  256.1 22.5 %collective-permute-start.25 = (bf16[128,2048]{1,0:T(8,128)(2,1)}, bf16[128,2048]{1,0:T(8,128)(2,1)S(1)}, u32[]{:S(2)}, u32[]{:S(2)}) collective-permute-start(bf16[128,2048]{1,0:T(8,128)(2,1)} %collective-permute-done.20.refs_2_), channel_id=1, source_target_pairs={{0,1},{1,2},{2,3},{3,0},{4,5},{5,6},{6,7},{7,4},{8,9},{9,10},{10,1... | collective-permute-start | bytes 1572872 | tf_op jit(solution)/shard_map/ppermute | solution.py:368
  258.6 3.4 %copy-start.4 = (bf16[2048,2048]{1,0:T(8,128)(2,1)S(1)}, bf16[2048,2048]{1,0:T(8,128)(2,1)}, u32[]{:S(2)}) copy-start(bf16[2048,2048]{1,0:T(8,128)(2,1)} %all-gather.8.cloned.1.call-done.refs_3_) | copy-start | bytes 25165828
  262.0 3.4 %copy-start.5 = (bf16[2048,2048]{1,0:T(8,128)(2,1)S(1)}, bf16[2048,2048]{1,0:T(8,128)(2,1)}, u32[]{:S(2)}) copy-start(bf16[2048,2048]{1,0:T(8,128)(2,1)} %all-gather.8.cloned.1.call-done.refs_3_) | copy-start | bytes 25165828
  270.0 19.7 %collective-permute-start.24 = (bf16[128,2048]{1,0:T(8,128)(2,1)S(1)}, bf16[128,2048]{1,0:T(8,128)(2,1)S(1)}, u32[]{:S(2)}, u32[]{:S(2)}) collective-permute-start(bf16[128,2048]{1,0:T(8,128)(2,1)S(1)} %collective-permute-done.19.refs_1_), channel_id=1, source_target_pairs={{0,1},{1,2},{2,3},{3,0},{4,5},{5,6},{6,7},{7,4},{8,9},{9,10},{10,1... | collective-permute-start | bytes 1572872 | tf_op jit(solution)/shard_map/ppermute | solution.py:368
  278.6 21.4 %collective-permute-start.26 = (bf16[128,2048]{1,0:T(8,128)(2,1)S(1)}, bf16[128,2048]{1,0:T(8,128)(2,1)S(1)}, u32[]{:S(2)}, u32[]{:S(2)}) collective-permute-start(bf16[128,2048]{1,0:T(8,128)(2,1)S(1)} %collective-permute-done.25.refs_2_), channel_id=1, source_target_pairs={{0,1},{1,2},{2,3},{3,0},{4,5},{5,6},{6,7},{7,4},{8,9},{9,10},{10,1... | collective-permute-start | bytes 1572872 | tf_op jit(solution)/shard_map/ppermute | solution.py:368
  300.0 3.4 %copy-start.1 = (f32[1024,8]{0,1:T(8,128)S(1)}, f32[1024,8]{0,1:T(8,128)}, u32[]{:S(2)}) copy-start(f32[1024,8]{0,1:T(8,128)} %param.16) | copy-start | bytes 98308
Sparse Core Ops, SparseCore 0:
  34.7 59.1 all-gather.3
  95.8 54.4 all-gather.5
  160.6 56.4 all-gather.7

commit v2 on v1

--- a/solution.py
+++ b/solution.py
@@ -201,7 +201,7 @@
     copies[count].wait()
     copies[count + 1].wait()
 
-    wide = min(wg, 2 * CHUNK)
+    wide = min(wg, 4 * CHUNK)
 
     def gating(i, _):
         band = chunk(i, wide)
@@ -215,7 +215,7 @@
     half = rows // len(out_refs)
 
     def leaving(i, _):
-        band = chunk(i, 2 * CHUNK)
+        band = chunk(i, 4 * CHUNK)
         branch = lax.dot_general(
             gated_ref[...], wo_ref[band, :], (((1,), (1,)), ((), ())), preferred_element_type=F32
         ).astype(BF)
@@ -223,7 +223,7 @@
             out_ref[:, band] = branch[k * half : (k + 1) * half]
         return _
 
-    lax.fori_loop(0, width // (2 * CHUNK), leaving, 0)
+    lax.fori_loop(0, width // (4 * CHUNK), leaving, 0)
 
 
 def retention(own, index, x, running, length, partner, blocks, w, heads, share):
@@ -286,7 +286,7 @@
 def ffn_kernel(count, scalars, *refs):
     w_ref, out_ref, x_ref = refs[count], refs[-2], refs[-1]
     x_ref[...] = stacked(refs[:count])
-    wide = min(out_ref.shape[1], 2 * CHUNK)
+    wide = min(out_ref.shape[1], 4 * CHUNK)
     chunks = out_ref.shape[1] // wide
 
     def one(i, _):

time: 311 us -> 310 us (level)
  transfers between devices with their start and end apart: 30 -> 30, of which waited for: 21 -> 21; matrix products, arithmetic and copies ran while one was open for 3% -> 3% of each run, Pallas kernels for 22% -> 21%
where the time goes in v2:
time: 310 us; the launch traced here: 309 us
  waiting for transfers between devices  145 us (47%)
  Pallas kernels  70.9 us (23%)
  starting transfers between devices  53.7 us (17%)
  between operations  15 us (5%)
  local copies, waits for them, and re-layouts  14.3 us (5%)
  other arithmetic  10 us (3%)
    ppermute x18, waiting for transfers between devices, onward(): return [lax.ppermute(half, 'mp', order) for half in halves]  110 us
    ppermute x18, starting transfers between devices, onward(): return [lax.ppermute(half, 'mp', order) for half in halves]  34.1 us
    ppermute x9, waiting for transfers between devices, exchanged(): lax.ppermute(piece, 'mp', [(i, (i + shift) % count) for i in range(count)])  30.8 us
    pallas_call x4, Pallas kernels, retention(): pl.pallas_call(lambda *refs: retention_kernel(dims, *refs), grid_spec=gri...  30.2 us
    pallas_call x4, Pallas kernels, project(): pl.pallas_call(lambda *refs: project_kernel(heads, *refs), grid_spec=grid...  21.6 us
    ppermute x9, starting transfers between devices, exchanged(): lax.ppermute(piece, 'mp', [(i, (i + shift) % count) for i in range(count)])  19.4 us
    pallas_call x4, Pallas kernels, ffn(): pl.pallas_call(lambda *refs: ffn_kernel(len(halves), *refs), grid_spec=gr...  14 us
    unnamed x38, local copies, waits for them, and re-layouts  11.6 us
  transfers between devices with their start and end apart: 30, of which 21 were waited for; matrix products, arithmetic and copies ran while one was open for 3% of the time, Pallas kernels for 21%

profile of v2, /device:TPU:0, one launch (start us, length us, event | category | flops | bytes accessed | tf_op | source)
XLA Modules:
  0.0 309.2 jit_solution(7266829151581181917)
XLA Ops:
  7.3 1.3 convert_element_type.121
  10.7 3.1 collective-permute-start
  13.8 2.6 collective-permute-start.1
  16.4 1.3 collective-permute-start.2
  18.1 5.0 %collective-permute-done.refs_1_ = bf16[64,2048]{1,0:T(8,128)(2,1)S(1)} collective-permute-done((bf16[64,2048]{1,0:T(8,128)(2,1)S(1)}, bf16[64,2048]{1,0:T(8,128)(2,1)S(1)}, u32[]{:S(2)}, u32[]{:S(2)}) %collective-permute-start) | collective-permute-done | bytes 262176 | tf_op jit(solution)/shard_map/ppermute | solution.py:75
  23.1 10.4 %collective-permute-done.1.refs_2_ = bf16[64,2048]{1,0:T(8,128)(2,1)S(1)} collective-permute-done((bf16[64,2048]{1,0:T(8,128)(2,1)S(1)}, bf16[64,2048]{1,0:T(8,128)(2,1)S(1)}, u32[]{:S(2)}, u32[]{:S(2)}) %collective-permute-start.1) | collective-permute-done | bytes 262176 | tf_op jit(solution)/shard_map/ppermute | solution.py:75
  33.5 1.0 assemble.3
  34.7 6.1 %collective-permute-start.9 = (bf16[64,2048]{1,0:T(8,128)(2,1)S(1)}, bf16[64,2048]{1,0:T(8,128)(2,1)S(1)}, u32[]{:S(2)}, u32[]{:S(2)}) collective-permute-start(bf16[64,2048]{1,0:T(8,128)(2,1)S(1)} %get-tuple-element.102), channel_id=1, source_target_pairs={{0,1},{1,2},{2,3},{3,0},{4,5},{5,6},{6,7},{7,4},{8,9},{9,10},{10,1... | collective-permute-start | bytes 786440 | tf_op jit(solution)/shard_map/ppermute | solution.py:75
  40.9 1.6 collective-permute-start.10
  43.3 5.9 %collective-permute-done.9.refs_1_ = bf16[64,2048]{1,0:T(8,128)(2,1)S(1)} collective-permute-done((bf16[64,2048]{1,0:T(8,128)(2,1)S(1)}, bf16[64,2048]{1,0:T(8,128)(2,1)S(1)}, u32[]{:S(2)}, u32[]{:S(2)}) %collective-permute-start.9) | collective-permute-done | bytes 262176 | tf_op jit(solution)/shard_map/ppermute | solution.py:75
  49.3 9.4 %collective-permute-done.10.refs_2_ = bf16[64,2048]{1,0:T(8,128)(2,1)S(1)} collective-permute-done((bf16[64,2048]{1,0:T(8,128)(2,1)S(1)}, bf16[64,2048]{1,0:T(8,128)(2,1)S(1)}, u32[]{:S(2)}, u32[]{:S(2)}) %collective-permute-start.10) | collective-permute-done | bytes 262176 | tf_op jit(solution)/shard_map/ppermute | solution.py:75
  58.7 1.1 assemble.4
  59.9 6.1 %collective-permute-start.3 = (bf16[128,2048]{1,0:T(8,128)(2,1)S(1)}, bf16[128,2048]{1,0:T(8,128)(2,1)S(1)}, u32[]{:S(2)}, u32[]{:S(2)}) collective-permute-start(bf16[128,2048]{1,0:T(8,128)(2,1)S(1)} %get-tuple-element.53.refs_1_.token_ref), channel_id=1, source_target_pairs={{0,1},{1,2},{2,3},{3,0},{4,5},{5,6},{6,7},{7,4},{8,9},{9,10},{10,1... | collective-permute-start | bytes 1572872 | tf_op jit(solution)/shard_map/ppermute | solution.py:368
  66.8 1.6 convert_element_type.123
  68.4 1.3 convert_element_type.122
  69.7 1.1 pad_maximum_fusion.2
  70.8 9.9 %collective-permute-done.3.refs_1_ = bf16[128,2048]{1,0:T(8,128)(2,1)S(1)} collective-permute-done((bf16[128,2048]{1,0:T(8,128)(2,1)S(1)}, bf16[128,2048]{1,0:T(8,128)(2,1)S(1)}, u32[]{:S(2)}, u32[]{:S(2)}) %collective-permute-start.3) | collective-permute-done | bytes 524320 | tf_op jit(solution)/shard_map/ppermute | solution.py:368
  80.9 11.0 %collective-permute-done.4.refs_2_ = bf16[128,2048]{1,0:T(8,128)(2,1)S(1)} collective-permute-done((bf16[128,2048]{1,0:T(8,128)(2,1)S(1)}, bf16[128,2048]{1,0:T(8,128)(2,1)S(1)}, u32[]{:S(2)}, u32[]{:S(2)}) %collective-permute-start.4) | collective-permute-done | bytes 524320 | tf_op jit(solution)/shard_map/ppermute | solution.py:368
  92.1 1.9 multiply_sine_fusion
  94.1 3.4 %copy-done.2 = bf16[2048,2048]{1,0:T(8,128)(2,1)S(1)} copy-done((bf16[2048,2048]{1,0:T(8,128)(2,1)S(1)}, bf16[2048,2048]{1,0:T(8,128)(2,1)}, u32[]{:S(2)}) %copy-start.2) | copy-done | bytes 8388632
  97.4 4.7 %project.5 = (bf16[256,2048]{1,0:T(8,128)(2,1)}, bf16[256,2048]{1,0:T(8,128)(2,1)}) custom-call(s32[1]{0:T(128)} %bitcast.21.refs_0_, bf16[128,2048]{1,0:T(8,128)(2,1)S(1)} %get-tuple-element.53.refs_1_.token_ref, bf16[128,2048]{1,0:T(8,128)(2,1)S(1)} %get-tuple-element.57.refs_2_.token_ref, f32[1,2048]{1,0:T(1,128)S(1)} %bitcast.94, ...), custom_call_target="tpu_custom_call" | custom-call | flops 536870912 | bytes 1048576 | tf_op jit(solution)/shard_map/project/pallas_call | solution.py:130
  102.2 1.1 collective-permute-done.5.refs_1_
  103.5 10.9 %collective-permute-done.6.refs_2_ = bf16[128,2048]{1,0:T(8,128)(2,1)} collective-permute-done((bf16[128,2048]{1,0:T(8,128)(2,1)S(1)}, bf16[128,2048]{1,0:T(8,128)(2,1)}, u32[]{:S(2)}, u32[]{:S(2)}) %collective-permute-start.6) | collective-permute-done | bytes 524320 | tf_op jit(solution)/shard_map/ppermute | solution.py:368
  116.2 3.4 %copy-done.3 = bf16[2048,2048]{1,0:T(8,128)(2,1)S(1)} copy-done((bf16[2048,2048]{1,0:T(8,128)(2,1)S(1)}, bf16[2048,2048]{1,0:T(8,128)(2,1)}, u32[]{:S(2)}) %copy-start.3) | copy-done | bytes 8388632
  119.5 1.0 copy-done.7
  120.6 4.7 %project.4 = (bf16[256,2048]{1,0:T(8,128)(2,1)}, bf16[256,2048]{1,0:T(8,128)(2,1)}) custom-call(s32[1]{0:T(128)} %bitcast.5.refs_0_, bf16[128,2048]{1,0:T(8,128)(2,1)S(1)} %collective-permute-done.3.refs_1_, bf16[128,2048]{1,0:T(8,128)(2,1)S(1)} %copy-done.7, f32[1,2048]{1,0:T(1,128)S(1)} %bitcast.95, f32[1024,128]{1,0:T(8,128)S(1)} %get-tuple-element.111.refs_4_, ...), custom_call_target="tpu_custom_call" | custom-call | flops 536870912 | bytes 1048576 | tf_op jit(solution)/shard_map/project/pallas_call | solution.py:130
  125.3 6.1 %project.6 = (bf16[256,2048]{1,0:T(8,128)(2,1)}, bf16[256,2048]{1,0:T(8,128)(2,1)}) custom-call(s32[1]{0:T(128)} %bitcast.22.refs_0_, bf16[128,2048]{1,0:T(8,128)(2,1)} %collective-permute-done.5.refs_1_, bf16[128,2048]{1,0:T(8,128)(2,1)} %collective-permute-done.6.refs_2_, f32[1,2048]{1,0:T(1,128)S(1)} %bitcast.96, ...), custom_call_target="tpu_custom_call" | custom-call | flops 536870912 | bytes 1048576 | tf_op jit(solution)/shard_map/project/pallas_call | solution.py:130
  131.4 4.3 %collective-permute-done.8.refs_2_ = bf16[128,2048]{1,0:T(8,128)(2,1)} collective-permute-done((bf16[128,2048]{1,0:T(8,128)(2,1)}, bf16[128,2048]{1,0:T(8,128)(2,1)}, u32[]{:S(2)}, u32[]{:S(2)}) %collective-permute-start.8) | collective-permute-done | bytes 524320 | tf_op jit(solution)/shard_map/ppermute | solution.py:368
  137.1 1.8 collective-permute-start.22
  139.0 1.5 collective-permute-start.23
  140.5 6.0 %project.7 = (bf16[256,2048]{1,0:T(8,128)(2,1)}, bf16[256,2048]{1,0:T(8,128)(2,1)}) custom-call(s32[1]{0:T(128)} %bitcast.23.refs_0_, bf16[128,2048]{1,0:T(8,128)(2,1)} %collective-permute-done.7.refs_1_, bf16[128,2048]{1,0:T(8,128)(2,1)} %collective-permute-done.8.refs_2_, f32[1,2048]{1,0:T(1,128)S(1)} %bitcast.97, ...), custom_call_target="tpu_custom_call" | custom-call | flops 536870912 | bytes 1048576 | tf_op jit(solution)/shard_map/project/pallas_call | solution.py:130
  146.5 3.8 %all-gather.6.cloned.1.call-done.refs_8_ = bf16[2048,2048]{1,0:T(8,128)(2,1)} async-done(((bf16[256,2048]{1,0:T(8,128)(2,1)}), bf16[2048,2048]{1,0:T(8,128)(2,1)}) %all-gather.6.cloned.1.call-update) | async-done | bytes 8388624 | tf_op jit(solution)/shard_map/all_gather | solution.py:390
  150.2 7.6 %retention.4 = (bf16[128,2048]{1,0:T(8,128)(2,1)S(1)}, bf16[128,2048]{1,0:T(8,128)(2,1)S(1)}) custom-call(s32[3]{0:T(128)S(1)} %pad_add_fusion.refs_0_, f32[1024,2]{1,0:T(8,128)S(1)} %bitcast.86, f32[4,2,256]{2,1,0:T(2,128)S(1)} %bitcast.90, bf16[256,2048]{1,0:T(8,128)(2,1)} %get-tuple-element.59.refs_3_, bf16[256,2048]{1,0:T(8,128)(2,1)} %get-tuple-element.60.refs_4_, ...), custom_call_target="tpu_custom_call" | custom-call | flops 3000000000 | bytes 1048576 | tf_op jit(solution)/shard_map/retention/pallas_call | solution.py:255
  157.9 2.0 assemble.5
  159.9 5.1 %collective-permute-start.12 = (bf16[128,2048]{1,0:T(8,128)(2,1)S(1)}, bf16[128,2048]{1,0:T(8,128)(2,1)S(1)}, u32[]{:S(2)}, u32[]{:S(2)}) collective-permute-start(bf16[128,2048]{1,0:T(8,128)(2,1)S(1)} %get-tuple-element.71), channel_id=1, source_target_pairs={{0,1},{1,2},{2,3},{3,0},{4,5},{5,6},{6,7},{7,4},{8,9},{9,10},{10,1... | collective-permute-start | bytes 1572872 | tf_op jit(solution)/shard_map/ppermute | solution.py:368
  165.1 7.6 %retention.5 = (bf16[128,2048]{1,0:T(8,128)(2,1)S(1)}, bf16[128,2048]{1,0:T(8,128)(2,1)S(1)}) custom-call(s32[3]{0:T(128)S(1)} %pad_add_fusion.refs_0_, f32[1024,2]{1,0:T(8,128)S(1)} %bitcast.87, f32[4,2,256]{2,1,0:T(2,128)S(1)} %bitcast.91, bf16[256,2048]{1,0:T(8,128)(2,1)} %get-tuple-element.73.refs_3_, bf16[256,2048]{1,0:T(8,128)(2,1)} %get-tuple-element.60.refs_4_, ...), custom_call_target="tpu_custom_call" | custom-call | flops 3000000000 | bytes 1048576 | tf_op jit(solution)/shard_map/retention/pallas_call | solution.py:255
  172.7 4.7 %collective-permute-done.12 = bf16[128,2048]{1,0:T(8,128)(2,1)S(1)} collective-permute-done((bf16[128,2048]{1,0:T(8,128)(2,1)S(1)}, bf16[128,2048]{1,0:T(8,128)(2,1)S(1)}, u32[]{:S(2)}, u32[]{:S(2)}) %collective-permute-start.12) | collective-permute-done | bytes 524320 | tf_op jit(solution)/shard_map/ppermute | solution.py:368
  177.6 2.5 collective-permute-start.13
  180.1 8.6 %collective-permute-done.15 = bf16[128,2048]{1,0:T(8,128)(2,1)S(1)} collective-permute-done((bf16[128,2048]{1,0:T(8,128)(2,1)S(1)}, bf16[128,2048]{1,0:T(8,128)(2,1)S(1)}, u32[]{:S(2)}, u32[]{:S(2)}) %collective-permute-start.15) | collective-permute-done | bytes 524320 | tf_op jit(solution)/shard_map/ppermute | solution.py:368
  188.8 2.5 collective-permute-start.16
  191.3 7.4 %retention.6 = (bf16[128,2048]{1,0:T(8,128)(2,1)S(1)}, bf16[128,2048]{1,0:T(8,128)(2,1)S(1)}) custom-call(s32[3]{0:T(128)S(1)} %pad_add_fusion.refs_0_, f32[1024,2]{1,0:T(8,128)S(1)} %bitcast.88, f32[4,2,256]{2,1,0:T(2,128)S(1)} %bitcast.92, bf16[256,2048]{1,0:T(8,128)(2,1)} %get-tuple-element.77.refs_3_, bf16[256,2048]{1,0:T(8,128)(2,1)} %get-tuple-element.60.refs_4_, ...), custom_call_target="tpu_custom_call" | custom-call | flops 3000000000 | bytes 1048576 | tf_op jit(solution)/shard_map/retention/pallas_call | solution.py:255
  198.7 1.2 collective-permute-done.13
  200.1 2.5 collective-permute-start.14
  202.5 8.6 %collective-permute-done.16 = bf16[128,2048]{1,0:T(8,128)(2,1)S(1)} collective-permute-done((bf16[128,2048]{1,0:T(8,128)(2,1)S(1)}, bf16[128,2048]{1,0:T(8,128)(2,1)S(1)}, u32[]{:S(2)}, u32[]{:S(2)}) %collective-permute-start.16) | collective-permute-done | bytes 524320 | tf_op jit(solution)/shard_map/ppermute | solution.py:368
  211.3 2.5 collective-permute-start.17
  213.8 7.5 %retention.7 = (bf16[128,2048]{1,0:T(8,128)(2,1)S(1)}, bf16[128,2048]{1,0:T(8,128)(2,1)S(1)}) custom-call(s32[3]{0:T(128)S(1)} %pad_add_fusion.refs_0_, f32[1024,2]{1,0:T(8,128)S(1)} %bitcast.89, f32[4,2,256]{2,1,0:T(2,128)S(1)} %bitcast.93, bf16[256,2048]{1,0:T(8,128)(2,1)} %get-tuple-element.80.refs_3_, bf16[256,2048]{1,0:T(8,128)(2,1)} %get-tuple-element.60.refs_4_, ...), custom_call_target="tpu_custom_call" | custom-call | flops 3000000000 | bytes 1048576 | tf_op jit(solution)/shard_map/retention/pallas_call | solution.py:255
  221.3 1.1 collective-permute-done.14.came_ref
  222.9 2.5 collective-permute-start.18
  225.4 8.3 %collective-permute-done.17.came_ref = bf16[128,2048]{1,0:T(8,128)(2,1)S(1)} collective-permute-done((bf16[128,2048]{1,0:T(8,128)(2,1)S(1)}, bf16[128,2048]{1,0:T(8,128)(2,1)S(1)}, u32[]{:S(2)}, u32[]{:S(2)}) %collective-permute-start.17) | collective-permute-done | bytes 524320 | tf_op jit(solution)/shard_map/ppermute | solution.py:368
  234.1 2.5 collective-permute-start.20
  236.6 8.4 %collective-permute-done.18.refs_1_ = bf16[128,2048]{1,0:T(8,128)(2,1)} collective-permute-done((bf16[128,2048]{1,0:T(8,128)(2,1)S(1)}, bf16[128,2048]{1,0:T(8,128)(2,1)}, u32[]{:S(2)}, u32[]{:S(2)}) %collective-permute-start.18) | collective-permute-done | bytes 524320 | tf_op jit(solution)/shard_map/ppermute | solution.py:368
  245.0 2.4 collective-permute-start.19
  247.4 8.8 %collective-permute-done.20.refs_2_ = bf16[128,2048]{1,0:T(8,128)(2,1)} collective-permute-done((bf16[128,2048]{1,0:T(8,128)(2,1)S(1)}, bf16[128,2048]{1,0:T(8,128)(2,1)}, u32[]{:S(2)}, u32[]{:S(2)}) %collective-permute-start.20) | collective-permute-done | bytes 524320 | tf_op jit(solution)/shard_map/ppermute | solution.py:368
  256.2 2.4 collective-permute-start.25
  258.6 3.4 %copy-done.4 = bf16[2048,2048]{1,0:T(8,128)(2,1)S(1)} copy-done((bf16[2048,2048]{1,0:T(8,128)(2,1)S(1)}, bf16[2048,2048]{1,0:T(8,128)(2,1)}, u32[]{:S(2)}) %copy-start.4) | copy-done | bytes 8388632
  262.0 3.2 %ffn.4.refs_4_ = bf16[1024,1024]{1,0:T(8,128)(2,1)} custom-call(s32[1]{0:T(128)} %bitcast.21.refs_0_, bf16[128,2048]{1,0:T(8,128)(2,1)S(1)} %get-tuple-element.85.refs_1_, bf16[128,2048]{1,0:T(8,128)(2,1)S(1)} %get-tuple-element.86.refs_2_, bf16[2048,2048]{1,0:T(8,128)(2,1)S(1)} %copy-done.4), custom_call_target="tpu_custom_call" | custom-call | flops 2147483648 | bytes 8388608 | tf_op jit(solution)/shard_map/ffn/pallas_call | solution.py:315
  265.4 4.4 %ffn.5.refs_4_ = bf16[1024,1024]{1,0:T(8,128)(2,1)} custom-call(s32[1]{0:T(128)} %bitcast.5.refs_0_, bf16[128,2048]{1,0:T(8,128)(2,1)} %collective-permute-done.18.refs_1_, bf16[128,2048]{1,0:T(8,128)(2,1)} %collective-permute-done.20.refs_2_, bf16[2048,2048]{1,0:T(8,128)(2,1)S(1)} %copy-done.5, ...), custom_call_target="tpu_custom_call", output_to_operand_aliasing={{}: (4, {})} | custom-call | flops 2147483648 | bytes 8388608 | tf_op jit(solution)/shard_map/ffn/pallas_call | solution.py:315
  269.8 8.8 %collective-permute-done.25.refs_2_ = bf16[128,2048]{1,0:T(8,128)(2,1)S(1)} collective-permute-done((bf16[128,2048]{1,0:T(8,128)(2,1)}, bf16[128,2048]{1,0:T(8,128)(2,1)S(1)}, u32[]{:S(2)}, u32[]{:S(2)}) %collective-permute-start.25) | collective-permute-done | bytes 524320 | tf_op jit(solution)/shard_map/ppermute | solution.py:368
  278.6 2.4 collective-permute-start.26
  281.0 1.0 pad_maximum_fusion.3
  282.0 3.2 %ffn.6.refs_4_ = bf16[1024,1024]{1,0:T(8,128)(2,1)} custom-call(s32[1]{0:T(128)} %bitcast.22.refs_0_, bf16[128,2048]{1,0:T(8,128)(2,1)S(1)} %collective-permute-done.19.refs_1_, bf16[128,2048]{1,0:T(8,128)(2,1)S(1)} %collective-permute-done.25.refs_2_, bf16[2048,2048]{1,0:T(8,128)(2,1)S(1)} %copy-done.5, ...), custom_call_target="tpu_custom_call", output_to_operand_aliasing={{}: (4, {})} | custom-call | flops 2147483648 | bytes 8388608 | tf_op jit(solution)/shard_map/ffn/pallas_call | solution.py:315
  285.2 4.6 %collective-permute-done.24.refs_1_ = bf16[128,2048]{1,0:T(8,128)(2,1)S(1)} collective-permute-done((bf16[128,2048]{1,0:T(8,128)(2,1)S(1)}, bf16[128,2048]{1,0:T(8,128)(2,1)S(1)}, u32[]{:S(2)}, u32[]{:S(2)}) %collective-permute-start.24) | collective-permute-done | bytes 524320 | tf_op jit(solution)/shard_map/ppermute | solution.py:368
  289.8 9.7 %collective-permute-done.26.refs_2_ = bf16[128,2048]{1,0:T(8,128)(2,1)S(1)} collective-permute-done((bf16[128,2048]{1,0:T(8,128)(2,1)S(1)}, bf16[128,2048]{1,0:T(8,128)(2,1)S(1)}, u32[]{:S(2)}, u32[]{:S(2)}) %collective-permute-start.26) | collective-permute-done | bytes 524320 | tf_op jit(solution)/shard_map/ppermute | solution.py:368
  299.5 3.2 %ffn.7 = bf16[1024,1024]{1,0:T(8,128)(2,1)} custom-call(s32[1]{0:T(128)} %bitcast.23.refs_0_, bf16[128,2048]{1,0:T(8,128)(2,1)S(1)} %collective-permute-done.24.refs_1_, bf16[128,2048]{1,0:T(8,128)(2,1)S(1)} %collective-permute-done.26.refs_2_, bf16[2048,2048]{1,0:T(8,128)(2,1)S(1)} %copy-done.5, ...), custom_call_target="tpu_custom_call", output_to_operand_aliasing={{}: (4, {})} | custom-call | flops 2147483648 | bytes 8388608 | tf_op jit(solution)/shard_map/ffn/pallas_call | solution.py:315
  (100 shorter events, 9.1 us)
Async XLA Ops:
  7.2 59.0 %copy-start = (f32[1024,8]{0,1:T(8,128)S(1)}, f32[1024,8]{0,1:T(8,128)}, u32[]{:S(2)}) copy-start(f32[1024,8]{0,1:T(8,128)} %param.16) | copy-start | bytes 98308
  7.2 1.5 copy-start.14
  7.2 86.8 %all-gather.4.cloned.1.call-start = ((), (), s32[]{:S(2)}) async-start(), calls=%async_computation | async-start | bytes 9437184 | tf_op jit(solution)/shard_map/all_gather | solution.py:363
  8.6 1.0 copy-start.15
  10.5 7.2 %copy-start.11 = (f32[4096,64]{0,1:T(8,128)S(1)}, f32[4096,64]{0,1:T(8,128)}, u32[]{:S(2)}) copy-start(f32[4096,64]{0,1:T(8,128)} %param.21) | copy-start | bytes 3145732
  10.6 7.2 %copy-start.12 = (f32[64,4096]{1,0:T(8,128)S(1)}, f32[64,4096]{1,0:T(8,128)}, u32[]{:S(2)}) copy-start(f32[64,4096]{1,0:T(8,128)} %param.20) | copy-start | bytes 3145732
  10.7 12.4 %collective-permute-start = (bf16[64,2048]{1,0:T(8,128)(2,1)S(1)}, bf16[64,2048]{1,0:T(8,128)(2,1)S(1)}, u32[]{:S(2)}, u32[]{:S(2)}) collective-permute-start(bf16[64,2048]{1,0:T(8,128)(2,1)S(1)} %get-tuple-element.108), channel_id=1, source_target_pairs={{0,1},{1,2},{2,3},{3,0},{4,5},{5,6},{6,7},{7,4},{8,9},{9,10},{10,1... | collective-permute-start | bytes 786440 | tf_op jit(solution)/shard_map/ppermute | solution.py:75
  13.8 19.7 %collective-permute-start.1 = (bf16[64,2048]{1,0:T(8,128)(2,1)S(1)}, bf16[64,2048]{1,0:T(8,128)(2,1)S(1)}, u32[]{:S(2)}, u32[]{:S(2)}) collective-permute-start(bf16[64,2048]{1,0:T(8,128)(2,1)S(1)} %get-tuple-element.107), channel_id=1, source_target_pairs={{0,2},{1,3},{2,0},{3,1},{4,6},{5,7},{6,4},{7,5},{8,10},{9,11},{10,... | collective-permute-start | bytes 786440 | tf_op jit(solution)/shard_map/ppermute | solution.py:75
  16.4 17.1 %collective-permute-start.2 = (bf16[64,2048]{1,0:T(8,128)(2,1)S(1)}, bf16[64,2048]{1,0:T(8,128)(2,1)S(1)}, u32[]{:S(2)}, u32[]{:S(2)}) collective-permute-start(bf16[64,2048]{1,0:T(8,128)(2,1)S(1)} %get-tuple-element.106), channel_id=1, source_target_pairs={{0,3},{1,0},{2,1},{3,2},{4,7},{5,4},{6,5},{7,6},{8,11},{9,8},{10,9... | collective-permute-start | bytes 786440 | tf_op jit(solution)/shard_map/ppermute | solution.py:75
  34.6 115.6 %all-gather.6.cloned.1.call-start = ((), (), s32[]{:S(2)}) async-start(), calls=%async_computation.1 | async-start | bytes 9437184 | tf_op jit(solution)/shard_map/all_gather | solution.py:390
  34.7 25.1 %copy-start.13 = (bf16[256,2048]{1,0:T(8,128)(2,1)S(1)}, bf16[256,2048]{1,0:T(8,128)(2,1)}, u32[]{:S(2)}) copy-start(bf16[256,2048]{1,0:T(8,128)(2,1)} %param.12) | copy-start | bytes 3145732
  34.7 14.5 %collective-permute-start.9 = (bf16[64,2048]{1,0:T(8,128)(2,1)S(1)}, bf16[64,2048]{1,0:T(8,128)(2,1)S(1)}, u32[]{:S(2)}, u32[]{:S(2)}) collective-permute-start(bf16[64,2048]{1,0:T(8,128)(2,1)S(1)} %get-tuple-element.102), channel_id=1, source_target_pairs={{0,1},{1,2},{2,3},{3,0},{4,5},{5,6},{6,7},{7,4},{8,9},{9,10},{10,1... | collective-permute-start | bytes 786440 | tf_op jit(solution)/shard_map/ppermute | solution.py:75
  40.9 17.8 %collective-permute-start.10 = (bf16[64,2048]{1,0:T(8,128)(2,1)S(1)}, bf16[64,2048]{1,0:T(8,128)(2,1)S(1)}, u32[]{:S(2)}, u32[]{:S(2)}) collective-permute-start(bf16[64,2048]{1,0:T(8,128)(2,1)S(1)} %get-tuple-element.101), channel_id=1, source_target_pairs={{0,2},{1,3},{2,0},{3,1},{4,6},{5,7},{6,4},{7,5},{8,10},{9,11},{10,... | collective-permute-start | bytes 786440 | tf_op jit(solution)/shard_map/ppermute | solution.py:75
  42.5 16.2 %collective-permute-start.11 = (bf16[64,2048]{1,0:T(8,128)(2,1)S(1)}, bf16[64,2048]{1,0:T(8,128)(2,1)S(1)}, u32[]{:S(2)}, u32[]{:S(2)}) collective-permute-start(bf16[64,2048]{1,0:T(8,128)(2,1)S(1)} %get-tuple-element.100), channel_id=1, source_target_pairs={{0,3},{1,0},{2,1},{3,2},{4,7},{5,4},{6,5},{7,6},{8,11},{9,8},{10,9... | collective-permute-start | bytes 786440 | tf_op jit(solution)/shard_map/ppermute | solution.py:75
  59.8 198.8 %all-gather.8.cloned.1.call-start = ((), (), s32[]{:S(2)}) async-start(), calls=%async_computation.2 | async-start | bytes 9437184 | tf_op jit(solution)/shard_map/all_gather | solution.py:407
  59.9 20.7 %collective-permute-start.3 = (bf16[128,2048]{1,0:T(8,128)(2,1)S(1)}, bf16[128,2048]{1,0:T(8,128)(2,1)S(1)}, u32[]{:S(2)}, u32[]{:S(2)}) collective-permute-start(bf16[128,2048]{1,0:T(8,128)(2,1)S(1)} %get-tuple-element.53.refs_1_.token_ref), channel_id=1, source_target_pairs={{0,1},{1,2},{2,3},{3,0},{4,5},{5,6},{6,7},{7,4},{8,9},{9,10},{10,1... | collective-permute-start | bytes 1572872 | tf_op jit(solution)/shard_map/ppermute | solution.py:368
  66.1 25.8 %collective-permute-start.4 = (bf16[128,2048]{1,0:T(8,128)(2,1)S(1)}, bf16[128,2048]{1,0:T(8,128)(2,1)S(1)}, u32[]{:S(2)}, u32[]{:S(2)}) collective-permute-start(bf16[128,2048]{1,0:T(8,128)(2,1)S(1)} %get-tuple-element.57.refs_2_.token_ref), channel_id=1, source_target_pairs={{0,1},{1,2},{2,3},{3,0},{4,5},{5,6},{6,7},{7,4},{8,9},{9,10},{10,1... | collective-permute-start | bytes 1572872 | tf_op jit(solution)/shard_map/ppermute | solution.py:368
  69.7 24.4 %copy-start.8 = (f32[2048]{0:T(1024)S(1)}, f32[2048]{0:T(1024)}, u32[]{:S(2)}) copy-start(f32[2048]{0:T(1024)} %param.13) | copy-start | bytes 24580
  80.7 22.6 %collective-permute-start.5 = (bf16[128,2048]{1,0:T(8,128)(2,1)S(1)}, bf16[128,2048]{1,0:T(8,128)(2,1)}, u32[]{:S(2)}, u32[]{:S(2)}) collective-permute-start(bf16[128,2048]{1,0:T(8,128)(2,1)S(1)} %collective-permute-done.3.refs_1_), channel_id=1, source_target_pairs={{0,1},{1,2},{2,3},{3,0},{4,5},{5,6},{6,7},{7,4},{8,9},{9,10},{10,1... | collective-permute-start | bytes 1572872 | tf_op jit(solution)/shard_map/ppermute | solution.py:368
  91.9 10.3 %copy-start.6 = (bf16[128,2048]{1,0:T(8,128)(2,1)}, bf16[128,2048]{1,0:T(8,128)(2,1)S(1)}, u32[]{:S(2)}) copy-start(bf16[128,2048]{1,0:T(8,128)(2,1)S(1)} %collective-permute-done.4.refs_2_) | copy-start | bytes 1572868
  91.9 22.6 %collective-permute-start.6 = (bf16[128,2048]{1,0:T(8,128)(2,1)S(1)}, bf16[128,2048]{1,0:T(8,128)(2,1)}, u32[]{:S(2)}, u32[]{:S(2)}) collective-permute-start(bf16[128,2048]{1,0:T(8,128)(2,1)S(1)} %collective-permute-done.4.refs_2_), channel_id=1, source_target_pairs={{0,1},{1,2},{2,3},{3,0},{4,5},{5,6},{6,7},{7,4},{8,9},{9,10},{10,1... | collective-permute-start | bytes 1572872 | tf_op jit(solution)/shard_map/ppermute | solution.py:368
  94.1 3.4 %copy-start.2 = (bf16[2048,2048]{1,0:T(8,128)(2,1)S(1)}, bf16[2048,2048]{1,0:T(8,128)(2,1)}, u32[]{:S(2)}) copy-start(bf16[2048,2048]{1,0:T(8,128)(2,1)} %all-gather.4.cloned.1.call-done.refs_6_) | copy-start | bytes 25165828
  103.3 28.2 %collective-permute-start.7 = (bf16[128,2048]{1,0:T(8,128)(2,1)}, bf16[128,2048]{1,0:T(8,128)(2,1)}, u32[]{:S(2)}, u32[]{:S(2)}) collective-permute-start(bf16[128,2048]{1,0:T(8,128)(2,1)} %collective-permute-done.5.refs_1_), channel_id=1, source_target_pairs={{0,1},{1,2},{2,3},{3,0},{4,5},{5,6},{6,7},{7,4},{8,9},{9,10},{10,1... | collective-permute-start | bytes 1572872 | tf_op jit(solution)/shard_map/ppermute | solution.py:368
  114.5 21.2 %collective-permute-start.8 = (bf16[128,2048]{1,0:T(8,128)(2,1)}, bf16[128,2048]{1,0:T(8,128)(2,1)}, u32[]{:S(2)}, u32[]{:S(2)}) collective-permute-start(bf16[128,2048]{1,0:T(8,128)(2,1)} %collective-permute-done.6.refs_2_), channel_id=1, source_target_pairs={{0,1},{1,2},{2,3},{3,0},{4,5},{5,6},{6,7},{7,4},{8,9},{9,10},{10,1... | collective-permute-start | bytes 1572872 | tf_op jit(solution)/shard_map/ppermute | solution.py:368
  116.2 3.4 %copy-start.3 = (bf16[2048,2048]{1,0:T(8,128)(2,1)S(1)}, bf16[2048,2048]{1,0:T(8,128)(2,1)}, u32[]{:S(2)}) copy-start(bf16[2048,2048]{1,0:T(8,128)(2,1)} %all-gather.4.cloned.1.call-done.refs_6_) | copy-start | bytes 25165828
  119.5 1.0 copy-start.7
  120.6 19.9 %slice-start = ((s8[8388608]{0:T(1024)(128)(4,1)}), s8[4194304]{0:T(1024)(128)(4,1)S(1)}, s32[]{:S(2)}) async-start(s8[8388608]{0:T(1024)(128)(4,1)} %bitcast.84), calls=%async_computation.3 | async-start | bytes 8388608
  125.3 10.4 %copy-start.10 = (bf16[4,64,2048]{2,1,0:T(8,128)(2,1)S(1)}, bf16[4,64,2048]{2,1,0:T(8,128)(2,1)}, u32[]{:S(2)}) copy-start(bf16[4,64,2048]{2,1,0:T(8,128)(2,1)} %pad_maximum_fusion.2) | copy-start | bytes 3145732
  125.3 15.2 %slice-start.1 = ((s8[8388608]{0:T(1024)(128)(4,1)}), s8[4194304]{0:T(1024)(128)(4,1)S(1)}, s32[]{:S(2)}) async-start(s8[8388608]{0:T(1024)(128)(4,1)} %bitcast.84), calls=%async_computation.4 | async-start | bytes 8388608
  136.7 21.2 %collective-permute-start.21 = (bf16[64,2048]{1,0:T(8,128)(2,1)}, bf16[64,2048]{1,0:T(8,128)(2,1)S(1)}, u32[]{:S(2)}, u32[]{:S(2)}) collective-permute-start(bf16[64,2048]{1,0:T(8,128)(2,1)} %get-tuple-element.98), channel_id=1, source_target_pairs={{0,1},{1,2},{2,3},{3,0},{4,5},{5,6},{6,7},{7,4},{8,9},{9,10},{10,1... | collective-permute-start | bytes 786440 | tf_op jit(solution)/shard_map/ppermute | solution.py:75
  137.1 20.7 %collective-permute-start.22 = (bf16[64,2048]{1,0:T(8,128)(2,1)}, bf16[64,2048]{1,0:T(8,128)(2,1)S(1)}, u32[]{:S(2)}, u32[]{:S(2)}) collective-permute-start(bf16[64,2048]{1,0:T(8,128)(2,1)} %get-tuple-element.97), channel_id=1, source_target_pairs={{0,2},{1,3},{2,0},{3,1},{4,6},{5,7},{6,4},{7,5},{8,10},{9,11},{10,... | collective-permute-start | bytes 786440 | tf_op jit(solution)/shard_map/ppermute | solution.py:75
  139.0 18.9 %collective-permute-start.23 = (bf16[64,2048]{1,0:T(8,128)(2,1)}, bf16[64,2048]{1,0:T(8,128)(2,1)}, u32[]{:S(2)}, u32[]{:S(2)}) collective-permute-start(bf16[64,2048]{1,0:T(8,128)(2,1)} %get-tuple-element.96), channel_id=1, source_target_pairs={{0,3},{1,0},{2,1},{3,2},{4,7},{5,4},{6,5},{7,6},{8,11},{9,8},{10,9... | collective-permute-start | bytes 786440 | tf_op jit(solution)/shard_map/ppermute | solution.py:75
  159.9 17.5 %collective-permute-start.12 = (bf16[128,2048]{1,0:T(8,128)(2,1)S(1)}, bf16[128,2048]{1,0:T(8,128)(2,1)S(1)}, u32[]{:S(2)}, u32[]{:S(2)}) collective-permute-start(bf16[128,2048]{1,0:T(8,128)(2,1)S(1)} %get-tuple-element.71), channel_id=1, source_target_pairs={{0,1},{1,2},{2,3},{3,0},{4,5},{5,6},{6,7},{7,4},{8,9},{9,10},{10,1... | collective-permute-start | bytes 1572872 | tf_op jit(solution)/shard_map/ppermute | solution.py:368
  165.0 23.7 %collective-permute-start.15 = (bf16[128,2048]{1,0:T(8,128)(2,1)S(1)}, bf16[128,2048]{1,0:T(8,128)(2,1)S(1)}, u32[]{:S(2)}, u32[]{:S(2)}) collective-permute-start(bf16[128,2048]{1,0:T(8,128)(2,1)S(1)} %get-tuple-element.72), channel_id=1, source_target_pairs={{0,1},{1,2},{2,3},{3,0},{4,5},{5,6},{6,7},{7,4},{8,9},{9,10},{10,1... | collective-permute-start | bytes 1572872 | tf_op jit(solution)/shard_map/ppermute | solution.py:368
  177.6 22.3 %collective-permute-start.13 = (bf16[128,2048]{1,0:T(8,128)(2,1)S(1)}, bf16[128,2048]{1,0:T(8,128)(2,1)S(1)}, u32[]{:S(2)}, u32[]{:S(2)}) collective-permute-start(bf16[128,2048]{1,0:T(8,128)(2,1)S(1)} %add_convert_fusion.3), channel_id=1, source_target_pairs={{0,1},{1,2},{2,3},{3,0},{4,5},{5,6},{6,7},{7,4},{8,9},{9,10},{10,1... | collective-permute-start | bytes 1572872 | tf_op jit(solution)/shard_map/ppermute | solution.py:368
  188.8 22.3 %collective-permute-start.16 = (bf16[128,2048]{1,0:T(8,128)(2,1)S(1)}, bf16[128,2048]{1,0:T(8,128)(2,1)S(1)}, u32[]{:S(2)}, u32[]{:S(2)}) collective-permute-start(bf16[128,2048]{1,0:T(8,128)(2,1)S(1)} %add_convert_fusion.1), channel_id=1, source_target_pairs={{0,1},{1,2},{2,3},{3,0},{4,5},{5,6},{6,7},{7,4},{8,9},{9,10},{10,1... | collective-permute-start | bytes 1572872 | tf_op jit(solution)/shard_map/ppermute | solution.py:368
  200.1 22.3 %collective-permute-start.14 = (bf16[128,2048]{1,0:T(8,128)(2,1)S(1)}, bf16[128,2048]{1,0:T(8,128)(2,1)S(1)}, u32[]{:S(2)}, u32[]{:S(2)}) collective-permute-start(bf16[128,2048]{1,0:T(8,128)(2,1)S(1)} %add_convert_fusion.2), channel_id=1, source_target_pairs={{0,1},{1,2},{2,3},{3,0},{4,5},{5,6},{6,7},{7,4},{8,9},{9,10},{10,1... | collective-permute-start | bytes 1572872 | tf_op jit(solution)/shard_map/ppermute | solution.py:368
  211.3 11.1 %copy-start.9 = (f32[2048]{0:T(1024)S(1)}, f32[2048]{0:T(1024)}, u32[]{:S(2)}) copy-start(f32[2048]{0:T(1024)} %param.14) | copy-start | bytes 24580
  211.3 22.3 %collective-permute-start.17 = (bf16[128,2048]{1,0:T(8,128)(2,1)S(1)}, bf16[128,2048]{1,0:T(8,128)(2,1)S(1)}, u32[]{:S(2)}, u32[]{:S(2)}) collective-permute-start(bf16[128,2048]{1,0:T(8,128)(2,1)S(1)} %add_convert_fusion), channel_id=1, source_target_pairs={{0,1},{1,2},{2,3},{3,0},{4,5},{5,6},{6,7},{7,4},{8,9},{9,10},{10,1... | collective-permute-start | bytes 1572872 | tf_op jit(solution)/shard_map/ppermute | solution.py:368
  222.9 22.1 %collective-permute-start.18 = (bf16[128,2048]{1,0:T(8,128)(2,1)S(1)}, bf16[128,2048]{1,0:T(8,128)(2,1)}, u32[]{:S(2)}, u32[]{:S(2)}) collective-permute-start(bf16[128,2048]{1,0:T(8,128)(2,1)S(1)} %get-tuple-element.85.refs_1_), channel_id=1, source_target_pairs={{0,1},{1,2},{2,3},{3,0},{4,5},{5,6},{6,7},{7,4},{8,9},{9,10},{10,1... | collective-permute-start | bytes 1572872 | tf_op jit(solution)/shard_map/ppermute | solution.py:368
  234.1 22.1 %collective-permute-start.20 = (bf16[128,2048]{1,0:T(8,128)(2,1)S(1)}, bf16[128,2048]{1,0:T(8,128)(2,1)}, u32[]{:S(2)}, u32[]{:S(2)}) collective-permute-start(bf16[128,2048]{1,0:T(8,128)(2,1)S(1)} %get-tuple-element.86.refs_2_), channel_id=1, source_target_pairs={{0,1},{1,2},{2,3},{3,0},{4,5},{5,6},{6,7},{7,4},{8,9},{9,10},{10,1... | collective-permute-start | bytes 1572872 | tf_op jit(solution)/shard_map/ppermute | solution.py:368
  245.0 24.8 %collective-permute-start.19 = (bf16[128,2048]{1,0:T(8,128)(2,1)}, bf16[128,2048]{1,0:T(8,128)(2,1)S(1)}, u32[]{:S(2)}, u32[]{:S(2)}) collective-permute-start(bf16[128,2048]{1,0:T(8,128)(2,1)} %collective-permute-done.18.refs_1_), channel_id=1, source_target_pairs={{0,1},{1,2},{2,3},{3,0},{4,5},{5,6},{6,7},{7,4},{8,9},{9,10},{10,1... | collective-permute-start | bytes 1572872 | tf_op jit(solution)/shard_map/ppermute | solution.py:368
  256.2 22.4 %collective-permute-start.25 = (bf16[128,2048]{1,0:T(8,128)(2,1)}, bf16[128,2048]{1,0:T(8,128)(2,1)S(1)}, u32[]{:S(2)}, u32[]{:S(2)}) collective-permute-start(bf16[128,2048]{1,0:T(8,128)(2,1)} %collective-permute-done.20.refs_2_), channel_id=1, source_target_pairs={{0,1},{1,2},{2,3},{3,0},{4,5},{5,6},{6,7},{7,4},{8,9},{9,10},{10,1... | collective-permute-start | bytes 1572872 | tf_op jit(solution)/shard_map/ppermute | solution.py:368
  258.6 3.4 %copy-start.4 = (bf16[2048,2048]{1,0:T(8,128)(2,1)S(1)}, bf16[2048,2048]{1,0:T(8,128)(2,1)}, u32[]{:S(2)}) copy-start(bf16[2048,2048]{1,0:T(8,128)(2,1)} %all-gather.8.cloned.1.call-done.refs_3_) | copy-start | bytes 25165828
  262.0 3.4 %copy-start.5 = (bf16[2048,2048]{1,0:T(8,128)(2,1)S(1)}, bf16[2048,2048]{1,0:T(8,128)(2,1)}, u32[]{:S(2)}) copy-start(bf16[2048,2048]{1,0:T(8,128)(2,1)} %all-gather.8.cloned.1.call-done.refs_3_) | copy-start | bytes 25165828
  269.8 20.0 %collective-permute-start.24 = (bf16[128,2048]{1,0:T(8,128)(2,1)S(1)}, bf16[128,2048]{1,0:T(8,128)(2,1)S(1)}, u32[]{:S(2)}, u32[]{:S(2)}) collective-permute-start(bf16[128,2048]{1,0:T(8,128)(2,1)S(1)} %collective-permute-done.19.refs_1_), channel_id=1, source_target_pairs={{0,1},{1,2},{2,3},{3,0},{4,5},{5,6},{6,7},{7,4},{8,9},{9,10},{10,1... | collective-permute-start | bytes 1572872 | tf_op jit(solution)/shard_map/ppermute | solution.py:368
  278.6 20.9 %collective-permute-start.26 = (bf16[128,2048]{1,0:T(8,128)(2,1)S(1)}, bf16[128,2048]{1,0:T(8,128)(2,1)S(1)}, u32[]{:S(2)}, u32[]{:S(2)}) collective-permute-start(bf16[128,2048]{1,0:T(8,128)(2,1)S(1)} %collective-permute-done.25.refs_2_), channel_id=1, source_target_pairs={{0,1},{1,2},{2,3},{3,0},{4,5},{5,6},{6,7},{7,4},{8,9},{9,10},{10,1... | collective-permute-start | bytes 1572872 | tf_op jit(solution)/shard_map/ppermute | solution.py:368
  299.5 3.2 %copy-start.1 = (f32[1024,8]{0,1:T(8,128)S(1)}, f32[1024,8]{0,1:T(8,128)}, u32[]{:S(2)}) copy-start(f32[1024,8]{0,1:T(8,128)} %param.16) | copy-start | bytes 98308
Sparse Core Ops, SparseCore 0:
  34.7 59.1 all-gather.3
  95.8 54.4 all-gather.5
  160.0 57.0 all-gather.7

commit v3 on v2

--- a/solution.py
+++ b/solution.py
@@ -270,7 +270,7 @@
 
 def middle(came, part, tokens, gain):
     rows, width = tokens.shape
-    step = min(rows, 64)
+    step = min(rows, 128)
     block = pl.BlockSpec((step, width), lambda i: (i, 0))
     return pl.pallas_call(
         middle_kernel,

time: 310 us -> 310 us (level)
  no operation moved by 1% of the time
where the time goes in v3:
time: 310 us; the launch traced here: 309 us
  waiting for transfers between devices  145 us (47%)
  Pallas kernels  70.8 us (23%)
  starting transfers between devices  53.7 us (17%)
  between operations  15 us (5%)
  local copies, waits for them, and re-layouts  14.3 us (5%)
  other arithmetic  10 us (3%)
    ppermute x18, waiting for transfers between devices, onward(): return [lax.ppermute(half, 'mp', order) for half in halves]  110 us
    ppermute x18, starting transfers between devices, onward(): return [lax.ppermute(half, 'mp', order) for half in halves]  34.1 us
    ppermute x9, waiting for transfers between devices, exchanged(): lax.ppermute(piece, 'mp', [(i, (i + shift) % count) for i in range(count)])  30.8 us
    pallas_call x4, Pallas kernels, retention(): pl.pallas_call(lambda *refs: retention_kernel(dims, *refs), grid_spec=gri...  30.2 us
    pallas_call x4, Pallas kernels, project(): pl.pallas_call(lambda *refs: project_kernel(heads, *refs), grid_spec=grid...  21.6 us
    ppermute x9, starting transfers between devices, exchanged(): lax.ppermute(piece, 'mp', [(i, (i + shift) % count) for i in range(count)])  19.4 us
    pallas_call x4, Pallas kernels, ffn(): pl.pallas_call(lambda *refs: ffn_kernel(len(halves), *refs), grid_spec=gr...  14 us
    unnamed x38, local copies, waits for them, and re-layouts  11.6 us
  transfers between devices with their start and end apart: 30, of which 21 were waited for; matrix products, arithmetic and copies ran while one was open for 3% of the time, Pallas kernels for 21%

profile of v3, /device:TPU:0, one launch (start us, length us, event | category | flops | bytes accessed | tf_op | source)
XLA Modules:
  0.0 309.2 jit_solution(12010730855828539991)
XLA Ops:
  7.3 1.3 convert_element_type.121
  10.7 3.1 collective-permute-start
  13.8 2.6 collective-permute-start.1
  16.4 1.3 collective-permute-start.2
  18.1 5.0 %collective-permute-done.refs_1_ = bf16[64,2048]{1,0:T(8,128)(2,1)S(1)} collective-permute-done((bf16[64,2048]{1,0:T(8,128)(2,1)S(1)}, bf16[64,2048]{1,0:T(8,128)(2,1)S(1)}, u32[]{:S(2)}, u32[]{:S(2)}) %collective-permute-start) | collective-permute-done | bytes 262176 | tf_op jit(solution)/shard_map/ppermute | solution.py:75
  23.1 10.4 %collective-permute-done.1.refs_2_ = bf16[64,2048]{1,0:T(8,128)(2,1)S(1)} collective-permute-done((bf16[64,2048]{1,0:T(8,128)(2,1)S(1)}, bf16[64,2048]{1,0:T(8,128)(2,1)S(1)}, u32[]{:S(2)}, u32[]{:S(2)}) %collective-permute-start.1) | collective-permute-done | bytes 262176 | tf_op jit(solution)/shard_map/ppermute | solution.py:75
  33.5 1.0 assemble.3
  34.7 6.1 %collective-permute-start.9 = (bf16[64,2048]{1,0:T(8,128)(2,1)S(1)}, bf16[64,2048]{1,0:T(8,128)(2,1)S(1)}, u32[]{:S(2)}, u32[]{:S(2)}) collective-permute-start(bf16[64,2048]{1,0:T(8,128)(2,1)S(1)} %get-tuple-element.102), channel_id=1, source_target_pairs={{0,1},{1,2},{2,3},{3,0},{4,5},{5,6},{6,7},{7,4},{8,9},{9,10},{10,1... | collective-permute-start | bytes 786440 | tf_op jit(solution)/shard_map/ppermute | solution.py:75
  40.9 1.6 collective-permute-start.10
  43.3 5.9 %collective-permute-done.9.refs_1_ = bf16[64,2048]{1,0:T(8,128)(2,1)S(1)} collective-permute-done((bf16[64,2048]{1,0:T(8,128)(2,1)S(1)}, bf16[64,2048]{1,0:T(8,128)(2,1)S(1)}, u32[]{:S(2)}, u32[]{:S(2)}) %collective-permute-start.9) | collective-permute-done | bytes 262176 | tf_op jit(solution)/shard_map/ppermute | solution.py:75
  49.3 9.4 %collective-permute-done.10.refs_2_ = bf16[64,2048]{1,0:T(8,128)(2,1)S(1)} collective-permute-done((bf16[64,2048]{1,0:T(8,128)(2,1)S(1)}, bf16[64,2048]{1,0:T(8,128)(2,1)S(1)}, u32[]{:S(2)}, u32[]{:S(2)}) %collective-permute-start.10) | collective-permute-done | bytes 262176 | tf_op jit(solution)/shard_map/ppermute | solution.py:75
  58.7 1.1 assemble.4
  59.9 6.1 %collective-permute-start.3 = (bf16[128,2048]{1,0:T(8,128)(2,1)S(1)}, bf16[128,2048]{1,0:T(8,128)(2,1)S(1)}, u32[]{:S(2)}, u32[]{:S(2)}) collective-permute-start(bf16[128,2048]{1,0:T(8,128)(2,1)S(1)} %get-tuple-element.53.refs_1_.token_ref), channel_id=1, source_target_pairs={{0,1},{1,2},{2,3},{3,0},{4,5},{5,6},{6,7},{7,4},{8,9},{9,10},{10,1... | collective-permute-start | bytes 1572872 | tf_op jit(solution)/shard_map/ppermute | solution.py:368
  66.8 1.6 convert_element_type.123
  68.4 1.3 convert_element_type.122
  69.7 1.1 pad_maximum_fusion.2
  70.8 9.9 %collective-permute-done.3.refs_1_ = bf16[128,2048]{1,0:T(8,128)(2,1)S(1)} collective-permute-done((bf16[128,2048]{1,0:T(8,128)(2,1)S(1)}, bf16[128,2048]{1,0:T(8,128)(2,1)S(1)}, u32[]{:S(2)}, u32[]{:S(2)}) %collective-permute-start.3) | collective-permute-done | bytes 524320 | tf_op jit(solution)/shard_map/ppermute | solution.py:368
  80.9 11.0 %collective-permute-done.4.refs_2_ = bf16[128,2048]{1,0:T(8,128)(2,1)S(1)} collective-permute-done((bf16[128,2048]{1,0:T(8,128)(2,1)S(1)}, bf16[128,2048]{1,0:T(8,128)(2,1)S(1)}, u32[]{:S(2)}, u32[]{:S(2)}) %collective-permute-start.4) | collective-permute-done | bytes 524320 | tf_op jit(solution)/shard_map/ppermute | solution.py:368
  92.1 1.9 multiply_sine_fusion
  94.1 3.4 %copy-done.2 = bf16[2048,2048]{1,0:T(8,128)(2,1)S(1)} copy-done((bf16[2048,2048]{1,0:T(8,128)(2,1)S(1)}, bf16[2048,2048]{1,0:T(8,128)(2,1)}, u32[]{:S(2)}) %copy-start.2) | copy-done | bytes 8388632
  97.4 4.7 %project.5 = (bf16[256,2048]{1,0:T(8,128)(2,1)}, bf16[256,2048]{1,0:T(8,128)(2,1)}) custom-call(s32[1]{0:T(128)} %bitcast.21.refs_0_, bf16[128,2048]{1,0:T(8,128)(2,1)S(1)} %get-tuple-element.53.refs_1_.token_ref, bf16[128,2048]{1,0:T(8,128)(2,1)S(1)} %get-tuple-element.57.refs_2_.token_ref, f32[1,2048]{1,0:T(1,128)S(1)} %bitcast.94, ...), custom_call_target="tpu_custom_call" | custom-call | flops 536870912 | bytes 1048576 | tf_op jit(solution)/shard_map/project/pallas_call | solution.py:130
  102.2 1.1 collective-permute-done.5.refs_1_
  103.5 10.9 %collective-permute-done.6.refs_2_ = bf16[128,2048]{1,0:T(8,128)(2,1)} collective-permute-done((bf16[128,2048]{1,0:T(8,128)(2,1)S(1)}, bf16[128,2048]{1,0:T(8,128)(2,1)}, u32[]{:S(2)}, u32[]{:S(2)}) %collective-permute-start.6) | collective-permute-done | bytes 524320 | tf_op jit(solution)/shard_map/ppermute | solution.py:368
  116.2 3.4 %copy-done.3 = bf16[2048,2048]{1,0:T(8,128)(2,1)S(1)} copy-done((bf16[2048,2048]{1,0:T(8,128)(2,1)S(1)}, bf16[2048,2048]{1,0:T(8,128)(2,1)}, u32[]{:S(2)}) %copy-start.3) | copy-done | bytes 8388632
  119.5 1.0 copy-done.7
  120.6 4.7 %project.4 = (bf16[256,2048]{1,0:T(8,128)(2,1)}, bf16[256,2048]{1,0:T(8,128)(2,1)}) custom-call(s32[1]{0:T(128)} %bitcast.5.refs_0_, bf16[128,2048]{1,0:T(8,128)(2,1)S(1)} %collective-permute-done.3.refs_1_, bf16[128,2048]{1,0:T(8,128)(2,1)S(1)} %copy-done.7, f32[1,2048]{1,0:T(1,128)S(1)} %bitcast.95, f32[1024,128]{1,0:T(8,128)S(1)} %get-tuple-element.111.refs_4_, ...), custom_call_target="tpu_custom_call" | custom-call | flops 536870912 | bytes 1048576 | tf_op jit(solution)/shard_map/project/pallas_call | solution.py:130
  125.3 6.1 %project.6 = (bf16[256,2048]{1,0:T(8,128)(2,1)}, bf16[256,2048]{1,0:T(8,128)(2,1)}) custom-call(s32[1]{0:T(128)} %bitcast.22.refs_0_, bf16[128,2048]{1,0:T(8,128)(2,1)} %collective-permute-done.5.refs_1_, bf16[128,2048]{1,0:T(8,128)(2,1)} %collective-permute-done.6.refs_2_, f32[1,2048]{1,0:T(1,128)S(1)} %bitcast.96, ...), custom_call_target="tpu_custom_call" | custom-call | flops 536870912 | bytes 1048576 | tf_op jit(solution)/shard_map/project/pallas_call | solution.py:130
  131.4 4.3 %collective-permute-done.8.refs_2_ = bf16[128,2048]{1,0:T(8,128)(2,1)} collective-permute-done((bf16[128,2048]{1,0:T(8,128)(2,1)}, bf16[128,2048]{1,0:T(8,128)(2,1)}, u32[]{:S(2)}, u32[]{:S(2)}) %collective-permute-start.8) | collective-permute-done | bytes 524320 | tf_op jit(solution)/shard_map/ppermute | solution.py:368
  137.1 1.8 collective-permute-start.22
  139.0 1.5 collective-permute-start.23
  140.5 6.0 %project.7 = (bf16[256,2048]{1,0:T(8,128)(2,1)}, bf16[256,2048]{1,0:T(8,128)(2,1)}) custom-call(s32[1]{0:T(128)} %bitcast.23.refs_0_, bf16[128,2048]{1,0:T(8,128)(2,1)} %collective-permute-done.7.refs_1_, bf16[128,2048]{1,0:T(8,128)(2,1)} %collective-permute-done.8.refs_2_, f32[1,2048]{1,0:T(1,128)S(1)} %bitcast.97, ...), custom_call_target="tpu_custom_call" | custom-call | flops 536870912 | bytes 1048576 | tf_op jit(solution)/shard_map/project/pallas_call | solution.py:130
  146.5 3.8 %all-gather.6.cloned.1.call-done.refs_8_ = bf16[2048,2048]{1,0:T(8,128)(2,1)} async-done(((bf16[256,2048]{1,0:T(8,128)(2,1)}), bf16[2048,2048]{1,0:T(8,128)(2,1)}) %all-gather.6.cloned.1.call-update) | async-done | bytes 8388624 | tf_op jit(solution)/shard_map/all_gather | solution.py:390
  150.2 7.6 %retention.4 = (bf16[128,2048]{1,0:T(8,128)(2,1)S(1)}, bf16[128,2048]{1,0:T(8,128)(2,1)S(1)}) custom-call(s32[3]{0:T(128)S(1)} %pad_add_fusion.refs_0_, f32[1024,2]{1,0:T(8,128)S(1)} %bitcast.86, f32[4,2,256]{2,1,0:T(2,128)S(1)} %bitcast.90, bf16[256,2048]{1,0:T(8,128)(2,1)} %get-tuple-element.59.refs_3_, bf16[256,2048]{1,0:T(8,128)(2,1)} %get-tuple-element.60.refs_4_, ...), custom_call_target="tpu_custom_call" | custom-call | flops 3000000000 | bytes 1048576 | tf_op jit(solution)/shard_map/retention/pallas_call | solution.py:255
  157.9 2.0 assemble.5
  159.9 5.1 %collective-permute-start.12 = (bf16[128,2048]{1,0:T(8,128)(2,1)S(1)}, bf16[128,2048]{1,0:T(8,128)(2,1)S(1)}, u32[]{:S(2)}, u32[]{:S(2)}) collective-permute-start(bf16[128,2048]{1,0:T(8,128)(2,1)S(1)} %get-tuple-element.71), channel_id=1, source_target_pairs={{0,1},{1,2},{2,3},{3,0},{4,5},{5,6},{6,7},{7,4},{8,9},{9,10},{10,1... | collective-permute-start | bytes 1572872 | tf_op jit(solution)/shard_map/ppermute | solution.py:368
  165.1 7.6 %retention.5 = (bf16[128,2048]{1,0:T(8,128)(2,1)S(1)}, bf16[128,2048]{1,0:T(8,128)(2,1)S(1)}) custom-call(s32[3]{0:T(128)S(1)} %pad_add_fusion.refs_0_, f32[1024,2]{1,0:T(8,128)S(1)} %bitcast.87, f32[4,2,256]{2,1,0:T(2,128)S(1)} %bitcast.91, bf16[256,2048]{1,0:T(8,128)(2,1)} %get-tuple-element.73.refs_3_, bf16[256,2048]{1,0:T(8,128)(2,1)} %get-tuple-element.60.refs_4_, ...), custom_call_target="tpu_custom_call" | custom-call | flops 3000000000 | bytes 1048576 | tf_op jit(solution)/shard_map/retention/pallas_call | solution.py:255
  172.7 4.7 %collective-permute-done.12 = bf16[128,2048]{1,0:T(8,128)(2,1)S(1)} collective-permute-done((bf16[128,2048]{1,0:T(8,128)(2,1)S(1)}, bf16[128,2048]{1,0:T(8,128)(2,1)S(1)}, u32[]{:S(2)}, u32[]{:S(2)}) %collective-permute-start.12) | collective-permute-done | bytes 524320 | tf_op jit(solution)/shard_map/ppermute | solution.py:368
  177.6 2.5 collective-permute-start.13
  180.1 8.6 %collective-permute-done.15 = bf16[128,2048]{1,0:T(8,128)(2,1)S(1)} collective-permute-done((bf16[128,2048]{1,0:T(8,128)(2,1)S(1)}, bf16[128,2048]{1,0:T(8,128)(2,1)S(1)}, u32[]{:S(2)}, u32[]{:S(2)}) %collective-permute-start.15) | collective-permute-done | bytes 524320 | tf_op jit(solution)/shard_map/ppermute | solution.py:368
  188.8 2.5 collective-permute-start.16
  191.3 7.4 %retention.6 = (bf16[128,2048]{1,0:T(8,128)(2,1)S(1)}, bf16[128,2048]{1,0:T(8,128)(2,1)S(1)}) custom-call(s32[3]{0:T(128)S(1)} %pad_add_fusion.refs_0_, f32[1024,2]{1,0:T(8,128)S(1)} %bitcast.88, f32[4,2,256]{2,1,0:T(2,128)S(1)} %bitcast.92, bf16[256,2048]{1,0:T(8,128)(2,1)} %get-tuple-element.77.refs_3_, bf16[256,2048]{1,0:T(8,128)(2,1)} %get-tuple-element.60.refs_4_, ...), custom_call_target="tpu_custom_call" | custom-call | flops 3000000000 | bytes 1048576 | tf_op jit(solution)/shard_map/retention/pallas_call | solution.py:255
  198.7 1.2 collective-permute-done.13
  200.1 2.5 collective-permute-start.14
  202.5 8.6 %collective-permute-done.16 = bf16[128,2048]{1,0:T(8,128)(2,1)S(1)} collective-permute-done((bf16[128,2048]{1,0:T(8,128)(2,1)S(1)}, bf16[128,2048]{1,0:T(8,128)(2,1)S(1)}, u32[]{:S(2)}, u32[]{:S(2)}) %collective-permute-start.16) | collective-permute-done | bytes 524320 | tf_op jit(solution)/shard_map/ppermute | solution.py:368
  211.3 2.5 collective-permute-start.17
  213.8 7.5 %retention.7 = (bf16[128,2048]{1,0:T(8,128)(2,1)S(1)}, bf16[128,2048]{1,0:T(8,128)(2,1)S(1)}) custom-call(s32[3]{0:T(128)S(1)} %pad_add_fusion.refs_0_, f32[1024,2]{1,0:T(8,128)S(1)} %bitcast.89, f32[4,2,256]{2,1,0:T(2,128)S(1)} %bitcast.93, bf16[256,2048]{1,0:T(8,128)(2,1)} %get-tuple-element.80.refs_3_, bf16[256,2048]{1,0:T(8,128)(2,1)} %get-tuple-element.60.refs_4_, ...), custom_call_target="tpu_custom_call" | custom-call | flops 3000000000 | bytes 1048576 | tf_op jit(solution)/shard_map/retention/pallas_call | solution.py:255
  221.3 1.1 collective-permute-done.14.came_ref
  222.9 2.5 collective-permute-start.18
  225.3 8.3 %collective-permute-done.17.came_ref = bf16[128,2048]{1,0:T(8,128)(2,1)S(1)} collective-permute-done((bf16[128,2048]{1,0:T(8,128)(2,1)S(1)}, bf16[128,2048]{1,0:T(8,128)(2,1)S(1)}, u32[]{:S(2)}, u32[]{:S(2)}) %collective-permute-start.17) | collective-permute-done | bytes 524320 | tf_op jit(solution)/shard_map/ppermute | solution.py:368
  234.1 2.5 collective-permute-start.20
  236.6 8.4 %collective-permute-done.18.refs_1_ = bf16[128,2048]{1,0:T(8,128)(2,1)} collective-permute-done((bf16[128,2048]{1,0:T(8,128)(2,1)S(1)}, bf16[128,2048]{1,0:T(8,128)(2,1)}, u32[]{:S(2)}, u32[]{:S(2)}) %collective-permute-start.18) | collective-permute-done | bytes 524320 | tf_op jit(solution)/shard_map/ppermute | solution.py:368
  245.0 2.4 collective-permute-start.19
  247.4 8.8 %collective-permute-done.20.refs_2_ = bf16[128,2048]{1,0:T(8,128)(2,1)} collective-permute-done((bf16[128,2048]{1,0:T(8,128)(2,1)S(1)}, bf16[128,2048]{1,0:T(8,128)(2,1)}, u32[]{:S(2)}, u32[]{:S(2)}) %collective-permute-start.20) | collective-permute-done | bytes 524320 | tf_op jit(solution)/shard_map/ppermute | solution.py:368
  256.2 2.4 collective-permute-start.25
  258.6 3.4 %copy-done.4 = bf16[2048,2048]{1,0:T(8,128)(2,1)S(1)} copy-done((bf16[2048,2048]{1,0:T(8,128)(2,1)S(1)}, bf16[2048,2048]{1,0:T(8,128)(2,1)}, u32[]{:S(2)}) %copy-start.4) | copy-done | bytes 8388632
  262.0 3.2 %ffn.4.refs_4_ = bf16[1024,1024]{1,0:T(8,128)(2,1)} custom-call(s32[1]{0:T(128)} %bitcast.21.refs_0_, bf16[128,2048]{1,0:T(8,128)(2,1)S(1)} %get-tuple-element.85.refs_1_, bf16[128,2048]{1,0:T(8,128)(2,1)S(1)} %get-tuple-element.86.refs_2_, bf16[2048,2048]{1,0:T(8,128)(2,1)S(1)} %copy-done.4), custom_call_target="tpu_custom_call" | custom-call | flops 2147483648 | bytes 8388608 | tf_op jit(solution)/shard_map/ffn/pallas_call | solution.py:315
  265.4 4.4 %ffn.5.refs_4_ = bf16[1024,1024]{1,0:T(8,128)(2,1)} custom-call(s32[1]{0:T(128)} %bitcast.5.refs_0_, bf16[128,2048]{1,0:T(8,128)(2,1)} %collective-permute-done.18.refs_1_, bf16[128,2048]{1,0:T(8,128)(2,1)} %collective-permute-done.20.refs_2_, bf16[2048,2048]{1,0:T(8,128)(2,1)S(1)} %copy-done.5, ...), custom_call_target="tpu_custom_call", output_to_operand_aliasing={{}: (4, {})} | custom-call | flops 2147483648 | bytes 8388608 | tf_op jit(solution)/shard_map/ffn/pallas_call | solution.py:315
  269.8 8.8 %collective-permute-done.25.refs_2_ = bf16[128,2048]{1,0:T(8,128)(2,1)S(1)} collective-permute-done((bf16[128,2048]{1,0:T(8,128)(2,1)}, bf16[128,2048]{1,0:T(8,128)(2,1)S(1)}, u32[]{:S(2)}, u32[]{:S(2)}) %collective-permute-start.25) | collective-permute-done | bytes 524320 | tf_op jit(solution)/shard_map/ppermute | solution.py:368
  278.6 2.4 collective-permute-start.26
  281.0 1.0 pad_maximum_fusion.3
  282.0 3.2 %ffn.6.refs_4_ = bf16[1024,1024]{1,0:T(8,128)(2,1)} custom-call(s32[1]{0:T(128)} %bitcast.22.refs_0_, bf16[128,2048]{1,0:T(8,128)(2,1)S(1)} %collective-permute-done.19.refs_1_, bf16[128,2048]{1,0:T(8,128)(2,1)S(1)} %collective-permute-done.25.refs_2_, bf16[2048,2048]{1,0:T(8,128)(2,1)S(1)} %copy-done.5, ...), custom_call_target="tpu_custom_call", output_to_operand_aliasing={{}: (4, {})} | custom-call | flops 2147483648 | bytes 8388608 | tf_op jit(solution)/shard_map/ffn/pallas_call | solution.py:315
  285.2 4.6 %collective-permute-done.24.refs_1_ = bf16[128,2048]{1,0:T(8,128)(2,1)S(1)} collective-permute-done((bf16[128,2048]{1,0:T(8,128)(2,1)S(1)}, bf16[128,2048]{1,0:T(8,128)(2,1)S(1)}, u32[]{:S(2)}, u32[]{:S(2)}) %collective-permute-start.24) | collective-permute-done | bytes 524320 | tf_op jit(solution)/shard_map/ppermute | solution.py:368
  289.8 9.7 %collective-permute-done.26.refs_2_ = bf16[128,2048]{1,0:T(8,128)(2,1)S(1)} collective-permute-done((bf16[128,2048]{1,0:T(8,128)(2,1)S(1)}, bf16[128,2048]{1,0:T(8,128)(2,1)S(1)}, u32[]{:S(2)}, u32[]{:S(2)}) %collective-permute-start.26) | collective-permute-done | bytes 524320 | tf_op jit(solution)/shard_map/ppermute | solution.py:368
  299.5 3.2 %ffn.7 = bf16[1024,1024]{1,0:T(8,128)(2,1)} custom-call(s32[1]{0:T(128)} %bitcast.23.refs_0_, bf16[128,2048]{1,0:T(8,128)(2,1)S(1)} %collective-permute-done.24.refs_1_, bf16[128,2048]{1,0:T(8,128)(2,1)S(1)} %collective-permute-done.26.refs_2_, bf16[2048,2048]{1,0:T(8,128)(2,1)S(1)} %copy-done.5, ...), custom_call_target="tpu_custom_call", output_to_operand_aliasing={{}: (4, {})} | custom-call | flops 2147483648 | bytes 8388608 | tf_op jit(solution)/shard_map/ffn/pallas_call | solution.py:315
  (100 shorter events, 9.0 us)
Async XLA Ops:
  7.2 59.0 %copy-start = (f32[1024,8]{0,1:T(8,128)S(1)}, f32[1024,8]{0,1:T(8,128)}, u32[]{:S(2)}) copy-start(f32[1024,8]{0,1:T(8,128)} %param.16) | copy-start | bytes 98308
  7.2 1.5 copy-start.14
  7.2 86.8 %all-gather.4.cloned.1.call-start = ((), (), s32[]{:S(2)}) async-start(), calls=%async_computation | async-start | bytes 9437184 | tf_op jit(solution)/shard_map/all_gather | solution.py:363
  8.6 1.0 copy-start.15
  10.5 7.2 %copy-start.11 = (f32[4096,64]{0,1:T(8,128)S(1)}, f32[4096,64]{0,1:T(8,128)}, u32[]{:S(2)}) copy-start(f32[4096,64]{0,1:T(8,128)} %param.21) | copy-start | bytes 3145732
  10.6 7.2 %copy-start.12 = (f32[64,4096]{1,0:T(8,128)S(1)}, f32[64,4096]{1,0:T(8,128)}, u32[]{:S(2)}) copy-start(f32[64,4096]{1,0:T(8,128)} %param.20) | copy-start | bytes 3145732
  10.7 12.4 %collective-permute-start = (bf16[64,2048]{1,0:T(8,128)(2,1)S(1)}, bf16[64,2048]{1,0:T(8,128)(2,1)S(1)}, u32[]{:S(2)}, u32[]{:S(2)}) collective-permute-start(bf16[64,2048]{1,0:T(8,128)(2,1)S(1)} %get-tuple-element.108), channel_id=1, source_target_pairs={{0,1},{1,2},{2,3},{3,0},{4,5},{5,6},{6,7},{7,4},{8,9},{9,10},{10,1... | collective-permute-start | bytes 786440 | tf_op jit(solution)/shard_map/ppermute | solution.py:75
  13.8 19.7 %collective-permute-start.1 = (bf16[64,2048]{1,0:T(8,128)(2,1)S(1)}, bf16[64,2048]{1,0:T(8,128)(2,1)S(1)}, u32[]{:S(2)}, u32[]{:S(2)}) collective-permute-start(bf16[64,2048]{1,0:T(8,128)(2,1)S(1)} %get-tuple-element.107), channel_id=1, source_target_pairs={{0,2},{1,3},{2,0},{3,1},{4,6},{5,7},{6,4},{7,5},{8,10},{9,11},{10,... | collective-permute-start | bytes 786440 | tf_op jit(solution)/shard_map/ppermute | solution.py:75
  16.4 17.1 %collective-permute-start.2 = (bf16[64,2048]{1,0:T(8,128)(2,1)S(1)}, bf16[64,2048]{1,0:T(8,128)(2,1)S(1)}, u32[]{:S(2)}, u32[]{:S(2)}) collective-permute-start(bf16[64,2048]{1,0:T(8,128)(2,1)S(1)} %get-tuple-element.106), channel_id=1, source_target_pairs={{0,3},{1,0},{2,1},{3,2},{4,7},{5,4},{6,5},{7,6},{8,11},{9,8},{10,9... | collective-permute-start | bytes 786440 | tf_op jit(solution)/shard_map/ppermute | solution.py:75
  34.6 115.6 %all-gather.6.cloned.1.call-start = ((), (), s32[]{:S(2)}) async-start(), calls=%async_computation.1 | async-start | bytes 9437184 | tf_op jit(solution)/shard_map/all_gather | solution.py:390
  34.7 25.1 %copy-start.13 = (bf16[256,2048]{1,0:T(8,128)(2,1)S(1)}, bf16[256,2048]{1,0:T(8,128)(2,1)}, u32[]{:S(2)}) copy-start(bf16[256,2048]{1,0:T(8,128)(2,1)} %param.12) | copy-start | bytes 3145732
  34.7 14.5 %collective-permute-start.9 = (bf16[64,2048]{1,0:T(8,128)(2,1)S(1)}, bf16[64,2048]{1,0:T(8,128)(2,1)S(1)}, u32[]{:S(2)}, u32[]{:S(2)}) collective-permute-start(bf16[64,2048]{1,0:T(8,128)(2,1)S(1)} %get-tuple-element.102), channel_id=1, source_target_pairs={{0,1},{1,2},{2,3},{3,0},{4,5},{5,6},{6,7},{7,4},{8,9},{9,10},{10,1... | collective-permute-start | bytes 786440 | tf_op jit(solution)/shard_map/ppermute | solution.py:75
  40.9 17.8 %collective-permute-start.10 = (bf16[64,2048]{1,0:T(8,128)(2,1)S(1)}, bf16[64,2048]{1,0:T(8,128)(2,1)S(1)}, u32[]{:S(2)}, u32[]{:S(2)}) collective-permute-start(bf16[64,2048]{1,0:T(8,128)(2,1)S(1)} %get-tuple-element.101), channel_id=1, source_target_pairs={{0,2},{1,3},{2,0},{3,1},{4,6},{5,7},{6,4},{7,5},{8,10},{9,11},{10,... | collective-permute-start | bytes 786440 | tf_op jit(solution)/shard_map/ppermute | solution.py:75
  42.5 16.2 %collective-permute-start.11 = (bf16[64,2048]{1,0:T(8,128)(2,1)S(1)}, bf16[64,2048]{1,0:T(8,128)(2,1)S(1)}, u32[]{:S(2)}, u32[]{:S(2)}) collective-permute-start(bf16[64,2048]{1,0:T(8,128)(2,1)S(1)} %get-tuple-element.100), channel_id=1, source_target_pairs={{0,3},{1,0},{2,1},{3,2},{4,7},{5,4},{6,5},{7,6},{8,11},{9,8},{10,9... | collective-permute-start | bytes 786440 | tf_op jit(solution)/shard_map/ppermute | solution.py:75
  59.8 198.8 %all-gather.8.cloned.1.call-start = ((), (), s32[]{:S(2)}) async-start(), calls=%async_computation.2 | async-start | bytes 9437184 | tf_op jit(solution)/shard_map/all_gather | solution.py:407
  59.9 20.7 %collective-permute-start.3 = (bf16[128,2048]{1,0:T(8,128)(2,1)S(1)}, bf16[128,2048]{1,0:T(8,128)(2,1)S(1)}, u32[]{:S(2)}, u32[]{:S(2)}) collective-permute-start(bf16[128,2048]{1,0:T(8,128)(2,1)S(1)} %get-tuple-element.53.refs_1_.token_ref), channel_id=1, source_target_pairs={{0,1},{1,2},{2,3},{3,0},{4,5},{5,6},{6,7},{7,4},{8,9},{9,10},{10,1... | collective-permute-start | bytes 1572872 | tf_op jit(solution)/shard_map/ppermute | solution.py:368
  66.1 25.8 %collective-permute-start.4 = (bf16[128,2048]{1,0:T(8,128)(2,1)S(1)}, bf16[128,2048]{1,0:T(8,128)(2,1)S(1)}, u32[]{:S(2)}, u32[]{:S(2)}) collective-permute-start(bf16[128,2048]{1,0:T(8,128)(2,1)S(1)} %get-tuple-element.57.refs_2_.token_ref), channel_id=1, source_target_pairs={{0,1},{1,2},{2,3},{3,0},{4,5},{5,6},{6,7},{7,4},{8,9},{9,10},{10,1... | collective-permute-start | bytes 1572872 | tf_op jit(solution)/shard_map/ppermute | solution.py:368
  69.7 24.4 %copy-start.8 = (f32[2048]{0:T(1024)S(1)}, f32[2048]{0:T(1024)}, u32[]{:S(2)}) copy-start(f32[2048]{0:T(1024)} %param.13) | copy-start | bytes 24580
  80.7 22.6 %collective-permute-start.5 = (bf16[128,2048]{1,0:T(8,128)(2,1)S(1)}, bf16[128,2048]{1,0:T(8,128)(2,1)}, u32[]{:S(2)}, u32[]{:S(2)}) collective-permute-start(bf16[128,2048]{1,0:T(8,128)(2,1)S(1)} %collective-permute-done.3.refs_1_), channel_id=1, source_target_pairs={{0,1},{1,2},{2,3},{3,0},{4,5},{5,6},{6,7},{7,4},{8,9},{9,10},{10,1... | collective-permute-start | bytes 1572872 | tf_op jit(solution)/shard_map/ppermute | solution.py:368
  91.9 10.3 %copy-start.6 = (bf16[128,2048]{1,0:T(8,128)(2,1)}, bf16[128,2048]{1,0:T(8,128)(2,1)S(1)}, u32[]{:S(2)}) copy-start(bf16[128,2048]{1,0:T(8,128)(2,1)S(1)} %collective-permute-done.4.refs_2_) | copy-start | bytes 1572868
  91.9 22.6 %collective-permute-start.6 = (bf16[128,2048]{1,0:T(8,128)(2,1)S(1)}, bf16[128,2048]{1,0:T(8,128)(2,1)}, u32[]{:S(2)}, u32[]{:S(2)}) collective-permute-start(bf16[128,2048]{1,0:T(8,128)(2,1)S(1)} %collective-permute-done.4.refs_2_), channel_id=1, source_target_pairs={{0,1},{1,2},{2,3},{3,0},{4,5},{5,6},{6,7},{7,4},{8,9},{9,10},{10,1... | collective-permute-start | bytes 1572872 | tf_op jit(solution)/shard_map/ppermute | solution.py:368
  94.1 3.4 %copy-start.2 = (bf16[2048,2048]{1,0:T(8,128)(2,1)S(1)}, bf16[2048,2048]{1,0:T(8,128)(2,1)}, u32[]{:S(2)}) copy-start(bf16[2048,2048]{1,0:T(8,128)(2,1)} %all-gather.4.cloned.1.call-done.refs_6_) | copy-start | bytes 25165828
  103.3 28.2 %collective-permute-start.7 = (bf16[128,2048]{1,0:T(8,128)(2,1)}, bf16[128,2048]{1,0:T(8,128)(2,1)}, u32[]{:S(2)}, u32[]{:S(2)}) collective-permute-start(bf16[128,2048]{1,0:T(8,128)(2,1)} %collective-permute-done.5.refs_1_), channel_id=1, source_target_pairs={{0,1},{1,2},{2,3},{3,0},{4,5},{5,6},{6,7},{7,4},{8,9},{9,10},{10,1... | collective-permute-start | bytes 1572872 | tf_op jit(solution)/shard_map/ppermute | solution.py:368
  114.5 21.2 %collective-permute-start.8 = (bf16[128,2048]{1,0:T(8,128)(2,1)}, bf16[128,2048]{1,0:T(8,128)(2,1)}, u32[]{:S(2)}, u32[]{:S(2)}) collective-permute-start(bf16[128,2048]{1,0:T(8,128)(2,1)} %collective-permute-done.6.refs_2_), channel_id=1, source_target_pairs={{0,1},{1,2},{2,3},{3,0},{4,5},{5,6},{6,7},{7,4},{8,9},{9,10},{10,1... | collective-permute-start | bytes 1572872 | tf_op jit(solution)/shard_map/ppermute | solution.py:368
  116.2 3.4 %copy-start.3 = (bf16[2048,2048]{1,0:T(8,128)(2,1)S(1)}, bf16[2048,2048]{1,0:T(8,128)(2,1)}, u32[]{:S(2)}) copy-start(bf16[2048,2048]{1,0:T(8,128)(2,1)} %all-gather.4.cloned.1.call-done.refs_6_) | copy-start | bytes 25165828
  119.5 1.0 copy-start.7
  120.6 19.9 %slice-start = ((s8[8388608]{0:T(1024)(128)(4,1)}), s8[4194304]{0:T(1024)(128)(4,1)S(1)}, s32[]{:S(2)}) async-start(s8[8388608]{0:T(1024)(128)(4,1)} %bitcast.84), calls=%async_computation.3 | async-start | bytes 8388608
  125.3 10.4 %copy-start.10 = (bf16[4,64,2048]{2,1,0:T(8,128)(2,1)S(1)}, bf16[4,64,2048]{2,1,0:T(8,128)(2,1)}, u32[]{:S(2)}) copy-start(bf16[4,64,2048]{2,1,0:T(8,128)(2,1)} %pad_maximum_fusion.2) | copy-start | bytes 3145732
  125.3 15.2 %slice-start.1 = ((s8[8388608]{0:T(1024)(128)(4,1)}), s8[4194304]{0:T(1024)(128)(4,1)S(1)}, s32[]{:S(2)}) async-start(s8[8388608]{0:T(1024)(128)(4,1)} %bitcast.84), calls=%async_computation.4 | async-start | bytes 8388608
  136.7 21.2 %collective-permute-start.21 = (bf16[64,2048]{1,0:T(8,128)(2,1)}, bf16[64,2048]{1,0:T(8,128)(2,1)S(1)}, u32[]{:S(2)}, u32[]{:S(2)}) collective-permute-start(bf16[64,2048]{1,0:T(8,128)(2,1)} %get-tuple-element.98), channel_id=1, source_target_pairs={{0,1},{1,2},{2,3},{3,0},{4,5},{5,6},{6,7},{7,4},{8,9},{9,10},{10,1... | collective-permute-start | bytes 786440 | tf_op jit(solution)/shard_map/ppermute | solution.py:75
  137.1 20.7 %collective-permute-start.22 = (bf16[64,2048]{1,0:T(8,128)(2,1)}, bf16[64,2048]{1,0:T(8,128)(2,1)S(1)}, u32[]{:S(2)}, u32[]{:S(2)}) collective-permute-start(bf16[64,2048]{1,0:T(8,128)(2,1)} %get-tuple-element.97), channel_id=1, source_target_pairs={{0,2},{1,3},{2,0},{3,1},{4,6},{5,7},{6,4},{7,5},{8,10},{9,11},{10,... | collective-permute-start | bytes 786440 | tf_op jit(solution)/shard_map/ppermute | solution.py:75
  139.0 18.9 %collective-permute-start.23 = (bf16[64,2048]{1,0:T(8,128)(2,1)}, bf16[64,2048]{1,0:T(8,128)(2,1)}, u32[]{:S(2)}, u32[]{:S(2)}) collective-permute-start(bf16[64,2048]{1,0:T(8,128)(2,1)} %get-tuple-element.96), channel_id=1, source_target_pairs={{0,3},{1,0},{2,1},{3,2},{4,7},{5,4},{6,5},{7,6},{8,11},{9,8},{10,9... | collective-permute-start | bytes 786440 | tf_op jit(solution)/shard_map/ppermute | solution.py:75
  159.9 17.5 %collective-permute-start.12 = (bf16[128,2048]{1,0:T(8,128)(2,1)S(1)}, bf16[128,2048]{1,0:T(8,128)(2,1)S(1)}, u32[]{:S(2)}, u32[]{:S(2)}) collective-permute-start(bf16[128,2048]{1,0:T(8,128)(2,1)S(1)} %get-tuple-element.71), channel_id=1, source_target_pairs={{0,1},{1,2},{2,3},{3,0},{4,5},{5,6},{6,7},{7,4},{8,9},{9,10},{10,1... | collective-permute-start | bytes 1572872 | tf_op jit(solution)/shard_map/ppermute | solution.py:368
  165.0 23.7 %collective-permute-start.15 = (bf16[128,2048]{1,0:T(8,128)(2,1)S(1)}, bf16[128,2048]{1,0:T(8,128)(2,1)S(1)}, u32[]{:S(2)}, u32[]{:S(2)}) collective-permute-start(bf16[128,2048]{1,0:T(8,128)(2,1)S(1)} %get-tuple-element.72), channel_id=1, source_target_pairs={{0,1},{1,2},{2,3},{3,0},{4,5},{5,6},{6,7},{7,4},{8,9},{9,10},{10,1... | collective-permute-start | bytes 1572872 | tf_op jit(solution)/shard_map/ppermute | solution.py:368
  177.6 22.3 %collective-permute-start.13 = (bf16[128,2048]{1,0:T(8,128)(2,1)S(1)}, bf16[128,2048]{1,0:T(8,128)(2,1)S(1)}, u32[]{:S(2)}, u32[]{:S(2)}) collective-permute-start(bf16[128,2048]{1,0:T(8,128)(2,1)S(1)} %add_convert_fusion.3), channel_id=1, source_target_pairs={{0,1},{1,2},{2,3},{3,0},{4,5},{5,6},{6,7},{7,4},{8,9},{9,10},{10,1... | collective-permute-start | bytes 1572872 | tf_op jit(solution)/shard_map/ppermute | solution.py:368
  188.8 22.3 %collective-permute-start.16 = (bf16[128,2048]{1,0:T(8,128)(2,1)S(1)}, bf16[128,2048]{1,0:T(8,128)(2,1)S(1)}, u32[]{:S(2)}, u32[]{:S(2)}) collective-permute-start(bf16[128,2048]{1,0:T(8,128)(2,1)S(1)} %add_convert_fusion.1), channel_id=1, source_target_pairs={{0,1},{1,2},{2,3},{3,0},{4,5},{5,6},{6,7},{7,4},{8,9},{9,10},{10,1... | collective-permute-start | bytes 1572872 | tf_op jit(solution)/shard_map/ppermute | solution.py:368
  200.1 22.3 %collective-permute-start.14 = (bf16[128,2048]{1,0:T(8,128)(2,1)S(1)}, bf16[128,2048]{1,0:T(8,128)(2,1)S(1)}, u32[]{:S(2)}, u32[]{:S(2)}) collective-permute-start(bf16[128,2048]{1,0:T(8,128)(2,1)S(1)} %add_convert_fusion.2), channel_id=1, source_target_pairs={{0,1},{1,2},{2,3},{3,0},{4,5},{5,6},{6,7},{7,4},{8,9},{9,10},{10,1... | collective-permute-start | bytes 1572872 | tf_op jit(solution)/shard_map/ppermute | solution.py:368
  211.3 11.1 %copy-start.9 = (f32[2048]{0:T(1024)S(1)}, f32[2048]{0:T(1024)}, u32[]{:S(2)}) copy-start(f32[2048]{0:T(1024)} %param.14) | copy-start | bytes 24580
  211.3 22.3 %collective-permute-start.17 = (bf16[128,2048]{1,0:T(8,128)(2,1)S(1)}, bf16[128,2048]{1,0:T(8,128)(2,1)S(1)}, u32[]{:S(2)}, u32[]{:S(2)}) collective-permute-start(bf16[128,2048]{1,0:T(8,128)(2,1)S(1)} %add_convert_fusion), channel_id=1, source_target_pairs={{0,1},{1,2},{2,3},{3,0},{4,5},{5,6},{6,7},{7,4},{8,9},{9,10},{10,1... | collective-permute-start | bytes 1572872 | tf_op jit(solution)/shard_map/ppermute | solution.py:368
  222.9 22.1 %collective-permute-start.18 = (bf16[128,2048]{1,0:T(8,128)(2,1)S(1)}, bf16[128,2048]{1,0:T(8,128)(2,1)}, u32[]{:S(2)}, u32[]{:S(2)}) collective-permute-start(bf16[128,2048]{1,0:T(8,128)(2,1)S(1)} %get-tuple-element.85.refs_1_), channel_id=1, source_target_pairs={{0,1},{1,2},{2,3},{3,0},{4,5},{5,6},{6,7},{7,4},{8,9},{9,10},{10,1... | collective-permute-start | bytes 1572872 | tf_op jit(solution)/shard_map/ppermute | solution.py:368
  234.1 22.1 %collective-permute-start.20 = (bf16[128,2048]{1,0:T(8,128)(2,1)S(1)}, bf16[128,2048]{1,0:T(8,128)(2,1)}, u32[]{:S(2)}, u32[]{:S(2)}) collective-permute-start(bf16[128,2048]{1,0:T(8,128)(2,1)S(1)} %get-tuple-element.86.refs_2_), channel_id=1, source_target_pairs={{0,1},{1,2},{2,3},{3,0},{4,5},{5,6},{6,7},{7,4},{8,9},{9,10},{10,1... | collective-permute-start | bytes 1572872 | tf_op jit(solution)/shard_map/ppermute | solution.py:368
  245.0 24.8 %collective-permute-start.19 = (bf16[128,2048]{1,0:T(8,128)(2,1)}, bf16[128,2048]{1,0:T(8,128)(2,1)S(1)}, u32[]{:S(2)}, u32[]{:S(2)}) collective-permute-start(bf16[128,2048]{1,0:T(8,128)(2,1)} %collective-permute-done.18.refs_1_), channel_id=1, source_target_pairs={{0,1},{1,2},{2,3},{3,0},{4,5},{5,6},{6,7},{7,4},{8,9},{9,10},{10,1... | collective-permute-start | bytes 1572872 | tf_op jit(solution)/shard_map/ppermute | solution.py:368
  256.2 22.4 %collective-permute-start.25 = (bf16[128,2048]{1,0:T(8,128)(2,1)}, bf16[128,2048]{1,0:T(8,128)(2,1)S(1)}, u32[]{:S(2)}, u32[]{:S(2)}) collective-permute-start(bf16[128,2048]{1,0:T(8,128)(2,1)} %collective-permute-done.20.refs_2_), channel_id=1, source_target_pairs={{0,1},{1,2},{2,3},{3,0},{4,5},{5,6},{6,7},{7,4},{8,9},{9,10},{10,1... | collective-permute-start | bytes 1572872 | tf_op jit(solution)/shard_map/ppermute | solution.py:368
  258.6 3.4 %copy-start.4 = (bf16[2048,2048]{1,0:T(8,128)(2,1)S(1)}, bf16[2048,2048]{1,0:T(8,128)(2,1)}, u32[]{:S(2)}) copy-start(bf16[2048,2048]{1,0:T(8,128)(2,1)} %all-gather.8.cloned.1.call-done.refs_3_) | copy-start | bytes 25165828
  262.0 3.4 %copy-start.5 = (bf16[2048,2048]{1,0:T(8,128)(2,1)S(1)}, bf16[2048,2048]{1,0:T(8,128)(2,1)}, u32[]{:S(2)}) copy-start(bf16[2048,2048]{1,0:T(8,128)(2,1)} %all-gather.8.cloned.1.call-done.refs_3_) | copy-start | bytes 25165828
  269.8 20.0 %collective-permute-start.24 = (bf16[128,2048]{1,0:T(8,128)(2,1)S(1)}, bf16[128,2048]{1,0:T(8,128)(2,1)S(1)}, u32[]{:S(2)}, u32[]{:S(2)}) collective-permute-start(bf16[128,2048]{1,0:T(8,128)(2,1)S(1)} %collective-permute-done.19.refs_1_), channel_id=1, source_target_pairs={{0,1},{1,2},{2,3},{3,0},{4,5},{5,6},{6,7},{7,4},{8,9},{9,10},{10,1... | collective-permute-start | bytes 1572872 | tf_op jit(solution)/shard_map/ppermute | solution.py:368
  278.6 20.9 %collective-permute-start.26 = (bf16[128,2048]{1,0:T(8,128)(2,1)S(1)}, bf16[128,2048]{1,0:T(8,128)(2,1)S(1)}, u32[]{:S(2)}, u32[]{:S(2)}) collective-permute-start(bf16[128,2048]{1,0:T(8,128)(2,1)S(1)} %collective-permute-done.25.refs_2_), channel_id=1, source_target_pairs={{0,1},{1,2},{2,3},{3,0},{4,5},{5,6},{6,7},{7,4},{8,9},{9,10},{10,1... | collective-permute-start | bytes 1572872 | tf_op jit(solution)/shard_map/ppermute | solution.py:368
  299.5 3.2 %copy-start.1 = (f32[1024,8]{0,1:T(8,128)S(1)}, f32[1024,8]{0,1:T(8,128)}, u32[]{:S(2)}) copy-start(f32[1024,8]{0,1:T(8,128)} %param.16) | copy-start | bytes 98308
Sparse Core Ops, SparseCore 0:
  34.7 59.1 all-gather.3
  95.8 54.4 all-gather.5
  160.0 57.0 all-gather.7
